TPU v7x, 128 devices: a whole 4x4x4 slice. The times are simulated.
128 devices in a mesh: dp: 8 (over z, x_lo), seq: 16 (over y, x_hi, core).
Axes of the slice: x: 4 (x_hi: 2, x_lo: 2; x = x_hi * 2 + x_lo), y: 4, z: 4, core: 2. Of those that a mesh axis runs over, the one named last changes fastest.
Arguments:
- frames: bfloat16 [8, 4096, 1536], P('dp', 'seq'), may hold values from -6 to 6
- upstream: bfloat16 [8, 4096, 1536], P('dp', 'seq'), may hold values from -6 to 6
- utt_span: int32 [2, 8, 4096], P(None, 'dp', 'seq'), may hold values from 0 to 4096, as said below
- w_qkv: bfloat16 [1536, 2304], P('dp')
- w_out: bfloat16 [768, 1536], P('dp'), may hold values from -0.21875 to 0.21875
Outputs:
- branch: bfloat16 [8, 4096, 1536], P('dp', 'seq')
- grad_in: bfloat16 [8, 4096, 1536], P('dp', 'seq')
- grad_qkv: float32 [1536, 2304], P(('dp', 'seq'))
- grad_out: float32 [768, 1536], P(('dp', 'seq'))
Inputs may be any that keep to these rules, and one draw needn't show every extreme that they name: In each row the utterances tile the frames: for frame i, utt_span[0] <= i < utt_span[1], and all frames of an utterance carry the same pair.
All inputs are finite; a program needn't handle non-finite values.
Results may differ from a plain program's by a relative error of at most 0.015.
Values may be sent and summed in bfloat16 or wider, within the bound.
No kernel may reach another device: no remote copies, remote signals or barrier semaphores. Data moves between devices by JAX's collectives and lax.ppermute only.
A program may use at most 128 MiB of HBM per device.

v0:
```python
import jax
import jax.numpy as jnp
from jax import lax
from jax.sharding import PartitionSpec as P

HEADS = 12
HEAD_DIM = 64
STRETCH = 64
PRIOR = 4


EPS = 1e-05


def from_behind(value, axis, by):
    length = lax.axis_size(axis)
    pairs = [(i, i + by) for i in range(length) if 0 <= i + by < length]
    return lax.ppermute(value, axis, pairs)


def normalize(inputs):
    widened = inputs.astype(jnp.float32)
    centered = widened - jnp.mean(widened, axis=-1, keepdims=True)
    inv_sigma = lax.rsqrt(jnp.mean(centered * centered, axis=-1, keepdims=True) + EPS)
    return (centered * inv_sigma, inv_sigma)


def contract(form, left, right):
    return jnp.einsum(form, left, right, preferred_element_type=jnp.float32)


def windows(extended):
    stretch_total = extended.shape[0] // STRETCH
    stretch_count = stretch_total - PRIOR
    blocked = extended.reshape((stretch_total, STRETCH) + extended.shape[1:])
    return jnp.concatenate(
        [blocked[shift_by : shift_by + stretch_count] for shift_by in range(PRIOR + 1)], axis=1
    )


def unwindow(windowed):
    stretch_count = windowed.shape[0]
    parted = windowed.reshape((stretch_count, PRIOR + 1, STRETCH) + windowed.shape[2:])
    running = jnp.zeros((stretch_count + PRIOR, STRETCH) + windowed.shape[2:], jnp.float32)
    for shift_by in range(PRIOR + 1):
        running = running.at[shift_by : shift_by + stretch_count].add(parted[:, shift_by])
    return running.reshape(((stretch_count + PRIOR) * STRETCH,) + windowed.shape[2:])


def visible(starts, limits, offset):
    stretch_count = starts.shape[0] // STRETCH
    block_first = jnp.arange(stretch_count, dtype=jnp.int32)[:, None] * STRETCH
    key_pos = (
        offset
        - PRIOR * STRETCH
        + block_first
        + jnp.arange((PRIOR + 1) * STRETCH, dtype=jnp.int32)[None, :]
    )
    lowest = starts.reshape(stretch_count, STRETCH)
    beyond = limits.reshape(stretch_count, STRETCH)
    return (key_pos[:, None, :] >= lowest[:, :, None]) & (key_pos[:, None, :] < beyond[:, :, None])


def attend_forward(queries, keys_ext, values_ext, mask):
    stretch_count = queries.shape[0] // STRETCH
    query_blocks = queries.reshape(stretch_count, STRETCH, HEADS, HEAD_DIM)
    key_windows = windows(keys_ext.reshape(-1, HEADS, HEAD_DIM))
    value_windows = windows(values_ext.reshape(-1, HEADS, HEAD_DIM))
    scores = contract("nqhd,nkhd->nhqk", query_blocks, key_windows) * HEAD_DIM ** (-0.5)
    allowed = mask[:, None]
    masked = jnp.where(allowed, scores, -1e30)
    highest = jnp.max(masked, axis=-1, keepdims=True)
    weights = jnp.where(allowed, jnp.exp(masked - highest), 0.0)
    probs = weights / jnp.sum(weights, axis=-1, keepdims=True)
    probs_low = probs.astype(jnp.bfloat16)
    context = contract("nhqk,nkhd->nqhd", probs_low, value_windows).astype(jnp.bfloat16)
    return (
        context.reshape(queries.shape),
        (query_blocks, key_windows, value_windows, probs, probs_low),
    )


def attend_backward(saved, d_context):
    query_blocks, key_windows, value_windows, probs, probs_low = saved
    d_blocks = d_context.reshape(query_blocks.shape)
    d_probs = contract("nqhd,nkhd->nhqk", d_blocks, value_windows)
    d_scores = probs * (d_probs - jnp.sum(probs * d_probs, axis=-1, keepdims=True))
    d_scores_low = (d_scores * HEAD_DIM ** (-0.5)).astype(jnp.bfloat16)
    d_queries = contract("nhqk,nkhd->nqhd", d_scores_low, key_windows).astype(jnp.bfloat16)
    d_keys = unwindow(contract("nhqk,nqhd->nkhd", d_scores_low, query_blocks))
    d_values = unwindow(contract("nhqk,nqhd->nkhd", probs_low, d_blocks))
    ext_rows = d_keys.shape[0]
    return (
        d_queries.reshape(d_context.shape),
        d_keys.reshape(ext_rows, -1),
        d_values.reshape(ext_rows, -1),
    )


def against_rows(left, piece_rows):
    return lax.dot_general(
        left, piece_rows, (((1,), (1,)), ((), ())), preferred_element_type=jnp.float32
    )


def over_frames(left, right):
    return lax.dot_general(
        left, right, (((0,), (0,)), ((), ())), preferred_element_type=jnp.float32
    )


def joint_term(left, right):
    return over_frames(left, right)


def body(frames, upstream, utt_span, w_qkv, w_out):
    own_frames = frames[0]
    own_grad = upstream[0]
    frame_count = own_frames.shape[0]
    inner_width = w_qkv.shape[1] // 3
    halo_rows = PRIOR * STRETCH
    offset = lax.axis_index("seq") * frame_count
    normed, inv_sigma = normalize(own_frames)
    normed_low = normed.astype(jnp.bfloat16)
    full_qkv, full_out = (
        lax.all_gather(w_qkv, "dp", axis=0, tiled=True),
        lax.all_gather(w_out, "dp", axis=0, tiled=True),
    )
    projected = jnp.dot(normed_low, full_qkv, preferred_element_type=jnp.float32)
    projected = projected.astype(jnp.bfloat16)
    queries = projected[:, :inner_width]
    keys_all = projected[:, inner_width : 2 * inner_width]
    values_all = projected[:, 2 * inner_width :]
    history = from_behind(jnp.stack([keys_all, values_all]), "seq", 1)
    keys_ext = jnp.concatenate([history[0], keys_all], axis=0)
    values_ext = jnp.concatenate([history[1], values_all], axis=0)
    context, saved = attend_forward(
        queries, keys_ext, values_ext, visible(utt_span[0, 0], utt_span[1, 0], offset)
    )
    branch = jnp.dot(context, full_out, preferred_element_type=jnp.float32)
    d_context = against_rows(own_grad, full_out)
    branch = branch.astype(jnp.bfloat16)
    d_context = d_context.astype(jnp.bfloat16)
    d_queries, d_keys, d_values = attend_backward(saved, d_context)
    returned = from_behind(
        jnp.stack([d_keys[:halo_rows], d_values[:halo_rows]]).astype(jnp.bfloat16), "seq", -1
    ).astype(jnp.float32)
    d_keys_own = (
        d_keys[halo_rows:].at[frame_count - halo_rows :].add(returned[0]).astype(jnp.bfloat16)
    )
    d_values_own = (
        d_values[halo_rows:].at[frame_count - halo_rows :].add(returned[1]).astype(jnp.bfloat16)
    )
    d_proj = jnp.concatenate([d_queries, d_keys_own, d_values_own], axis=1)
    grad_qkv = lax.psum_scatter(
        joint_term(normed_low, d_proj), ("dp", "seq"), scatter_dimension=0, tiled=True
    )
    grad_out = lax.psum_scatter(
        joint_term(context, own_grad), ("dp", "seq"), scatter_dimension=0, tiled=True
    )
    d_normed = against_rows(d_proj, full_qkv)
    grad_in = inv_sigma * (
        d_normed
        - jnp.mean(d_normed, axis=-1, keepdims=True)
        - normed * jnp.mean(d_normed * normed, axis=-1, keepdims=True)
    )
    return (branch[None], grad_in.astype(jnp.bfloat16)[None], grad_qkv, grad_out)


def solution(mesh):
    in_specs = (
        P("dp", "seq", None),
        P("dp", "seq", None),
        P(None, "dp", "seq"),
        P("dp", None),
        P("dp", None),
    )
    out_specs = (
        P("dp", "seq", None),
        P("dp", "seq", None),
        P(("dp", "seq"), None),
        P(("dp", "seq"), None),
    )
    return jax.shard_map(body, mesh=mesh, in_specs=in_specs, out_specs=out_specs, check_vma=False)
```

profile of v0, /device:TPU:9, one launch (start us, length us, event | category | flops | bytes accessed | tf_op | source)
XLA Modules:
  0.0 1092.2 jit_solution(9958152777341482748)
XLA Ops:
  11.1 144.7 %all-gather.3.cloned.1.call-done = bf16[1536,2304]{1,0:T(8,128)(2,1)} async-done(((bf16[192,2304]{1,0:T(8,128)(2,1)}), bf16[1536,2304]{1,0:T(8,128)(2,1)}) %all-gather.3.cloned.1.call-update) | async-done | bytes 7077904 | tf_op jit(solution)/shard_map/all_gather | solution.py:126
  155.8 5.1 convolution_convert_fusion
  162.0 5.1 collective-permute-start
  167.5 55.3 %all-gather.5.cloned.1.call-done = bf16[768,1536]{1,0:T(8,128)(2,1)} async-done(((bf16[96,1536]{1,0:T(8,128)(2,1)}), bf16[768,1536]{1,0:T(8,128)(2,1)}) %all-gather.5.cloned.1.call-update) | async-done | bytes 2359312 | tf_op jit(solution)/shard_map/all_gather | solution.py:127
  222.8 2.5 convolution_convert_fusion.3
  234.2 2.1 slice_bitcast_fusion.12
  240.7 2.4 pad_maximum_fusion.5
  257.2 4.9 concatenate.42
  262.2 4.2 fusion.87
  266.4 5.8 concatenate.44
  272.2 6.3 fusion.86
  278.5 4.4 fusion.51
  282.9 2.8 convolution_bitcast_fusion
  285.6 6.9 copy.108
  299.3 24.8 %fusion.20 = f32[4,320,12,64]{1,3,2,0:T(8,128)} fusion(bf16[4,64,12,64]{1,3,2,0:T(8,128)(2,1)S(1)} %copy-done.19, f32[4,12,64,320]{3,2,1,0:T(8,128)} %fusion.87, f32[4,12,64,320]{3,2,1,0:T(8,128)} %get-tuple-element.190, f32[4,12,64]{2,1,0:T(8,128)S(1)} %get-tuple-element.189), kind=kOutput, calls=%fused_computation.20 | convolution fusion | flops 132713792 | bytes 12201984 | tf_op jit(solution)/shard_map/nhqk,nqhd->nkhd/dot_general | solution.py:29
  325.2 6.9 copy.100
  341.4 2.5 collective-permute-start.1
  343.9 24.3 %fusion.52 = bf16[4,64,12,64]{1,3,2,0:T(8,128)(2,1)S(1)} fusion(bf16[4,320,12,64]{1,3,2,0:T(8,128)(2,1)} %concatenate.44, f32[4,12,64,320]{3,2,1,0:T(8,128)} %fusion.87, f32[4,12,64,320]{3,2,1,0:T(8,128)} %get-tuple-element.190, f32[4,12,64]{2,1,0:T(8,128)} %copy-done.78), kind=kOutput, calls=%fused_computation.63 | convolution fusion | flops 132910400 | bytes 10235904 | tf_op jit(solution)/shard_map/nhqk,nkhd->nqhd/dot_general | solution.py:29
  371.2 2.0 copy.114
  374.1 3.4 fusion.41
  381.0 3.0 fusion.62
  386.8 7.3 fusion.65
  394.1 374.8 %fusion.84 = (f32[16,2304]{1,0:T(8,128)S(1)}, f32[8,1536]{1,0:T(8,128)S(1)}) fusion(f32[1536,2304]{1,0:T(8,128)} %fusion.65, f32[768,1536]{1,0:T(8,128)} %fusion.62), kind=kCustom, calls=%all-reduce-scatter.2 | all-reduce-scatter fusion | flops 6291458 | bytes 19070976
  772.9 25.4 %collective-permute-start.62 = (f32[8,1536]{1,0:T(8,128)S(1)}, f32[8,1536]{1,0:T(8,128)S(1)}, u32[]{:S(2)}, u32[]{:S(2)}) collective-permute-start(f32[8,1536]{1,0:T(8,128)S(1)} %get-tuple-element.171), channel_id=1, source_target_pairs={{0,29},{1,30},{2,31},{3,32},{4,33},{5,34},{6,35},{7,36},{8,37},{9,... | collective-permute-start | bytes 147464
  806.2 5.5 collective-permute-start.55
  811.7 5.6 collective-permute-start.54
  818.7 2.0 collective-permute-start.52
  820.7 2.9 collective-permute-start.51
  823.6 2.2 collective-permute-start.50
  828.5 3.1 collective-permute-start.47
  831.6 4.8 collective-permute-start.46
  837.8 2.0 collective-permute-start.44
  839.8 2.5 collective-permute-start.43
  842.3 5.1 collective-permute-start.42
  847.4 3.8 collective-permute-start.41
  855.4 2.0 collective-permute-start.33
  857.3 4.0 collective-permute-start.39
  861.4 3.4 collective-permute-start.38
  864.8 4.3 collective-permute-start.37
  869.1 3.0 collective-permute-start.36
  872.2 2.6 collective-permute-start.35
  874.8 4.3 collective-permute-start.34
  883.1 3.4 collective-permute-start.28
  886.5 2.0 collective-permute-start.27
  888.5 3.3 fusion.14
  891.8 3.1 collective-permute-start.26
  897.6 11.2 %collective-permute-done.28 = f32[16,2304]{1,0:T(8,128)S(1)} collective-permute-done((f32[16,2304]{1,0:T(8,128)S(1)}, f32[16,2304]{1,0:T(8,128)S(1)}, u32[]{:S(2)}, u32[]{:S(2)}) %collective-permute-start.28) | collective-permute-done | bytes 147488
  910.8 7.2 collective-permute-start.22
  918.1 5.3 fusion.83
  926.1 3.1 collective-permute-start.19
  929.2 2.2 collective-permute-start.18
  932.8 2.4 collective-permute-start.16
  935.2 3.7 collective-permute-start.15
  939.0 16.2 %collective-permute-start.14 = (f32[16,2304]{1,0:T(8,128)S(1)}, f32[16,2304]{1,0:T(8,128)S(1)}, u32[]{:S(2)}, u32[]{:S(2)}) collective-permute-start(f32[16,2304]{1,0:T(8,128)S(1)} %get-tuple-element.170), channel_id=1, source_target_pairs={{0,13},{1,14},{2,15},{3,16},{4,17},{5,18},{6,19},{7,20},{8,21},{9,... | collective-permute-start | bytes 442376
  957.8 2.0 collective-permute-start.11
  959.8 2.0 collective-permute-start.10
  961.8 6.5 collective-permute-start.9
  968.2 2.0 collective-permute-start.8
  970.2 3.3 collective-permute-start.7
  975.0 28.8 %concatenate.47 = f32[262,1536]{1,0:T(8,128)S(1)} concatenate(f32[6,1536]{1,0:T(8,128)} %copy-done.49, f32[8,1536]{1,0:T(8,128)S(1)} %collective-permute-done.64, f32[8,1536]{1,0:T(8,128)} %copy-done.50, f32[8,1536]{1,0:T(8,128)} %copy-done.51, f32[8,1536]{1,0:T(8,128)} %copy-done.52, f32[8,1536]{1,0:T(8,128)} %copy-done.53, f32[8,1536]{1,0:T(8,128)} %copy-done.54, ...), dimensions={0} | concatenate | bytes 3219456
  1003.8 9.1 collective-permute-start.6
  1016.8 4.6 collective-permute-start.3
  1021.4 3.7 collective-permute-start.2
  1027.5 56.0 %concatenate.46 = f32[524,2304]{1,0:T(8,128)} concatenate(f32[12,2304]{1,0:T(8,128)} %collective-permute-done.33, f32[16,2304]{1,0:T(8,128)} %collective-permute-done.32, f32[16,2304]{1,0:T(8,128)S(1)} %copy-done.22, f32[16,2304]{1,0:T(8,128)S(1)} %copy-done.24, f32[16,2304]{1,0:T(8,128)S(1)} %copy-done.26, f32[16,2304]{1,0:T(8,128)S(1)} %collective-permute-done.28, ...), dimensions={0} | concatenate | bytes 9658368
  (325 shorter events, 104.9 us)
Async XLA Ops:
  7.2 148.6 %all-gather.3.cloned.1.call-start = ((), (), s32[]{:S(2)}) async-start(), calls=%async_computation | async-start | bytes 7962624 | tf_op jit(solution)/shard_map/all_gather | solution.py:126
  7.9 214.9 %all-gather.5.cloned.1.call-start = ((), (), s32[]{:S(2)}) async-start(), calls=%async_computation.1 | async-start | bytes 2654208 | tf_op jit(solution)/shard_map/all_gather | solution.py:127
  162.0 72.2 %collective-permute-start = (bf16[2,256,768]{2,1,0:T(8,128)(2,1)}, bf16[2,256,768]{2,1,0:T(8,128)(2,1)}, u32[]{:S(2)}, u32[]{:S(2)}) collective-permute-start(bf16[2,256,768]{2,1,0:T(8,128)(2,1)} %pad_maximum_fusion.1), channel_id=1, source_target_pairs={{0,1},{1,2},{2,3},{3,4},{4,5},{5,6},{6,7},{7,8},{8,9},{9,10},{10,1... | collective-permute-start | bytes 2359304 | tf_op jit(solution)/shard_map/ppermute | solution.py:18
  341.4 42.6 %collective-permute-start.1 = (bf16[2,256,768]{1,2,0:T(8,128)(2,1)}, bf16[2,256,768]{1,2,0:T(8,128)(2,1)}, u32[]{:S(2)}, u32[]{:S(2)}) collective-permute-start(bf16[2,256,768]{1,2,0:T(8,128)(2,1)} %pad_maximum_fusion.2), channel_id=1, source_target_pairs={{1,0},{2,1},{3,2},{4,3},{5,4},{6,5},{7,6},{8,7},{9,8},{10,9},{11,1... | collective-permute-start | bytes 2359304 | tf_op jit(solution)/shard_map/ppermute | solution.py:18
  768.9 32.0 %collective-permute-start.64 = (f32[8,1536]{1,0:T(8,128)S(1)}, f32[8,1536]{1,0:T(8,128)S(1)}, u32[]{:S(2)}, u32[]{:S(2)}) collective-permute-start(f32[8,1536]{1,0:T(8,128)S(1)} %get-tuple-element.171), channel_id=1, source_target_pairs={{0,31},{1,32},{2,33},{3,34},{4,35},{5,36},{6,37},{7,38},{8,39},{9,... | collective-permute-start | bytes 147464
  770.3 29.3 %collective-permute-start.65 = (f32[6,1536]{1,0:T(8,128)S(1)}, f32[6,1536]{1,0:T(8,128)S(1)}, u32[]{:S(2)}, u32[]{:S(2)}) collective-permute-start(f32[6,1536]{1,0:T(8,128)S(1)} %slice.520), channel_id=1, source_target_pairs={{0,32},{1,33},{2,34},{3,35},{4,36},{5,37},{6,38},{7,39},{8,40},{9,... | collective-permute-start | bytes 110600
  771.6 30.6 %collective-permute-start.63 = (f32[8,1536]{1,0:T(8,128)S(1)}, f32[8,1536]{1,0:T(8,128)S(1)}, u32[]{:S(2)}, u32[]{:S(2)}) collective-permute-start(f32[8,1536]{1,0:T(8,128)S(1)} %get-tuple-element.171), channel_id=1, source_target_pairs={{0,30},{1,31},{2,32},{3,33},{4,34},{5,35},{6,36},{7,37},{8,38},{9,... | collective-permute-start | bytes 147464
  772.9 30.6 %collective-permute-start.62 = (f32[8,1536]{1,0:T(8,128)S(1)}, f32[8,1536]{1,0:T(8,128)S(1)}, u32[]{:S(2)}, u32[]{:S(2)}) collective-permute-start(f32[8,1536]{1,0:T(8,128)S(1)} %get-tuple-element.171), channel_id=1, source_target_pairs={{0,29},{1,30},{2,31},{3,32},{4,33},{5,34},{6,35},{7,36},{8,37},{9,... | collective-permute-start | bytes 147464
  800.9 10.8 collective-permute-start.59
  802.2 15.1 %collective-permute-start.58 = (f32[8,1536]{1,0:T(8,128)S(1)}, f32[8,1536]{1,0:T(8,128)S(1)}, u32[]{:S(2)}, u32[]{:S(2)}) collective-permute-start(f32[8,1536]{1,0:T(8,128)S(1)} %get-tuple-element.171), channel_id=1, source_target_pairs={{0,25},{1,26},{2,27},{3,28},{4,29},{5,30},{6,31},{7,32},{8,33},{9,... | collective-permute-start | bytes 147464
  803.6 15.1 %collective-permute-start.57 = (f32[8,1536]{1,0:T(8,128)S(1)}, f32[8,1536]{1,0:T(8,128)S(1)}, u32[]{:S(2)}, u32[]{:S(2)}) collective-permute-start(f32[8,1536]{1,0:T(8,128)S(1)} %get-tuple-element.171), channel_id=1, source_target_pairs={{0,24},{1,25},{2,26},{3,27},{4,28},{5,29},{6,30},{7,31},{8,32},{9,... | collective-permute-start | bytes 147464
  804.9 15.8 %collective-permute-start.56 = (f32[8,1536]{1,0:T(8,128)S(1)}, f32[8,1536]{1,0:T(8,128)S(1)}, u32[]{:S(2)}, u32[]{:S(2)}) collective-permute-start(f32[8,1536]{1,0:T(8,128)S(1)} %get-tuple-element.171), channel_id=1, source_target_pairs={{0,23},{1,24},{2,25},{3,26},{4,27},{5,28},{6,29},{7,30},{8,31},{9,... | collective-permute-start | bytes 147464
  806.2 17.4 %collective-permute-start.55 = (f32[8,1536]{1,0:T(8,128)S(1)}, f32[8,1536]{1,0:T(8,128)S(1)}, u32[]{:S(2)}, u32[]{:S(2)}) collective-permute-start(f32[8,1536]{1,0:T(8,128)S(1)} %get-tuple-element.171), channel_id=1, source_target_pairs={{0,22},{1,23},{2,24},{3,25},{4,26},{5,27},{6,28},{7,29},{8,30},{9,... | collective-permute-start | bytes 147464
  811.7 14.1 %collective-permute-start.54 = (f32[8,1536]{1,0:T(8,128)S(1)}, f32[8,1536]{1,0:T(8,128)S(1)}, u32[]{:S(2)}, u32[]{:S(2)}) collective-permute-start(f32[8,1536]{1,0:T(8,128)S(1)} %get-tuple-element.171), channel_id=1, source_target_pairs={{0,21},{1,22},{2,23},{3,24},{4,25},{5,26},{6,27},{7,28},{8,29},{9,... | collective-permute-start | bytes 147464
  817.3 9.8 collective-permute-start.53
  818.7 9.8 collective-permute-start.52
  820.7 10.9 collective-permute-start.51
  823.6 12.9 %collective-permute-start.50 = (f32[8,1536]{1,0:T(8,128)S(1)}, f32[8,1536]{1,0:T(8,128)S(1)}, u32[]{:S(2)}, u32[]{:S(2)}) collective-permute-start(f32[8,1536]{1,0:T(8,128)S(1)} %get-tuple-element.171), channel_id=1, source_target_pairs={{0,17},{1,18},{2,19},{3,20},{4,21},{5,22},{6,23},{7,24},{8,25},{9,... | collective-permute-start | bytes 147464
  825.8 12.0 %collective-permute-start.49 = (f32[8,1536]{1,0:T(8,128)S(1)}, f32[8,1536]{1,0:T(8,128)S(1)}, u32[]{:S(2)}, u32[]{:S(2)}) collective-permute-start(f32[8,1536]{1,0:T(8,128)S(1)} %get-tuple-element.171), channel_id=1, source_target_pairs={{0,16},{1,17},{2,18},{3,19},{4,20},{5,21},{6,22},{7,23},{8,24},{9,... | collective-permute-start | bytes 147464
  827.1 12.6 %collective-permute-start.48 = (f32[8,1536]{1,0:T(8,128)S(1)}, f32[8,1536]{1,0:T(8,128)S(1)}, u32[]{:S(2)}, u32[]{:S(2)}) collective-permute-start(f32[8,1536]{1,0:T(8,128)S(1)} %get-tuple-element.171), channel_id=1, source_target_pairs={{0,15},{1,16},{2,17},{3,18},{4,19},{5,20},{6,21},{7,22},{8,23},{9,... | collective-permute-start | bytes 147464
  828.5 13.8 %collective-permute-start.47 = (f32[8,1536]{1,0:T(8,128)S(1)}, f32[8,1536]{1,0:T(8,128)S(1)}, u32[]{:S(2)}, u32[]{:S(2)}) collective-permute-start(f32[8,1536]{1,0:T(8,128)S(1)} %get-tuple-element.171), channel_id=1, source_target_pairs={{0,14},{1,15},{2,16},{3,17},{4,18},{5,19},{6,20},{7,21},{8,22},{9,... | collective-permute-start | bytes 147464
  831.6 15.8 %collective-permute-start.46 = (f32[8,1536]{1,0:T(8,128)S(1)}, f32[8,1536]{1,0:T(8,128)S(1)}, u32[]{:S(2)}, u32[]{:S(2)}) collective-permute-start(f32[8,1536]{1,0:T(8,128)S(1)} %get-tuple-element.171), channel_id=1, source_target_pairs={{0,13},{1,14},{2,15},{3,16},{4,17},{5,18},{6,19},{7,20},{8,21},{9,... | collective-permute-start | bytes 147464
  836.5 14.7 %collective-permute-start.45 = (f32[8,1536]{1,0:T(8,128)S(1)}, f32[8,1536]{1,0:T(8,128)S(1)}, u32[]{:S(2)}, u32[]{:S(2)}) collective-permute-start(f32[8,1536]{1,0:T(8,128)S(1)} %get-tuple-element.171), channel_id=1, source_target_pairs={{0,12},{1,13},{2,14},{3,15},{4,16},{5,17},{6,18},{7,19},{8,20},{9,... | collective-permute-start | bytes 147464
  837.8 15.0 %collective-permute-start.44 = (f32[8,1536]{1,0:T(8,128)S(1)}, f32[8,1536]{1,0:T(8,128)S(1)}, u32[]{:S(2)}, u32[]{:S(2)}) collective-permute-start(f32[8,1536]{1,0:T(8,128)S(1)} %get-tuple-element.171), channel_id=1, source_target_pairs={{0,11},{1,12},{2,13},{3,14},{4,15},{5,16},{6,17},{7,18},{8,19},{9,... | collective-permute-start | bytes 147464
  839.8 15.6 %collective-permute-start.43 = (f32[8,1536]{1,0:T(8,128)S(1)}, f32[8,1536]{1,0:T(8,128)S(1)}, u32[]{:S(2)}, u32[]{:S(2)}) collective-permute-start(f32[8,1536]{1,0:T(8,128)S(1)} %get-tuple-element.171), channel_id=1, source_target_pairs={{0,10},{1,11},{2,12},{3,13},{4,14},{5,15},{6,16},{7,17},{8,18},{9,... | collective-permute-start | bytes 147464
  842.3 15.1 %collective-permute-start.42 = (f32[8,1536]{1,0:T(8,128)S(1)}, f32[8,1536]{1,0:T(8,128)S(1)}, u32[]{:S(2)}, u32[]{:S(2)}) collective-permute-start(f32[8,1536]{1,0:T(8,128)S(1)} %get-tuple-element.171), channel_id=1, source_target_pairs={{0,9},{1,10},{2,11},{3,12},{4,13},{5,14},{6,15},{7,16},{8,17},{9,1... | collective-permute-start | bytes 147464
  847.4 13.9 %collective-permute-start.41 = (f32[8,1536]{1,0:T(8,128)S(1)}, f32[8,1536]{1,0:T(8,128)S(1)}, u32[]{:S(2)}, u32[]{:S(2)}) collective-permute-start(f32[8,1536]{1,0:T(8,128)S(1)} %get-tuple-element.171), channel_id=1, source_target_pairs={{0,8},{1,9},{2,10},{3,11},{4,12},{5,13},{6,14},{7,15},{8,16},{9,17... | collective-permute-start | bytes 147464
  851.2 13.6 %collective-permute-start.40 = (f32[8,1536]{1,0:T(8,128)S(1)}, f32[8,1536]{1,0:T(8,128)S(1)}, u32[]{:S(2)}, u32[]{:S(2)}) collective-permute-start(f32[8,1536]{1,0:T(8,128)S(1)} %get-tuple-element.171), channel_id=1, source_target_pairs={{0,7},{1,8},{2,9},{3,10},{4,11},{5,12},{6,13},{7,14},{8,15},{9,16}... | collective-permute-start | bytes 147464
  853.4 33.1 %collective-permute-start.32 = (f32[16,2304]{1,0:T(8,128)S(1)}, f32[16,2304]{1,0:T(8,128)}, u32[]{:S(2)}, u32[]{:S(2)}) collective-permute-start(f32[16,2304]{1,0:T(8,128)S(1)} %get-tuple-element.170), channel_id=1, source_target_pairs={{0,31},{1,32},{2,33},{3,34},{4,35},{5,36},{6,37},{7,38},{8,39},{9,... | collective-permute-start | bytes 442376
  855.4 27.8 %collective-permute-start.33 = (f32[12,2304]{1,0:T(8,128)S(1)}, f32[12,2304]{1,0:T(8,128)}, u32[]{:S(2)}, u32[]{:S(2)}) collective-permute-start(f32[12,2304]{1,0:T(8,128)S(1)} %slice.519), channel_id=1, source_target_pairs={{0,32},{1,33},{2,34},{3,35},{4,36},{5,37},{6,38},{7,39},{8,40},{9,... | collective-permute-start | bytes 331784
  857.3 11.8 %collective-permute-start.39 = (f32[8,1536]{1,0:T(8,128)S(1)}, f32[8,1536]{1,0:T(8,128)S(1)}, u32[]{:S(2)}, u32[]{:S(2)}) collective-permute-start(f32[8,1536]{1,0:T(8,128)S(1)} %get-tuple-element.171), channel_id=1, source_target_pairs={{0,6},{1,7},{2,8},{3,9},{4,10},{5,11},{6,12},{7,13},{8,14},{9,15},... | collective-permute-start | bytes 147464
  861.4 10.8 collective-permute-start.38
  864.8 10.0 collective-permute-start.37
  869.1 10.1 collective-permute-start.36
  872.2 8.3 collective-permute-start.35
  879.2 12.7 %collective-permute-start.31 = (f32[16,2304]{1,0:T(8,128)S(1)}, f32[16,2304]{1,0:T(8,128)S(1)}, u32[]{:S(2)}, u32[]{:S(2)}) collective-permute-start(f32[16,2304]{1,0:T(8,128)S(1)} %get-tuple-element.170), channel_id=1, source_target_pairs={{0,30},{1,31},{2,32},{3,33},{4,34},{5,35},{6,36},{7,37},{8,38},{9,... | collective-permute-start | bytes 442376
  880.5 14.5 %collective-permute-start.30 = (f32[16,2304]{1,0:T(8,128)S(1)}, f32[16,2304]{1,0:T(8,128)S(1)}, u32[]{:S(2)}, u32[]{:S(2)}) collective-permute-start(f32[16,2304]{1,0:T(8,128)S(1)} %get-tuple-element.170), channel_id=1, source_target_pairs={{0,29},{1,30},{2,31},{3,32},{4,33},{5,34},{6,35},{7,36},{8,37},{9,... | collective-permute-start | bytes 442376
  881.8 14.5 %collective-permute-start.29 = (f32[16,2304]{1,0:T(8,128)S(1)}, f32[16,2304]{1,0:T(8,128)S(1)}, u32[]{:S(2)}, u32[]{:S(2)}) collective-permute-start(f32[16,2304]{1,0:T(8,128)S(1)} %get-tuple-element.170), channel_id=1, source_target_pairs={{0,28},{1,29},{2,30},{3,31},{4,32},{5,33},{6,34},{7,35},{8,36},{9,... | collective-permute-start | bytes 442376
  883.1 25.7 %collective-permute-start.28 = (f32[16,2304]{1,0:T(8,128)S(1)}, f32[16,2304]{1,0:T(8,128)S(1)}, u32[]{:S(2)}, u32[]{:S(2)}) collective-permute-start(f32[16,2304]{1,0:T(8,128)S(1)} %get-tuple-element.170), channel_id=1, source_target_pairs={{0,27},{1,28},{2,29},{3,30},{4,31},{5,32},{6,33},{7,34},{8,35},{9,... | collective-permute-start | bytes 442376
  886.5 23.6 %collective-permute-start.27 = (f32[16,2304]{1,0:T(8,128)S(1)}, f32[16,2304]{1,0:T(8,128)S(1)}, u32[]{:S(2)}, u32[]{:S(2)}) collective-permute-start(f32[16,2304]{1,0:T(8,128)S(1)} %get-tuple-element.170), channel_id=1, source_target_pairs={{0,26},{1,27},{2,28},{3,29},{4,30},{5,31},{6,32},{7,33},{8,34},{9,... | collective-permute-start | bytes 442376
  891.8 31.6 %collective-permute-start.26 = (f32[16,2304]{1,0:T(8,128)S(1)}, f32[16,2304]{1,0:T(8,128)S(1)}, u32[]{:S(2)}, u32[]{:S(2)}) collective-permute-start(f32[16,2304]{1,0:T(8,128)S(1)} %get-tuple-element.170), channel_id=1, source_target_pairs={{0,25},{1,26},{2,27},{3,28},{4,29},{5,30},{6,31},{7,32},{8,33},{9,... | collective-permute-start | bytes 442376
  895.0 29.7 %collective-permute-start.25 = (f32[16,2304]{1,0:T(8,128)S(1)}, f32[16,2304]{1,0:T(8,128)S(1)}, u32[]{:S(2)}, u32[]{:S(2)}) collective-permute-start(f32[16,2304]{1,0:T(8,128)S(1)} %get-tuple-element.170), channel_id=1, source_target_pairs={{0,24},{1,25},{2,26},{3,27},{4,28},{5,29},{6,30},{7,31},{8,32},{9,... | collective-permute-start | bytes 442376
  896.3 29.7 %collective-permute-start.24 = (f32[16,2304]{1,0:T(8,128)S(1)}, f32[16,2304]{1,0:T(8,128)S(1)}, u32[]{:S(2)}, u32[]{:S(2)}) collective-permute-start(f32[16,2304]{1,0:T(8,128)S(1)} %get-tuple-element.170), channel_id=1, source_target_pairs={{0,23},{1,24},{2,25},{3,26},{4,27},{5,28},{6,29},{7,30},{8,31},{9,... | collective-permute-start | bytes 442376
  908.9 20.3 %collective-permute-start.23 = (f32[16,2304]{1,0:T(8,128)S(1)}, f32[16,2304]{1,0:T(8,128)S(1)}, u32[]{:S(2)}, u32[]{:S(2)}) collective-permute-start(f32[16,2304]{1,0:T(8,128)S(1)} %get-tuple-element.170), channel_id=1, source_target_pairs={{0,22},{1,23},{2,24},{3,25},{4,26},{5,27},{6,28},{7,29},{8,30},{9,... | collective-permute-start | bytes 442376
  910.8 20.6 %collective-permute-start.22 = (f32[16,2304]{1,0:T(8,128)S(1)}, f32[16,2304]{1,0:T(8,128)S(1)}, u32[]{:S(2)}, u32[]{:S(2)}) collective-permute-start(f32[16,2304]{1,0:T(8,128)S(1)} %get-tuple-element.170), channel_id=1, source_target_pairs={{0,21},{1,22},{2,23},{3,24},{4,25},{5,26},{6,27},{7,28},{8,29},{9,... | collective-permute-start | bytes 442376
  923.4 9.3 collective-permute-start.21
  924.8 10.4 collective-permute-start.20
  926.1 12.9 %collective-permute-start.19 = (f32[16,2304]{1,0:T(8,128)S(1)}, f32[16,2304]{1,0:T(8,128)S(1)}, u32[]{:S(2)}, u32[]{:S(2)}) collective-permute-start(f32[16,2304]{1,0:T(8,128)S(1)} %get-tuple-element.170), channel_id=1, source_target_pairs={{0,18},{1,19},{2,20},{3,21},{4,22},{5,23},{6,24},{7,25},{8,26},{9,... | collective-permute-start | bytes 442376
  929.2 26.0 %collective-permute-start.18 = (f32[16,2304]{1,0:T(8,128)S(1)}, f32[16,2304]{1,0:T(8,128)S(1)}, u32[]{:S(2)}, u32[]{:S(2)}) collective-permute-start(f32[16,2304]{1,0:T(8,128)S(1)} %get-tuple-element.170), channel_id=1, source_target_pairs={{0,17},{1,18},{2,19},{3,20},{4,21},{5,22},{6,23},{7,24},{8,25},{9,... | collective-permute-start | bytes 442376
  931.4 25.1 %collective-permute-start.17 = (f32[16,2304]{1,0:T(8,128)S(1)}, f32[16,2304]{1,0:T(8,128)S(1)}, u32[]{:S(2)}, u32[]{:S(2)}) collective-permute-start(f32[16,2304]{1,0:T(8,128)S(1)} %get-tuple-element.170), channel_id=1, source_target_pairs={{0,16},{1,17},{2,18},{3,19},{4,20},{5,21},{6,22},{7,23},{8,24},{9,... | collective-permute-start | bytes 442376
  932.8 25.1 %collective-permute-start.16 = (f32[16,2304]{1,0:T(8,128)S(1)}, f32[16,2304]{1,0:T(8,128)S(1)}, u32[]{:S(2)}, u32[]{:S(2)}) collective-permute-start(f32[16,2304]{1,0:T(8,128)S(1)} %get-tuple-element.170), channel_id=1, source_target_pairs={{0,15},{1,16},{2,17},{3,18},{4,19},{5,20},{6,21},{7,22},{8,23},{9,... | collective-permute-start | bytes 442376
  935.2 24.6 %collective-permute-start.15 = (f32[16,2304]{1,0:T(8,128)S(1)}, f32[16,2304]{1,0:T(8,128)S(1)}, u32[]{:S(2)}, u32[]{:S(2)}) collective-permute-start(f32[16,2304]{1,0:T(8,128)S(1)} %get-tuple-element.170), channel_id=1, source_target_pairs={{0,14},{1,15},{2,16},{3,17},{4,18},{5,19},{6,20},{7,21},{8,22},{9,... | collective-permute-start | bytes 442376
  939.0 22.8 %collective-permute-start.14 = (f32[16,2304]{1,0:T(8,128)S(1)}, f32[16,2304]{1,0:T(8,128)S(1)}, u32[]{:S(2)}, u32[]{:S(2)}) collective-permute-start(f32[16,2304]{1,0:T(8,128)S(1)} %get-tuple-element.170), channel_id=1, source_target_pairs={{0,13},{1,14},{2,15},{3,16},{4,17},{5,18},{6,19},{7,20},{8,21},{9,... | collective-permute-start | bytes 442376
  955.2 13.1 %collective-permute-start.13 = (f32[16,2304]{1,0:T(8,128)S(1)}, f32[16,2304]{1,0:T(8,128)S(1)}, u32[]{:S(2)}, u32[]{:S(2)}) collective-permute-start(f32[16,2304]{1,0:T(8,128)S(1)} %get-tuple-element.170), channel_id=1, source_target_pairs={{0,12},{1,13},{2,14},{3,15},{4,16},{5,17},{6,18},{7,19},{8,20},{9,... | collective-permute-start | bytes 442376
  956.5 13.7 %collective-permute-start.12 = (f32[16,2304]{1,0:T(8,128)S(1)}, f32[16,2304]{1,0:T(8,128)S(1)}, u32[]{:S(2)}, u32[]{:S(2)}) collective-permute-start(f32[16,2304]{1,0:T(8,128)S(1)} %get-tuple-element.170), channel_id=1, source_target_pairs={{0,11},{1,12},{2,13},{3,14},{4,15},{5,16},{6,17},{7,18},{8,19},{9,... | collective-permute-start | bytes 442376
  957.8 46.0 %collective-permute-start.11 = (f32[16,2304]{1,0:T(8,128)S(1)}, f32[16,2304]{1,0:T(8,128)}, u32[]{:S(2)}, u32[]{:S(2)}) collective-permute-start(f32[16,2304]{1,0:T(8,128)S(1)} %get-tuple-element.170), channel_id=1, source_target_pairs={{0,10},{1,11},{2,12},{3,13},{4,14},{5,15},{6,16},{7,17},{8,18},{9,... | collective-permute-start | bytes 442376
  959.8 53.2 %collective-permute-start.10 = (f32[16,2304]{1,0:T(8,128)S(1)}, f32[16,2304]{1,0:T(8,128)}, u32[]{:S(2)}, u32[]{:S(2)}) collective-permute-start(f32[16,2304]{1,0:T(8,128)S(1)} %get-tuple-element.170), channel_id=1, source_target_pairs={{0,9},{1,10},{2,11},{3,12},{4,13},{5,14},{6,15},{7,16},{8,17},{9,1... | collective-permute-start | bytes 442376
  961.8 53.1 %collective-permute-start.9 = (f32[16,2304]{1,0:T(8,128)S(1)}, f32[16,2304]{1,0:T(8,128)}, u32[]{:S(2)}, u32[]{:S(2)}) collective-permute-start(f32[16,2304]{1,0:T(8,128)S(1)} %get-tuple-element.170), channel_id=1, source_target_pairs={{0,8},{1,9},{2,10},{3,11},{4,12},{5,13},{6,14},{7,15},{8,16},{9,17... | collective-permute-start | bytes 442376
  968.2 48.6 %collective-permute-start.8 = (f32[16,2304]{1,0:T(8,128)S(1)}, f32[16,2304]{1,0:T(8,128)}, u32[]{:S(2)}, u32[]{:S(2)}) collective-permute-start(f32[16,2304]{1,0:T(8,128)S(1)} %get-tuple-element.170), channel_id=1, source_target_pairs={{0,7},{1,8},{2,9},{3,10},{4,11},{5,12},{6,13},{7,14},{8,15},{9,16}... | collective-permute-start | bytes 442376
  970.2 51.2 %collective-permute-start.7 = (f32[16,2304]{1,0:T(8,128)S(1)}, f32[16,2304]{1,0:T(8,128)}, u32[]{:S(2)}, u32[]{:S(2)}) collective-permute-start(f32[16,2304]{1,0:T(8,128)S(1)} %get-tuple-element.170), channel_id=1, source_target_pairs={{0,6},{1,7},{2,8},{3,9},{4,10},{5,11},{6,12},{7,13},{8,14},{9,15},... | collective-permute-start | bytes 442376
  1003.8 21.9 %collective-permute-start.6 = (f32[16,2304]{1,0:T(8,128)S(1)}, f32[16,2304]{1,0:T(8,128)S(1)}, u32[]{:S(2)}, u32[]{:S(2)}) collective-permute-start(f32[16,2304]{1,0:T(8,128)S(1)} %get-tuple-element.170), channel_id=1, source_target_pairs={{0,5},{1,6},{2,7},{3,8},{4,9},{5,10},{6,11},{7,12},{8,13},{9,14},{... | collective-permute-start | bytes 442376
  1013.0 12.8 %collective-permute-start.5 = (f32[16,2304]{1,0:T(8,128)S(1)}, f32[16,2304]{1,0:T(8,128)S(1)}, u32[]{:S(2)}, u32[]{:S(2)}) collective-permute-start(f32[16,2304]{1,0:T(8,128)S(1)} %get-tuple-element.170), channel_id=1, source_target_pairs={{0,4},{1,5},{2,6},{3,7},{4,8},{5,9},{6,10},{7,11},{8,12},{9,13},{1... | collective-permute-start | bytes 442376
  1014.9 10.9 collective-permute-start.4
  1016.8 9.7 collective-permute-start.3
  (83 other events, 2206.1 us)
Sparse Core Ops, SparseCore 0:
  9.7 146.0 all-gather.2
  157.5 65.2 all-gather.4
where the time goes:
time: 1110 us; the launch traced here: 1090 us
  blocking collectives  375 us (34%)
  waiting for transfers between devices  214 us (19%)
  starting transfers between devices  211 us (19%)
  local copies, waits for them, and re-layouts  166 us (15%)
  matrix products  93.3 us (8%)
  other arithmetic  16.8 us (2%)
  between operations  16.5 us (1%)
    unnamed x1, blocking collectives  375 us
    unnamed x64, starting transfers between devices  203 us
    all_gather x1, waiting for transfers between devices, body(): lax.all_gather(w_qkv, 'dp', axis=0, tiled=True)  145 us
    unnamed x164, local copies, waits for them, and re-layouts  95.2 us
    dot_general x5, matrix products, contract(): return jnp.einsum(form, left, right, preferred_element_type=jnp.float32)  60.5 us
    all_gather x1, waiting for transfers between devices, body(): lax.all_gather(w_out, 'dp', axis=0, tiled=True)  55.3 us
    slice x20, local copies, waits for them, and re-layouts, windows(): blocked[shift_by:shift_by + stretch_count]  22.7 us
  transfers between devices with their start and end apart: 68, of which 5 were waited for; matrix products, arithmetic and copies ran while one was open for 9% of the time, Pallas kernels for 0%

commit v1 on v0

v1 whole, which is shorter than its diff:
```python
import functools

import jax
import jax.numpy as jnp
from jax import lax
from jax.experimental import pallas as pl
from jax.experimental.pallas import tpu as pltpu
from jax.sharding import Mesh
from jax.sharding import PartitionSpec as P

HEAD_DIM = 64
STRETCH = 64
PRIOR = 4
WINDOW = (PRIOR + 1) * STRETCH
PAIR = 2 * HEAD_DIM
EPS = 1e-05

BF = jnp.bfloat16
F32 = jnp.float32


def nt(a, b):
    return lax.dot_general(a, b, (((1,), (1,)), ((), ())), preferred_element_type=F32)


def tn(a, b):
    return lax.dot_general(a, b, (((0,), (0,)), ((), ())), preferred_element_type=F32)


def nn(a, b):
    return lax.dot_general(a, b, (((1,), (0,)), ((), ())), preferred_element_type=F32)


def attend(first, lo_ref, hi_ref, proj_ref, dctx_ref, ctx_ref, dq_ref, dk_ref, dv_ref):
    width = ctx_ref.shape[1]
    blocks = ctx_ref.shape[0] // STRETCH
    dk_ref[...] = jnp.zeros_like(dk_ref)
    dv_ref[...] = jnp.zeros_like(dv_ref)
    lanes = lax.broadcasted_iota(jnp.int32, (STRETCH, PAIR), 1) < HEAD_DIM
    key_at = lax.broadcasted_iota(jnp.int32, (WINDOW, PAIR), 0)

    def stack(value):
        none = jnp.zeros_like(value)
        return jnp.concatenate(
            [jnp.where(lanes, value, none), jnp.where(lanes, none, value)], axis=0
        )

    def unstack(value):
        return jnp.where(lanes, value[:STRETCH], value[STRETCH:])

    for b in range(blocks):
        rows = pl.ds(b * STRETCH, STRETCH)
        seen = (key_at >= lo_ref[b : b + 1, :]) & (key_at < hi_ref[b : b + 1, :])
        for pair in range(width // PAIR):
            cols = pl.ds(pair * PAIR, PAIR)
            window = pl.ds(b * STRETCH, WINDOW)
            queries = stack(
                proj_ref[pl.ds(first + PRIOR * STRETCH + b * STRETCH, STRETCH), cols]
            )
            source = pl.ds(first + b * STRETCH, WINDOW)
            keys = proj_ref[source, pl.ds(width + pair * PAIR, PAIR)]
            values = proj_ref[source, pl.ds(2 * width + pair * PAIR, PAIR)]
            d_out = stack(dctx_ref[rows, cols])
            scores = jnp.where(seen, nt(keys, queries) * HEAD_DIM ** (-0.5), -1e30)
            weights = jnp.exp(scores - jnp.max(scores, axis=0, keepdims=True))
            probs = weights * (1.0 / jnp.sum(weights, axis=0, keepdims=True))
            low = probs.astype(BF)
            d_probs = nt(values, d_out)
            centre = jnp.sum(probs * d_probs, axis=0, keepdims=True)
            d_scores = (probs * (d_probs - centre) * HEAD_DIM ** (-0.5)).astype(BF)
            ctx_ref[rows, cols] = unstack(tn(low, values)).astype(BF)
            dq_ref[rows, cols] = unstack(tn(d_scores, keys)).astype(BF)
            dk_ref[window, cols] += nn(d_scores, queries)
            dv_ref[window, cols] += nn(low, d_out)


def attention(first, lo, hi, proj, d_context):
    queries, width = d_context.shape
    ext = queries + PRIOR * STRETCH
    whole = pl.BlockSpec(memory_space=pltpu.VMEM)
    return pl.pallas_call(
        functools.partial(attend, first),
        in_specs=[whole] * 4,
        out_specs=[whole] * 4,
        out_shape=[
            jax.ShapeDtypeStruct((queries, width), BF),
            jax.ShapeDtypeStruct((queries, width), BF),
            jax.ShapeDtypeStruct((ext, width), F32),
            jax.ShapeDtypeStruct((ext, width), F32),
        ],
        compiler_params=pltpu.CompilerParams(vmem_limit_bytes=40 * 1024 * 1024),
        name="attend",
    )(lo, hi, proj, d_context)


def normalize(inputs):
    widened = inputs.astype(F32)
    centered = widened - jnp.mean(widened, axis=-1, keepdims=True)
    inv_sigma = lax.rsqrt(jnp.mean(centered * centered, axis=-1, keepdims=True) + EPS)
    return (centered * inv_sigma, inv_sigma)


DP, CHIPS, CORES = 8, 8, 2
ALL = ("dp", "t", "c")


def device(dp, t, c):
    return (dp * CHIPS + t) * CORES + c


EVERY = [(d, t, c) for d in range(DP) for t in range(CHIPS) for c in range(CORES)]
SWAP = [(device(d, t, c), device(d, t, 1 - c)) for d, t, c in EVERY]
ONWARD = [(device(d, t, c), device(d, t + 1, c)) for d, t, c in EVERY if t + 1 < CHIPS]
BACK = [(device(d, t, c), device(d, t - 1, c)) for d, t, c in EVERY if t > 0]
OWNER = [(device(d, t, c), c * DP * CHIPS + d * CHIPS + t) for d, t, c in EVERY]


def swap(value):
    return lax.ppermute(value, ALL, SWAP)


def spread(grad):
    rows, columns = grad.shape
    third = columns // 4
    to = lax.broadcasted_iota(jnp.int32, (rows // 6 * 8, rows), 0)
    at = lax.broadcasted_iota(jnp.int32, (rows // 6 * 8, rows), 1)
    base = to // 8 * 6
    slot = to % 8
    keep = ((slot < 6) & (at == base + slot)).astype(BF)
    parts = []
    for b in range(3):
        tail = (((slot == 6) & (at == base + b)) | ((slot == 7) & (at == base + 3 + b))).astype(BF)
        parts.append(nn(keep, grad[:, b * third : (b + 1) * third]) + nn(tail, grad[:, 3 * third :]))
    return jnp.concatenate(parts, axis=1).astype(BF)


def gather(shard):
    copies = jnp.broadcast_to(shard[None], (DP,) + shard.shape)
    return lax.all_to_all(copies, "dp", 0, 0, tiled=True)


def body(frames, upstream, utt_span, w_qkv, w_out):
    core = lax.axis_index("c")
    lower = core == 0
    own_frames = frames[0]
    own_grad = upstream[0]
    count, wide = own_frames.shape
    inner = w_qkv.shape[1] // 3
    width = inner // CORES
    halo = PRIOR * STRETCH

    def both(own):
        other = swap(own)
        return jnp.concatenate(
            [jnp.where(lower, own, other), jnp.where(lower, other, own)], axis=0
        )

    normed, inv_sigma = normalize(own_frames)
    own_low = normed.astype(BF)
    low = both(own_low)
    history = lax.ppermute(low[count:], ALL, ONWARD)
    low_ext = jnp.concatenate([history, low], axis=0)
    grad_all = both(own_grad)

    spans = jnp.swapaxes(utt_span[:, 0], 0, 1)
    spans = both(spans).T - lax.axis_index("t") * (CORES * count) + halo
    blocked = spans.reshape(2, -1, STRETCH)
    blocked = blocked - (jnp.arange(blocked.shape[1], dtype=jnp.int32) * STRETCH)[None, :, None]
    blocked = jnp.concatenate([blocked, blocked], axis=-1)
    half = blocked.shape[1] // 2

    mine = lax.dynamic_index_in_dim(
        w_qkv.reshape(-1, 3, CORES, width), core, axis=2, keepdims=False
    ).reshape(-1, 3 * width)
    full_qkv = gather(mine).reshape(wide, 3 * width)
    out_cols = wide // CORES
    out_mine = gather(
        lax.dynamic_slice_in_dim(w_out, core * out_cols, out_cols, axis=1)
    ).reshape(inner, out_cols)
    out_kept = lax.dynamic_slice_in_dim(out_mine, core * width, width, axis=0)
    out_other = swap(lax.dynamic_slice_in_dim(out_mine, (1 - core) * width, width, axis=0))
    full_out = jnp.concatenate(
        [jnp.where(lower, out_kept, out_other), jnp.where(lower, out_other, out_kept)], axis=1
    )

    projected = nn(low_ext, full_qkv).astype(BF)
    d_context = nt(grad_all, full_out).astype(BF)

    ctx_a, dq_a, dk_a, dv_a = attention(
        0, blocked[0, :half], blocked[1, :half], projected, d_context[:count]
    )
    returned = lax.ppermute(
        jnp.concatenate([dk_a[:halo], dv_a[:halo]], axis=1).astype(BF), ALL, BACK
    ).astype(F32)
    ctx_b, dq_b, dk_b, dv_b = attention(
        count, blocked[0, half:], blocked[1, half:], projected, d_context[count:]
    )
    context = jnp.concatenate([ctx_a, ctx_b], axis=0)
    partial = nn(context, full_out)
    kept = lax.dynamic_slice_in_dim(partial, core * count, count, axis=0)
    other = swap(lax.dynamic_slice_in_dim(partial, (1 - core) * count, count, axis=0).astype(BF))
    branch = (kept + other.astype(F32)).astype(BF)

    d_low = jnp.concatenate([dk_a[halo:] + dk_b[:halo], dv_a[halo:] + dv_b[:halo]], axis=1)
    d_high = jnp.concatenate([dk_b[halo:], dv_b[halo:]], axis=1) + returned
    d_proj = jnp.concatenate(
        [
            jnp.concatenate([dq_a, d_low.astype(BF)], axis=1),
            jnp.concatenate([dq_b, d_high.astype(BF)], axis=1),
        ],
        axis=0,
    )
    grad_out = spread(tn(context, grad_all).astype(BF))
    grad_qkv = tn(low, d_proj).astype(BF)
    chips = DP * CHIPS
    sent = jnp.concatenate(
        [grad_qkv.reshape(chips, -1, 3 * width), grad_out.reshape(chips, -1, 3 * width)], axis=1
    )
    arrived = lax.all_to_all(sent, ("dp", "t"), 0, 0, tiled=True)
    total = jnp.sum(arrived.astype(F32), axis=0)
    rows = wide // chips // CORES
    q_total, o_total = total[: CORES * rows], total[CORES * rows :]
    q_kept = lax.dynamic_slice_in_dim(q_total, core * rows, rows, axis=0)
    q_other = swap(lax.dynamic_slice_in_dim(q_total, (1 - core) * rows, rows, axis=0))
    q_kept = q_kept.reshape(rows, 3, 1, width)
    q_other = q_other.reshape(rows, 3, 1, width)
    q_out = jnp.concatenate(
        [jnp.where(lower, q_kept, q_other), jnp.where(lower, q_other, q_kept)], axis=2
    ).reshape(rows, 3 * inner)
    o_rows = inner // chips // CORES
    o_out = jnp.concatenate(
        [o_total[:o_rows], o_total[o_rows:].reshape(o_rows, wide - 3 * width)], axis=1
    )
    o_out = lax.ppermute(o_out, ALL, OWNER)

    d_partial = nt(d_proj, full_qkv)
    d_kept = lax.dynamic_slice_in_dim(d_partial, core * count, count, axis=0)
    d_other = swap(
        lax.dynamic_slice_in_dim(d_partial, (1 - core) * count, count, axis=0).astype(BF)
    )
    d_normed = d_kept + d_other.astype(F32)
    grad_in = inv_sigma * (
        d_normed
        - jnp.mean(d_normed, axis=-1, keepdims=True)
        - normed * jnp.mean(d_normed * normed, axis=-1, keepdims=True)
    )
    return (branch[None], grad_in.astype(BF)[None], q_out, o_out)


def solution(mesh):
    fine = Mesh(mesh.devices.reshape(DP, CHIPS, CORES), ALL)
    rows = P("dp", ("t", "c"), None)
    in_specs = (rows, rows, P(None, "dp", ("t", "c")), P("dp", None), P("dp", None))
    out_specs = (rows, rows, P(ALL, None), P(ALL, None))
    return jax.shard_map(body, mesh=fine, in_specs=in_specs, out_specs=out_specs, check_vma=False)
```

time: 1110 us -> 213 us (0.19); the launches traced: 1090 us -> 212 us
  blocking collectives: 375 us -> 0 us
  starting transfers between devices: 211 us -> 49.6 us
  local copies, waits for them, and re-layouts: 166 us -> 14.5 us
  waiting for transfers between devices: 214 us -> 98.2 us
  matrix products: 93.3 us -> 20.4 us
  between operations: 16.5 us -> 1.27 us
    unnamed x1 -> x0, blocking collectives: 375 us -> none
    unnamed x64 -> x0, starting transfers between devices: 203 us -> none
    all_gather x2 -> x0, waiting for transfers between devices: 200 us -> none  [the longest x1 145 us: body(): lax.all_gather(w_qkv, 'dp', axis=0, tiled=True)]
    unnamed x164 -> x44, local copies, waits for them, and re-layouts: 95.2 us -> 4.81 us
    dot_general x11 -> x12, matrix products: 87 us -> 20.4 us  [the longest x8 11.9 us: nn(): lax.dot_general(a, b, (((1,), (0,)), ((), ())), preferred_element_type=F32)]
    ppermute x2 -> x10, waiting for transfers between devices: 0.01 us -> 51.8 us  [the longest x1 45.5 us: body(): history = lax.ppermute(low[count:], ALL, ONWARD)]
    all_to_all x0 -> x3, waiting for transfers between devices: none -> 46.3 us  [the longest x1 37 us: body(): arrived = lax.all_to_all(sent, ('dp', 't'), 0, 0, tiled=True)]
    slice x28 -> x6, local copies, waits for them, and re-layouts: 27.8 us -> 0.11 us  [the longest x1 0.04 us: body(): d_context[count:]]
  transfers between devices with their start and end apart: 68 -> 13, of which waited for: 5 -> 4; matrix products, arithmetic and copies ran while one was open for 9% -> 14% of each run, Pallas kernels for 0% -> 0%
where the time goes in v1:
time: 213 us; the launch traced here: 212 us
  waiting for transfers between devices  98.2 us (46%)
  starting transfers between devices  49.6 us (23%)
  matrix products  20.4 us (10%)
  other arithmetic  18.1 us (8%)
  local copies, waits for them, and re-layouts  14.5 us (7%)
  Pallas kernels  10.2 us (5%)
    ppermute x1, waiting for transfers between devices, body(): history = lax.ppermute(low[count:], ALL, ONWARD)  45.5 us
    all_to_all x1, waiting for transfers between devices, body(): arrived = lax.all_to_all(sent, ('dp', 't'), 0, 0, tiled=True)  37 us
    ppermute x1, starting transfers between devices, body(): o_out = lax.ppermute(o_out, ALL, OWNER)  15 us
    dot_general x8, matrix products, nn(): lax.dot_general(a, b, (((1,), (0,)), ((), ())), preferred_element_type=F32)  11.9 us
    all_to_all x2, starting transfers between devices, gather(): return lax.all_to_all(copies, 'dp', 0, 0, tiled=True)  10.6 us
    pallas_call x2, Pallas kernels, attention(): pl.pallas_call(functools.partial(attend, first), in_specs=[whole] * 4, ou...  10.2 us
    all_to_all x1, starting transfers between devices, body(): arrived = lax.all_to_all(sent, ('dp', 't'), 0, 0, tiled=True)  9.53 us
    all_to_all x2, waiting for transfers between devices, gather(): return lax.all_to_all(copies, 'dp', 0, 0, tiled=True)  9.33 us
  transfers between devices with their start and end apart: 13, of which 4 were waited for; matrix products, arithmetic and copies ran while one was open for 14% of the time, Pallas kernels for 0%

profile of v1, /device:TPU:9, one launch (start us, length us, event | category | flops | bytes accessed | tf_op | source)
XLA Modules:
  0.0 212.3 jit_solution(13776224499582717185)
XLA Ops:
  0.6 0.0 copy-start
  0.6 0.7 copy.21
  1.4 0.7 collective-permute-start
  2.1 0.0 copy-start.1
  2.1 1.1 broadcast_in_dim.12
  3.2 6.0 %all-to-all-start.1 = ((bf16[8,96,768]{2,1,0:T(8,128)(2,1)}), bf16[8,96,768]{2,1,0:T(8,128)(2,1)S(1)}, u32[]{:S(2)}, u32[]{:S(2)}) async-start(bf16[8,96,768]{2,1,0:T(8,128)(2,1)} %broadcast_in_dim.12), calls=%async_computation.1 | async-start | bytes 2359296 | tf_op jit(solution)/shard_map/all_to_all | solution.py:139
  9.1 0.2 convert_reduce_fusion.1
  9.3 0.3 fusion.15
  9.7 1.2 fusion.10
  10.9 0.5 collective-permute-start.1
  11.4 2.2 %reshape.111 = bf16[192,3,2,384]{3,2,1,0:T(2,128)(2,1)S(1)} reshape(bf16[192,2304]{1,0:T(8,128)(2,1)} %param.8) | data formatting | bytes 1769472 | tf_op jit(solution)/shard_map/reshape | solution.py:173
  13.6 2.9 %dynamic-slice_reduce_fusion = bf16[192,3,384]{2,1,0:T(4,128)(2,1)S(1)} fusion(bf16[192,3,2,384]{3,2,1,0:T(2,128)(2,1)S(1)} %reshape.111, s32[]{:T(128)S(6)} %select_n.143), kind=kLoop, calls=%fused_computation.53 | loop fusion | bytes 884740 | tf_op jit(solution)/shard_map/jit(dynamic_index_in_dim)/dynamic_slice | solution.py:172
  16.5 0.1 copy.15
  16.6 9.3 %all-to-all-done.1 = bf16[8,96,768]{2,1,0:T(8,128)(2,1)S(1)} async-done(((bf16[8,96,768]{2,1,0:T(8,128)(2,1)}), bf16[8,96,768]{2,1,0:T(8,128)(2,1)S(1)}, u32[]{:S(2)}, u32[]{:S(2)}) %all-to-all-start.1) | async-done | bytes 1179680 | tf_op jit(solution)/shard_map/all_to_all | solution.py:139
  25.9 2.2 %broadcast_in_dim.11 = bf16[8,192,1152]{2,1,0:T(8,128)(2,1)} broadcast(bf16[192,1152]{1,0:T(8,128)(2,1)S(1)} %bitcast.73), dimensions={1,2} | broadcast | bytes 3981312 | tf_op jit(solution)/shard_map/broadcast_in_dim | solution.py:138
  28.1 4.6 %all-to-all-start = ((bf16[8,192,1152]{2,1,0:T(8,128)(2,1)}), bf16[8,192,1152]{2,1,0:T(8,128)(2,1)}, u32[]{:S(2)}, u32[]{:S(2)}) async-start(bf16[8,192,1152]{2,1,0:T(8,128)(2,1)} %broadcast_in_dim.11), calls=%async_computation | async-start | bytes 7077888 | tf_op jit(solution)/shard_map/all_to_all | solution.py:139
  32.8 0.1 reshape.110
  32.9 0.1 broadcast_subtract_fusion
  33.0 0.1 fusion.97
  33.1 1.4 collective-permute-start.4
  34.5 2.5 %broadcast_select_fusion.2 = (bf16[256,1536]{1,0:T(8,128)(2,1)}, bf16[256,1536]{1,0:T(8,128)(2,1)S(1)}) fusion(bf16[256,1536]{1,0:T(8,128)(2,1)} %collective-permute-done.1, pred[]{:T(512)S(6)} %eq.48, f32[256]{0:T(256)S(1)} %add_rsqrt_fusion, f32[256]{0:T(256)S(1)} %broadcast_multiply_fusion.2, bf16[1,256,1536]{2,1,0:T(8,128)(2,1)S(1)} %copy-done.1), kind=kLoop, calls=%fused_computation.72 | loop fusion | flops 2359296 | bytes 3147777 | tf_op jit(solution)/shard_map/jit(_where)/select_n | solution.py:155
  37.0 4.5 %collective-permute-start.2 = (bf16[256,1536]{1,0:T(8,128)(2,1)S(1)}, bf16[256,1536]{1,0:T(8,128)(2,1)}, u32[]{:S(2)}, u32[]{:S(2)}) collective-permute-start(bf16[256,1536]{1,0:T(8,128)(2,1)S(1)} %get-tuple-element.27), channel_id=1, source_target_pairs={{0,2},{1,3},{2,4},{3,5},{4,6},{5,7},{6,8},{7,9},{8,10},{9,11},{10,... | collective-permute-start | bytes 2359304 | tf_op jit(solution)/shard_map/ppermute | solution.py:161
  41.6 1.5 broadcast_select_fusion.1
  43.1 0.3 broadcast_select_fusion.5
  43.4 0.0 copy-start.7
  43.4 1.0 convolution_convert_fusion.3
  44.5 45.5 %collective-permute-done.2 = bf16[256,1536]{1,0:T(8,128)(2,1)} collective-permute-done((bf16[256,1536]{1,0:T(8,128)(2,1)S(1)}, bf16[256,1536]{1,0:T(8,128)(2,1)}, u32[]{:S(2)}, u32[]{:S(2)}) %collective-permute-start.2) | collective-permute-done | bytes 786464 | tf_op jit(solution)/shard_map/ppermute | solution.py:161
  90.0 5.7 %convolution_convert_fusion.1.proj_ref = bf16[768,1152]{1,0:T(8,128)(2,1)S(1)} fusion(bf16[1536,1152]{1,0:T(8,128)(2,1)} %bitcast.5, bf16[256,1536]{1,0:T(8,128)(2,1)} %copy-done.9, bf16[256,1536]{1,0:T(8,128)(2,1)S(1)} %copy-done.7, bf16[256,1536]{1,0:T(8,128)(2,1)} %collective-permute-done.2), kind=kOutput, calls=%fused_computation.3 | convolution fusion | flops 2725871616 | bytes 7667712 | tf_op jit(solution)/shard_map/dot_general | solution.py:31
  95.7 5.1 %attend.2 = (bf16[256,384]{1,0:T(8,128)(2,1)S(1)}, bf16[256,384]{1,0:T(8,128)(2,1)S(1)}, f32[512,384]{1,0:T(8,128)S(1)}, f32[512,384]{1,0:T(8,128)S(1)}) custom-call(s32[4,128]{1,0:T(4,128)S(1)} %get-tuple-element.39.lo_ref, s32[4,128]{1,0:T(4,128)S(1)} %get-tuple-element.37.hi_ref, bf16[768,1152]{1,0:T(8,128)(2,1)S(1)} %convolution_convert_fusion.1.proj_ref, ...), custom_call_target="tpu_custom_call" | custom-call | tf_op jit(solution)/shard_map/attend/pallas_call | solution.py:81
  100.8 5.1 %attend.3 = (bf16[256,384]{1,0:T(8,128)(2,1)S(1)}, bf16[256,384]{1,0:T(8,128)(2,1)S(1)}, f32[512,384]{1,0:T(8,128)S(1)}, f32[512,384]{1,0:T(8,128)S(1)}) custom-call(s32[4,128]{1,0:T(4,128)S(1)} %get-tuple-element.38.lo_ref, s32[4,128]{1,0:T(4,128)S(1)} %get-tuple-element.36.hi_ref, bf16[768,1152]{1,0:T(8,128)(2,1)S(1)} %convolution_convert_fusion.1.proj_ref, ...), custom_call_target="tpu_custom_call" | custom-call | tf_op jit(solution)/shard_map/attend/pallas_call | solution.py:81
  106.0 1.0 convolution_convert_fusion.2
  107.0 0.7 fusion.76
  107.8 0.7 fusion.78
  108.5 0.7 fusion.80
  109.4 2.4 %collective-permute-start.6 = (bf16[256,768]{1,0:T(8,128)(2,1)S(1)}, bf16[256,768]{1,0:T(8,128)(2,1)S(1)}, u32[]{:S(2)}, u32[]{:S(2)}) collective-permute-start(bf16[256,768]{1,0:T(8,128)(2,1)S(1)} %pad_maximum_fusion.6), channel_id=1, source_target_pairs={{2,0},{3,1},{4,2},{5,3},{6,4},{7,5},{8,6},{9,7},{10,8},{11,9},{12,... | collective-permute-start | bytes 1179656 | tf_op jit(solution)/shard_map/ppermute | solution.py:192
  111.8 1.0 fusion.22
  112.8 1.0 fusion.23
  113.9 1.0 fusion.24
  114.9 0.1 add_convert_fusion.1
  115.0 0.0 copy-start.8
  115.0 0.0 copy-start.10
  115.1 6.3 %collective-permute-done.6 = bf16[256,768]{1,0:T(8,128)(2,1)S(1)} collective-permute-done((bf16[256,768]{1,0:T(8,128)(2,1)S(1)}, bf16[256,768]{1,0:T(8,128)(2,1)S(1)}, u32[]{:S(2)}, u32[]{:S(2)}) %collective-permute-start.6) | collective-permute-done | bytes 393248 | tf_op jit(solution)/shard_map/ppermute | solution.py:192
  121.4 0.1 fusion.34
  121.5 2.2 %convolution_convert_fusion = bf16[1536,1152]{1,0:T(8,128)(2,1)S(1)} fusion(bf16[256,1536]{1,0:T(8,128)(2,1)S(1)} %copy-done.10, bf16[256,1536]{1,0:T(8,128)(2,1)S(1)} %copy-done.8, bf16[256,768]{1,0:T(8,128)(2,1)S(1)} %fusion.34, bf16[256,384]{1,0:T(8,128)(2,1)S(1)} %get-tuple-element.19, bf16[256,384]{1,0:T(8,128)(2,1)S(1)} %get-tuple-element.30, ...), kind=kOutput, calls=%fused_computation.1 | convolution fusion | flops 1822752768 | bytes 6291456 | tf_op jit(solution)/shard_map/dot_general | solution.py:27
  123.8 2.4 %maximum_maximum_fusion = bf16[64,32,1152]{2,1,0:T(8,128)(2,1)} fusion(bf16[64,8,384]{2,1,0:T(8,128)(2,1)S(1)} %fusion.22, bf16[64,8,384]{2,1,0:T(8,128)(2,1)S(1)} %fusion.23, bf16[64,8,384]{2,1,0:T(8,128)(2,1)S(1)} %fusion.24, bf16[64,24,1152]{2,1,0:T(8,128)(2,1)S(1)} %bitcast.71), kind=kLoop, calls=%fused_computation.2 | loop fusion | flops 18874368 | bytes 9437184 | tf_op jit(solution)/shard_map/concatenate | solution.py:216
  126.2 9.5 %all-to-all-start.2 = ((bf16[64,32,1152]{2,1,0:T(8,128)(2,1)}), bf16[64,32,1152]{2,1,0:T(8,128)(2,1)}, u32[]{:S(2)}, u32[]{:S(2)}) async-start(bf16[64,32,1152]{2,1,0:T(8,128)(2,1)} %maximum_maximum_fusion), calls=%async_computation.2 | async-start | bytes 9437184 | tf_op jit(solution)/shard_map/all_to_all | solution.py:219
  135.7 1.0 fusion.45
  136.7 1.6 copy-done.2
  138.4 0.1 dynamic-slice_convert_fusion.1
  138.4 3.9 %collective-permute-start.5 = (bf16[256,1536]{1,0:T(8,128)(2,1)S(1)}, bf16[256,1536]{1,0:T(8,128)(2,1)}, u32[]{:S(2)}, u32[]{:S(2)}) collective-permute-start(bf16[256,1536]{1,0:T(8,128)(2,1)S(1)} %dynamic-slice_convert_fusion.1), channel_id=1, source_target_pairs={{0,1},{1,0},{2,3},{3,2},{4,5},{5,4},{6,7},{7,6},{8,9},{9,8},{10,11... | collective-permute-start | bytes 2359304 | tf_op jit(solution)/shard_map/ppermute | solution.py:119
  142.3 4.2 %fusion.116 = f32[512,1536]{1,0:T(8,128)S(1)} fusion(bf16[1536,1152]{1,0:T(8,128)(2,1)} %bitcast.5, bf16[256,768]{1,0:T(8,128)(2,1)S(1)} %copy-done.16, bf16[256,384]{1,0:T(8,128)(2,1)S(1)} %get-tuple-element.19, bf16[256,384]{1,0:T(8,128)(2,1)S(1)} %get-tuple-element.30, bf16[256,384]{1,0:T(8,128)(2,1)S(1)} %copy-done.18, ...), kind=kOutput, calls=%fused_computation.182 | convolution fusion | flops 1817837568 | bytes 7864320 | tf_op jit(solution)/shard_map/dot_general | solution.py:23
  146.5 1.7 copy-done.3
  148.2 0.1 dynamic-slice_convert_fusion
  148.3 0.9 collective-permute-start.7
  149.2 2.9 %fusion.31 = bf16[1,256,1536]{2,1,0:T(8,128)(2,1)} fusion(bf16[256,1536]{1,0:T(8,128)(2,1)} %collective-permute-done.5, f32[512,1536]{1,0:T(8,128)} %copy-done.2, s32[]{:T(128)S(6)} %select_n.152), kind=kLoop, calls=%fused_computation.60 | loop fusion | flops 1179648 | bytes 3145732 | tf_op jit(solution)/shard_map/broadcast_in_dim | solution.py:247
  152.1 0.5 fusion.46
  152.7 37.0 %all-to-all-done.2 = bf16[64,32,1152]{2,1,0:T(8,128)(2,1)} async-done(((bf16[64,32,1152]{2,1,0:T(8,128)(2,1)}), bf16[64,32,1152]{2,1,0:T(8,128)(2,1)}, u32[]{:S(2)}, u32[]{:S(2)}) %all-to-all-start.2) | async-done | bytes 4718624 | tf_op jit(solution)/shard_map/all_to_all | solution.py:219
  189.7 3.0 %convert_reduce_fusion = f32[32,1152]{1,0:T(8,128)S(1)} fusion(bf16[64,32,1152]{2,1,0:T(8,128)(2,1)} %all-to-all-done.2), kind=kLoop, calls=%fused_computation | loop fusion | flops 4681728 | bytes 4866048 | tf_op jit(solution)/shard_map/reduce_sum | solution.py:220
  192.7 15.0 %collective-permute-start.9 = (f32[6,1536]{1,0:T(8,128)S(1)}, f32[6,1536]{1,0:T(8,128)S(1)}, u32[]{:S(2)}, u32[]{:S(2)}) collective-permute-start(f32[6,1536]{1,0:T(8,128)S(1)} %pad_maximum_fusion.8), channel_id=1, source_target_pairs={{0,0},{1,64},{2,1},{3,65},{4,2},{5,66},{6,3},{7,67},{8,4},{9,68},{... | collective-permute-start | bytes 110600 | tf_op jit(solution)/shard_map/ppermute | solution.py:234
  207.7 0.1 collective-permute-start.8
  207.8 2.8 %fusion.32 = bf16[1,256,1536]{2,1,0:T(8,128)(2,1)} fusion(bf16[1,256,1536]{2,1,0:T(8,128)(2,1)S(1)} %copy-done.1, f32[256]{0:T(256)S(1)} %broadcast_multiply_fusion, f32[256]{0:T(256)S(1)} %broadcast_multiply_fusion.1, f32[256]{0:T(256)S(1)} %add_rsqrt_fusion, f32[256]{0:T(256)S(1)} %broadcast_multiply_fusion.2, ...), kind=kLoop, calls=%fused_computation.61 | loop fusion | flops 3932160 | bytes 3936260 | tf_op jit(solution)/shard_map/broadcast_in_dim | solution.py:247
  210.8 0.1 copy.12
  210.9 0.8 reshape.115
  211.6 0.6 copy.24
  (72 shorter events, 0.5 us)
Async XLA Ops:
  0.6 1.4 copy-start
  1.4 31.4 %collective-permute-start = (s32[256,2]{0,1:T(2,128)S(1)}, s32[256,2]{0,1:T(2,128)S(1)}, u32[]{:S(2)}, u32[]{:S(2)}) collective-permute-start(s32[256,2]{0,1:T(2,128)S(1)} %bitcast.74), channel_id=1, source_target_pairs={{0,1},{1,0},{2,3},{3,2},{4,5},{5,4},{6,7},{7,6},{8,9},{9,8},{10,11... | collective-permute-start | bytes 6152 | tf_op jit(solution)/shard_map/ppermute | solution.py:119
  2.1 7.1 %copy-start.1 = (bf16[1,256,1536]{2,1,0:T(8,128)(2,1)S(1)}, bf16[1,256,1536]{2,1,0:T(8,128)(2,1)}, u32[]{:S(2)}) copy-start(bf16[1,256,1536]{2,1,0:T(8,128)(2,1)} %param.5) | copy-start | bytes 2359300
  3.2 22.7 %all-to-all-start.1 = ((bf16[8,96,768]{2,1,0:T(8,128)(2,1)}), bf16[8,96,768]{2,1,0:T(8,128)(2,1)S(1)}, u32[]{:S(2)}, u32[]{:S(2)}) async-start(bf16[8,96,768]{2,1,0:T(8,128)(2,1)} %broadcast_in_dim.12), calls=%async_computation.1 | async-start | bytes 2359296 | tf_op jit(solution)/shard_map/all_to_all | solution.py:139
  10.9 23.7 %collective-permute-start.1 = (bf16[256,1536]{1,0:T(8,128)(2,1)}, bf16[256,1536]{1,0:T(8,128)(2,1)}, u32[]{:S(2)}, u32[]{:S(2)}) collective-permute-start(bf16[256,1536]{1,0:T(8,128)(2,1)} %fusion.10), channel_id=1, source_target_pairs={{0,1},{1,0},{2,3},{3,2},{4,5},{5,4},{6,7},{7,6},{8,9},{9,8},{10,11... | collective-permute-start | bytes 2359304 | tf_op jit(solution)/shard_map/ppermute | solution.py:119
  11.4 30.2 %collective-permute-start.3 = (bf16[256,1536]{1,0:T(8,128)(2,1)}, bf16[256,1536]{1,0:T(8,128)(2,1)}, u32[]{:S(2)}, u32[]{:S(2)}) collective-permute-start(bf16[256,1536]{1,0:T(8,128)(2,1)} %bitcast.6), channel_id=1, source_target_pairs={{0,1},{1,0},{2,3},{3,2},{4,5},{5,4},{6,7},{7,6},{8,9},{9,8},{10,11... | collective-permute-start | bytes 2359304 | tf_op jit(solution)/shard_map/ppermute | solution.py:119
  28.1 4.7 %copy-start.19 = (s32[2,1,256]{2,1,0:T(1,128)S(1)}, s32[2,1,256]{2,1,0:T(1,128)}, u32[]{:S(2)}) copy-start(s32[2,1,256]{2,1,0:T(1,128)} %param.7) | copy-start | bytes 6148
  28.1 61.9 %all-to-all-start = ((bf16[8,192,1152]{2,1,0:T(8,128)(2,1)}), bf16[8,192,1152]{2,1,0:T(8,128)(2,1)}, u32[]{:S(2)}, u32[]{:S(2)}) async-start(bf16[8,192,1152]{2,1,0:T(8,128)(2,1)} %broadcast_in_dim.11), calls=%async_computation | async-start | bytes 7077888 | tf_op jit(solution)/shard_map/all_to_all | solution.py:139
  33.1 10.0 %collective-permute-start.4 = (bf16[384,768]{1,0:T(8,128)(2,1)S(1)}, bf16[384,768]{1,0:T(8,128)(2,1)S(1)}, u32[]{:S(2)}, u32[]{:S(2)}) collective-permute-start(bf16[384,768]{1,0:T(8,128)(2,1)S(1)} %constant_dynamic-slice_fusion.1), channel_id=1, source_target_pairs={{0,1},{1,0},{2,3},{3,2},{4,5},{5,4},{6,7},{7,6},{8,9},{9,8},{10,11... | collective-permute-start | bytes 1769480 | tf_op jit(solution)/shard_map/ppermute | solution.py:119
  37.0 6.0 %copy-start.9 = (bf16[256,1536]{1,0:T(8,128)(2,1)}, bf16[256,1536]{1,0:T(8,128)(2,1)S(1)}, u32[]{:S(2)}) copy-start(bf16[256,1536]{1,0:T(8,128)(2,1)S(1)} %get-tuple-element.27) | copy-start | bytes 2359300
  37.0 52.9 %collective-permute-start.2 = (bf16[256,1536]{1,0:T(8,128)(2,1)S(1)}, bf16[256,1536]{1,0:T(8,128)(2,1)}, u32[]{:S(2)}, u32[]{:S(2)}) collective-permute-start(bf16[256,1536]{1,0:T(8,128)(2,1)S(1)} %get-tuple-element.27), channel_id=1, source_target_pairs={{0,2},{1,3},{2,4},{3,5},{4,6},{5,7},{6,8},{7,9},{8,10},{9,11},{10,... | collective-permute-start | bytes 2359304 | tf_op jit(solution)/shard_map/ppermute | solution.py:161
  43.1 1.3 copy-start.11
  43.1 1.3 copy-start.13
  43.4 1.0 copy-start.5
  43.4 46.6 %copy-start.7 = (bf16[256,1536]{1,0:T(8,128)(2,1)S(1)}, bf16[256,1536]{1,0:T(8,128)(2,1)}, u32[]{:S(2)}) copy-start(bf16[256,1536]{1,0:T(8,128)(2,1)} %get-tuple-element.26) | copy-start | bytes 2359300
  100.8 5.2 %copy-start.12 = (bf16[256,1536]{1,0:T(8,128)(2,1)S(1)}, bf16[256,1536]{1,0:T(8,128)(2,1)}, u32[]{:S(2)}) copy-start(bf16[256,1536]{1,0:T(8,128)(2,1)} %copy-done.11) | copy-start | bytes 2359300
  100.8 5.2 %copy-start.14 = (bf16[256,1536]{1,0:T(8,128)(2,1)S(1)}, bf16[256,1536]{1,0:T(8,128)(2,1)}, u32[]{:S(2)}) copy-start(bf16[256,1536]{1,0:T(8,128)(2,1)} %copy-done.13) | copy-start | bytes 2359300
  109.4 12.0 %collective-permute-start.6 = (bf16[256,768]{1,0:T(8,128)(2,1)S(1)}, bf16[256,768]{1,0:T(8,128)(2,1)S(1)}, u32[]{:S(2)}, u32[]{:S(2)}) collective-permute-start(bf16[256,768]{1,0:T(8,128)(2,1)S(1)} %pad_maximum_fusion.6), channel_id=1, source_target_pairs={{2,0},{3,1},{4,2},{5,3},{6,4},{7,5},{8,6},{9,7},{10,8},{11,9},{12,... | collective-permute-start | bytes 1179656 | tf_op jit(solution)/shard_map/ppermute | solution.py:192
  115.0 8.7 %copy-start.17 = (bf16[256,384]{1,0:T(8,128)(2,1)}, bf16[256,384]{1,0:T(8,128)(2,1)S(1)}, u32[]{:S(2)}) copy-start(bf16[256,384]{1,0:T(8,128)(2,1)S(1)} %get-tuple-element.43) | copy-start | bytes 589828
  115.0 6.4 %copy-start.8 = (bf16[256,1536]{1,0:T(8,128)(2,1)S(1)}, bf16[256,1536]{1,0:T(8,128)(2,1)}, u32[]{:S(2)}) copy-start(bf16[256,1536]{1,0:T(8,128)(2,1)} %get-tuple-element.26) | copy-start | bytes 2359300
  115.0 6.4 %copy-start.10 = (bf16[256,1536]{1,0:T(8,128)(2,1)S(1)}, bf16[256,1536]{1,0:T(8,128)(2,1)}, u32[]{:S(2)}) copy-start(bf16[256,1536]{1,0:T(8,128)(2,1)} %copy-done.9) | copy-start | bytes 2359300
  121.5 2.3 %copy-start.15 = (bf16[256,768]{1,0:T(8,128)(2,1)}, bf16[256,768]{1,0:T(8,128)(2,1)S(1)}, u32[]{:S(2)}) copy-start(bf16[256,768]{1,0:T(8,128)(2,1)S(1)} %fusion.34) | copy-start | bytes 1179652
  126.2 9.5 %copy-start.6 = (bf16[384,768]{1,0:T(8,128)(2,1)S(1)}, bf16[384,768]{1,0:T(8,128)(2,1)}, u32[]{:S(2)}) copy-start(bf16[384,768]{1,0:T(8,128)(2,1)} %copy-done.5) | copy-start | bytes 1769476
  126.2 63.5 %all-to-all-start.2 = ((bf16[64,32,1152]{2,1,0:T(8,128)(2,1)}), bf16[64,32,1152]{2,1,0:T(8,128)(2,1)}, u32[]{:S(2)}, u32[]{:S(2)}) async-start(bf16[64,32,1152]{2,1,0:T(8,128)(2,1)} %maximum_maximum_fusion), calls=%async_computation.2 | async-start | bytes 9437184 | tf_op jit(solution)/shard_map/all_to_all | solution.py:219
  136.7 1.6 copy-start.2
  138.3 4.0 %copy-start.16 = (bf16[256,768]{1,0:T(8,128)(2,1)S(1)}, bf16[256,768]{1,0:T(8,128)(2,1)}, u32[]{:S(2)}) copy-start(bf16[256,768]{1,0:T(8,128)(2,1)} %copy-done.15) | copy-start | bytes 1179652
  138.4 4.0 %copy-start.18 = (bf16[256,384]{1,0:T(8,128)(2,1)S(1)}, bf16[256,384]{1,0:T(8,128)(2,1)}, u32[]{:S(2)}) copy-start(bf16[256,384]{1,0:T(8,128)(2,1)} %copy-done.17) | copy-start | bytes 589828
  138.4 10.8 %collective-permute-start.5 = (bf16[256,1536]{1,0:T(8,128)(2,1)S(1)}, bf16[256,1536]{1,0:T(8,128)(2,1)}, u32[]{:S(2)}, u32[]{:S(2)}) collective-permute-start(bf16[256,1536]{1,0:T(8,128)(2,1)S(1)} %dynamic-slice_convert_fusion.1), channel_id=1, source_target_pairs={{0,1},{1,0},{2,3},{3,2},{4,5},{5,4},{6,7},{7,6},{8,9},{9,8},{10,11... | collective-permute-start | bytes 2359304 | tf_op jit(solution)/shard_map/ppermute | solution.py:119
  146.5 1.7 copy-start.3
  148.3 3.8 %collective-permute-start.7 = (bf16[256,1536]{1,0:T(8,128)(2,1)S(1)}, bf16[256,1536]{1,0:T(8,128)(2,1)S(1)}, u32[]{:S(2)}, u32[]{:S(2)}) collective-permute-start(bf16[256,1536]{1,0:T(8,128)(2,1)S(1)} %dynamic-slice_convert_fusion), channel_id=1, source_target_pairs={{0,1},{1,0},{2,3},{3,2},{4,5},{5,4},{6,7},{7,6},{8,9},{9,8},{10,11... | collective-permute-start | bytes 2359304 | tf_op jit(solution)/shard_map/ppermute | solution.py:119
  149.2 2.9 %copy-start.4 = (f32[512,1536]{1,0:T(8,128)S(1)}, f32[512,1536]{1,0:T(8,128)}, u32[]{:S(2)}) copy-start(f32[512,1536]{1,0:T(8,128)} %copy-done.3) | copy-start | bytes 9437188
  192.7 17.9 %collective-permute-start.9 = (f32[6,1536]{1,0:T(8,128)S(1)}, f32[6,1536]{1,0:T(8,128)S(1)}, u32[]{:S(2)}, u32[]{:S(2)}) collective-permute-start(f32[6,1536]{1,0:T(8,128)S(1)} %pad_maximum_fusion.8), channel_id=1, source_target_pairs={{0,0},{1,64},{2,1},{3,65},{4,2},{5,66},{6,3},{7,67},{8,4},{9,68},{... | collective-permute-start | bytes 110600 | tf_op jit(solution)/shard_map/ppermute | solution.py:234
  207.7 2.9 %collective-permute-start.8 = (f32[12,1152]{1,0:T(8,128)S(1)}, f32[12,1152]{1,0:T(8,128)S(1)}, u32[]{:S(2)}, u32[]{:S(2)}) collective-permute-start(f32[12,1152]{1,0:T(8,128)S(1)} %constant_dynamic-slice_fusion), channel_id=1, source_target_pairs={{0,1},{1,0},{2,3},{3,2},{4,5},{5,4},{6,7},{7,6},{8,9},{9,8},{10,11... | collective-permute-start | bytes 165896 | tf_op jit(solution)/shard_map/ppermute | solution.py:119

commit v2 on v1

v2 whole, which is shorter than its diff:
```python
import functools

import jax
import jax.numpy as jnp
from jax import lax
from jax.experimental import pallas as pl
from jax.experimental.pallas import tpu as pltpu
from jax.sharding import Mesh
from jax.sharding import PartitionSpec as P

HEAD_DIM = 64
STRETCH = 64
PRIOR = 4
WINDOW = (PRIOR + 1) * STRETCH
PAIR = 2 * HEAD_DIM
EPS = 1e-05

BF = jnp.bfloat16
F32 = jnp.float32


def nt(a, b):
    return lax.dot_general(a, b, (((1,), (1,)), ((), ())), preferred_element_type=F32)


def tn(a, b):
    return lax.dot_general(a, b, (((0,), (0,)), ((), ())), preferred_element_type=F32)


def nn(a, b):
    return lax.dot_general(a, b, (((1,), (0,)), ((), ())), preferred_element_type=F32)


def attend(first, lo_ref, hi_ref, proj_ref, dctx_ref, ctx_ref, dq_ref, dk_ref, dv_ref):
    width = ctx_ref.shape[1]
    blocks = ctx_ref.shape[0] // STRETCH
    dk_ref[...] = jnp.zeros_like(dk_ref)
    dv_ref[...] = jnp.zeros_like(dv_ref)
    lanes = lax.broadcasted_iota(jnp.int32, (STRETCH, PAIR), 1) < HEAD_DIM
    key_at = lax.broadcasted_iota(jnp.int32, (WINDOW, PAIR), 0)

    def stack(value):
        none = jnp.zeros_like(value)
        return jnp.concatenate(
            [jnp.where(lanes, value, none), jnp.where(lanes, none, value)], axis=0
        )

    def unstack(value):
        return jnp.where(lanes, value[:STRETCH], value[STRETCH:])

    for b in range(blocks):
        rows = pl.ds(b * STRETCH, STRETCH)
        seen = (key_at >= lo_ref[b : b + 1, :]) & (key_at < hi_ref[b : b + 1, :])
        for pair in range(width // PAIR):
            cols = pl.ds(pair * PAIR, PAIR)
            window = pl.ds(b * STRETCH, WINDOW)
            queries = stack(
                proj_ref[pl.ds(first + PRIOR * STRETCH + b * STRETCH, STRETCH), cols]
            )
            source = pl.ds(first + b * STRETCH, WINDOW)
            keys = proj_ref[source, pl.ds(width + pair * PAIR, PAIR)]
            values = proj_ref[source, pl.ds(2 * width + pair * PAIR, PAIR)]
            d_out = stack(dctx_ref[rows, cols])
            scores = jnp.where(seen, nt(keys, queries) * HEAD_DIM ** (-0.5), -1e30)
            weights = jnp.exp(scores - jnp.max(scores, axis=0, keepdims=True))
            probs = weights * (1.0 / jnp.sum(weights, axis=0, keepdims=True))
            low = probs.astype(BF)
            d_probs = nt(values, d_out)
            centre = jnp.sum(probs * d_probs, axis=0, keepdims=True)
            d_scores = (probs * (d_probs - centre) * HEAD_DIM ** (-0.5)).astype(BF)
            ctx_ref[rows, cols] = unstack(tn(low, values)).astype(BF)
            dq_ref[rows, cols] = unstack(tn(d_scores, keys)).astype(BF)
            dk_ref[window, cols] += nn(d_scores, queries)
            dv_ref[window, cols] += nn(low, d_out)


def attention(first, lo, hi, proj, d_context):
    queries, width = d_context.shape
    ext = queries + PRIOR * STRETCH
    whole = pl.BlockSpec(memory_space=pltpu.VMEM)
    return pl.pallas_call(
        functools.partial(attend, first),
        in_specs=[whole] * 4,
        out_specs=[whole] * 4,
        out_shape=[
            jax.ShapeDtypeStruct((queries, width), BF),
            jax.ShapeDtypeStruct((queries, width), BF),
            jax.ShapeDtypeStruct((ext, width), F32),
            jax.ShapeDtypeStruct((ext, width), F32),
        ],
        compiler_params=pltpu.CompilerParams(vmem_limit_bytes=40 * 1024 * 1024),
        name="attend",
    )(lo, hi, proj, d_context)


def normalize(inputs):
    widened = inputs.astype(F32)
    centered = widened - jnp.mean(widened, axis=-1, keepdims=True)
    inv_sigma = lax.rsqrt(jnp.mean(centered * centered, axis=-1, keepdims=True) + EPS)
    return (centered * inv_sigma, inv_sigma)


SIZES = {"z": 4, "xl": 2, "y": 4, "xh": 2, "c": 2}
ALL = tuple(SIZES)
DP, CHIPS, CORES, ROWS_Y = 8, 8, 2, 4


def device(dp, t, c):
    return (dp * CHIPS + t) * CORES + c


EVERY = [(d, t, c) for d in range(DP) for t in range(CHIPS) for c in range(CORES)]
SWAP = [(device(d, t, c), device(d, t, 1 - c)) for d, t, c in EVERY]
ONWARD = [(device(d, t, 1), device(d, t + 1, 1)) for d, t, c in EVERY if c and t + 1 < CHIPS]
BACK = [(device(d, t, c), device(d, t - 1, c)) for d, t, c in EVERY if t > 0]
OWNER = [(device(d, t, c), c * DP * CHIPS + d * CHIPS + t) for d, t, c in EVERY]


def from_y(by):
    return [(device(d, (t + 2 * by) % CHIPS, c), device(d, t, c)) for d, t, c in EVERY]


def swap(value):
    return lax.ppermute(value, ALL, SWAP)


def gradients(
    ctx_a, ctx_b, up_ref, low_ref, dq_a, dq_b, dk_a, dk_b, dv_a, dv_b, first_ref, late_ref, out_scr, d_ref
):
    step = pl.program_id(0)

    @pl.when(step == 0)
    def _():
        count, width = ctx_a.shape
        out_scr[...] = (
            tn(ctx_a[...], up_ref[:count, :]) + tn(ctx_b[...], up_ref[count:, :])
        ).astype(BF)
        halo = d_ref.shape[0] - 2 * count
        d_ref[:halo, :width] = jnp.zeros((halo, width), BF)
        d_ref[halo : halo + count, :width] = dq_a[...]
        d_ref[halo + count :, :width] = dq_b[...]
        for at, early, late in ((width, dk_a, dk_b), (2 * width, dv_a, dv_b)):
            cols = slice(at, at + width)
            d_ref[:halo, cols] = early[:halo, :].astype(BF)
            d_ref[halo : halo + count, cols] = (early[halo:, :] + late[:halo, :]).astype(BF)
            d_ref[halo + count :, cols] = late[halo:, :].astype(BF)

    own = 2 * CHIPS
    columns = d_ref.shape[1]
    third = columns // 3
    to = lax.broadcasted_iota(jnp.int32, (own * 8, own * 6), 0)
    at = lax.broadcasted_iota(jnp.int32, (own * 8, own * 6), 1)
    base, slot = to // 8 * 6, to % 8
    keep = ((slot < 6) & (at == base + slot)).astype(BF)
    rows = out_scr[pl.ds(pl.multiple_of(step * own * 6, 32), own * 6), :]
    parts = []
    for b in range(3):
        tail = (((slot == 6) & (at == base + b)) | ((slot == 7) & (at == base + 3 + b))).astype(BF)
        parts.append(
            nn(keep, rows[:, b * third : (b + 1) * third]) + nn(tail, rows[:, 3 * third :])
        )
    folded = jnp.concatenate(parts, axis=1)
    grad = tn(low_ref[...], d_ref[...])
    for j in range(own):
        dp, y, xh = j // CHIPS, j % CHIPS // 2, j % 2
        late_ref[dp, xh, y] = grad[j * 24 : j * 24 + 16].astype(BF)
        first_ref[y, dp, xh] = jnp.concatenate(
            [grad[j * 24 + 16 : j * 24 + 24], folded[j * 8 : j * 8 + 8]], axis=0
        ).astype(BF)


def weight_gradients(grad_all, low_ext, contexts, d_queries, d_keys, d_values):
    wide = grad_all.shape[1]
    width = contexts[0].shape[1]
    ext, columns = low_ext.shape[0], 3 * width
    steps = DP // 2
    parts = (*d_queries, *d_keys, *d_values)

    def whole(value):
        return pl.BlockSpec(value.shape, lambda i: (0, 0))

    return pl.pallas_call(
        gradients,
        grid=(steps,),
        in_specs=[
            whole(contexts[0]),
            whole(contexts[1]),
            whole(grad_all),
            pl.BlockSpec((ext, wide // steps), lambda i: (0, i)),
            *[whole(part) for part in parts],
        ],
        out_specs=[
            pl.BlockSpec((ROWS_Y, 2, 2, 16, columns), lambda i: (0, i, 0, 0, 0)),
            pl.BlockSpec((2, 2, ROWS_Y, 16, columns), lambda i: (i, 0, 0, 0, 0)),
        ],
        out_shape=[
            jax.ShapeDtypeStruct((ROWS_Y, DP, 2, 16, columns), BF),
            jax.ShapeDtypeStruct((DP, 2, ROWS_Y, 16, columns), BF),
        ],
        scratch_shapes=[pltpu.VMEM((width, wide), BF), pltpu.VMEM((ext, columns), BF)],
        compiler_params=pltpu.CompilerParams(vmem_limit_bytes=48 * 1024 * 1024),
        name="weight_gradients",
    )(*contexts, grad_all, low_ext, *parts)


def own_half(core, value, size, axis=0):
    return lax.dynamic_slice_in_dim(value, core * size, size, axis=axis)


def other_half(core, value, size, axis=0):
    return lax.dynamic_slice_in_dim(value, (1 - core) * size, size, axis=axis)


def in_order(lower, own, other, axis):
    return jnp.concatenate(
        [jnp.where(lower, own, other), jnp.where(lower, other, own)], axis=axis
    )


def scatter(chunks):
    return lax.all_to_all(chunks, ("z", "xl", "xh"), 0, 0, tiled=True)


def gather(shard):
    copies = jnp.broadcast_to(shard[None], (DP,) + shard.shape)
    return lax.all_to_all(copies, ("z", "xl"), 0, 0, tiled=True)


def body(frames, upstream, utt_span, w_qkv, w_out):
    core = lax.axis_index("c")
    lower = core == 0
    own_frames = frames[0]
    own_grad = upstream[0]
    count, wide = own_frames.shape
    inner = w_qkv.shape[1] // 3
    width = inner // CORES
    halo = PRIOR * STRETCH
    chips = DP * CHIPS
    out_cols = wide // CORES

    def both(own):
        return in_order(lower, own, swap(own), 0)

    y = lax.axis_index("y")
    mine = own_half(core, w_qkv.reshape(-1, 3, inner), width, axis=2).reshape(-1, 3 * width)
    out_mine = own_half(core, w_out, out_cols, axis=1)
    deep = mine.shape[0]
    direct = deep * 2 // 3
    low_rows = deep // 3
    tail = out_mine[low_rows:]
    folded = jnp.concatenate(
        [out_mine[:low_rows], jnp.concatenate([tail[:, :width], tail[:, width:]], axis=0)],
        axis=1,
    )
    indirect = jnp.concatenate(
        [
            mine[direct:].reshape(ROWS_Y, -1, 3 * width),
            folded.reshape(ROWS_Y, -1, 3 * width),
        ],
        axis=1,
    )
    quarter = gather(lax.dynamic_index_in_dim(indirect, y, axis=0, keepdims=False))
    shard, quarter = lax.optimization_barrier((mine[:direct], quarter))
    full_direct = gather(shard)
    quarters = jnp.zeros((ROWS_Y,) + quarter.shape, BF)
    for k in range(ROWS_Y):
        got = quarter if k == 0 else lax.ppermute(quarter, ALL, from_y(k))
        quarters = lax.dynamic_update_index_in_dim(quarters, got, (y + k) % ROWS_Y, 0)
    qkv_rows = (deep - direct) // ROWS_Y
    full_qkv = jnp.concatenate(
        [full_direct] + [quarters[i, :, :qkv_rows] for i in range(ROWS_Y)], axis=1
    ).reshape(wide, 3 * width)
    unfolded = jnp.concatenate([quarters[i, :, qkv_rows:] for i in range(ROWS_Y)], axis=1)
    rest = unfolded[:, :, out_cols:]
    half = rest.shape[1] // 2
    out_half = jnp.concatenate(
        [
            unfolded[:, :, :out_cols],
            jnp.concatenate([rest[:, :half], rest[:, half:]], axis=2),
        ],
        axis=1,
    ).reshape(inner, out_cols)
    full_out = in_order(
        lower,
        own_half(core, out_half, width),
        swap(other_half(core, out_half, width)),
        1,
    )

    normed, inv_sigma = normalize(own_frames)
    own_low = normed.astype(BF)
    low = both(own_low)
    past = lax.ppermute(own_low, ALL, ONWARD)
    low_ext = jnp.concatenate([jnp.where(lower, swap(past), past), low], axis=0)
    grad_all = both(own_grad)

    spans = jnp.swapaxes(utt_span[:, 0], 0, 1)
    spans = both(spans).T - (y * 2 + lax.axis_index("xh")) * (CORES * count) + halo
    blocked = spans.reshape(2, -1, STRETCH)
    blocked = blocked - (jnp.arange(blocked.shape[1], dtype=jnp.int32) * STRETCH)[None, :, None]
    blocked = jnp.concatenate([blocked, blocked], axis=-1)
    middle = blocked.shape[1] // 2

    d_context = nt(grad_all, full_out).astype(BF)
    projected = nn(low_ext, full_qkv).astype(BF)
    ctx_a, dq_a, dk_a, dv_a = attention(
        0, blocked[0, :middle], blocked[1, :middle], projected, d_context[:count]
    )
    d_history = jnp.concatenate([dk_a[:halo], dv_a[:halo]], axis=1).astype(BF)
    returned = lax.ppermute(d_history, ALL, BACK)
    ctx_b, dq_b, dk_b, dv_b = attention(
        count, blocked[0, middle:], blocked[1, middle:], projected, d_context[count:]
    )
    context = jnp.concatenate([ctx_a, ctx_b], axis=0)

    d_low = jnp.concatenate([dk_a[halo:] + dk_b[:halo], dv_a[halo:] + dv_b[:halo]], axis=1)
    d_low = jnp.concatenate([dq_a, d_low.astype(BF)], axis=1)
    d_last = jnp.concatenate([dk_b[halo:], dv_b[halo:]], axis=1)
    first, late = weight_gradients(
        grad_all, low_ext, (ctx_a, ctx_b), (dq_a, dq_b), (dk_a, dk_b), (dv_a, dv_b)
    )
    first, late, returned = lax.optimization_barrier((first, late, returned))
    summed = lax.dynamic_index_in_dim(first, y, axis=0, keepdims=False).astype(F32)
    for k in range(1, ROWS_Y):
        away = lax.dynamic_index_in_dim(first, (y + k) % ROWS_Y, axis=0, keepdims=False)
        summed = summed + lax.ppermute(away, ALL, from_y(-k)).astype(F32)
    summed = summed.astype(BF).reshape(chips // ROWS_Y, 16, 3 * width)
    arrived = scatter(late.reshape(chips // ROWS_Y, ROWS_Y * 16, 3 * width))
    summed, arrived = lax.optimization_barrier((summed, arrived))
    planes = jnp.sum(arrived.astype(F32), axis=0).reshape(ROWS_Y, 16, 3 * width)
    total_late = lax.dynamic_index_in_dim(planes, y, axis=0, keepdims=False)
    for k in range(1, ROWS_Y):
        away = lax.dynamic_index_in_dim(planes, (y + k) % ROWS_Y, axis=0, keepdims=False)
        total_late = total_late + lax.ppermute(away, ALL, from_y(-k))
    total_first = jnp.sum(scatter(summed).astype(F32), axis=0)
    total = jnp.concatenate([total_late, total_first], axis=0)
    d_proj = jnp.concatenate(
        [d_low, jnp.concatenate([dq_b, (d_last + returned.astype(F32)).astype(BF)], axis=1)], axis=0
    )

    o_total = total[CORES * (wide // chips // CORES) :]
    o_rows = inner // chips // CORES
    o_out = jnp.concatenate(
        [o_total[:o_rows], o_total[o_rows:].reshape(o_rows, wide - 3 * width)], axis=1
    )
    o_out = lax.ppermute(o_out, ALL, OWNER)

    rows = wide // chips // CORES
    total = total[: CORES * rows]
    q_kept = own_half(core, total, rows).reshape(rows, 3, width)
    q_other = swap(other_half(core, total, rows)).reshape(rows, 3, width)
    q_out = in_order(lower, q_kept, q_other, 2).reshape(rows, 3 * inner)

    partial = nn(context, full_out)
    branch = (
        own_half(core, partial, count)
        + swap(other_half(core, partial, count).astype(BF)).astype(F32)
    ).astype(BF)

    d_partial = nt(d_proj, full_qkv)
    d_normed = own_half(core, d_partial, count) + swap(
        other_half(core, d_partial, count).astype(BF)
    ).astype(F32)
    grad_in = inv_sigma * (
        d_normed
        - jnp.mean(d_normed, axis=-1, keepdims=True)
        - normed * jnp.mean(d_normed * normed, axis=-1, keepdims=True)
    )
    return (branch[None], grad_in.astype(BF)[None], q_out, o_out)


def solution(mesh):
    fine = Mesh(mesh.devices.reshape(tuple(SIZES.values())), ALL)
    dp, seq = ("z", "xl"), ("y", "xh", "c")
    rows = P(dp, seq, None)
    in_specs = (rows, rows, P(None, dp, seq), P(dp, None), P(dp, None))
    out_specs = (rows, rows, P(ALL, None), P(ALL, None))
    return jax.shard_map(body, mesh=fine, in_specs=in_specs, out_specs=out_specs, check_vma=False)
```

time: 213 us -> 177 us (0.83)
  waiting for transfers between devices: 98.2 us -> 46.2 us
  matrix products: 20.4 us -> 9.55 us
  Pallas kernels: 10.2 us -> 18.1 us
  starting transfers between devices: 49.6 us -> 57.4 us
  other arithmetic: 18.1 us -> 23.2 us
  local copies, waits for them, and re-layouts: 14.5 us -> 18.9 us
    all_to_all x3 -> x4, waiting for transfers between devices: 46.3 us -> 16 us  [the longest x2 10.8 us: gather(): return lax.all_to_all(copies, ('z', 'xl'), 0, 0, tiled=True)]
    ppermute x2 -> x11, waiting for transfers between devices: 51.8 us -> 28.9 us  [the longest x3 12.9 us: body(): summed = summed + lax.ppermute(away, ALL, from_y(-k)).astype(F32)]
    ppermute x2 -> x11, starting transfers between devices: 6.95 us -> 20 us  [the longest x1 5.38 us: body(): returned = lax.ppermute(d_history, ALL, BACK)]
    pallas_call x0 -> x1, Pallas kernels: none -> 7.89 us  [weight_gradients(): pl.pallas_call(gradients, grid=(steps,), in_specs=[whole(contexts[0]), wh...]
    dot_general x8 -> x2, matrix products: 11.9 us -> 4.18 us  [nn(): lax.dot_general(a, b, (((1,), (0,)), ((), ())), preferred_element_type=F32)]
    unnamed x44 -> x60, local copies, waits for them, and re-layouts: 4.81 us -> 10.2 us
    ppermute x1, starting transfers between devices: 15 us -> 11.2 us  [body(): o_out = lax.ppermute(o_out, ALL, OWNER)]
    convert_element_type x1 -> x2, other arithmetic: 0.07 us -> 3.59 us  [the longest x1 2.53 us: body(): summed = summed.astype(BF).reshape(chips // ROWS_Y, 16, 3 * width)]
  transfers between devices with their start and end apart: 13 -> 24, of which waited for: 4 -> 10; matrix products, arithmetic and copies ran while one was open for 14% -> 19% of each run, Pallas kernels for 0% -> 7%
where the time goes in v2:
time: 177 us; the launch traced here: 175 us
  starting transfers between devices  57.4 us (32%)
  waiting for transfers between devices  46.2 us (26%)
  other arithmetic  23.2 us (13%)
  local copies, waits for them, and re-layouts  18.9 us (11%)
  Pallas kernels  18.1 us (10%)
  matrix products  9.55 us (5%)
    ppermute x3, waiting for transfers between devices, body(): summed = summed + lax.ppermute(away, ALL, from_y(-k)).astype(F32)  12.9 us
    ppermute x3, waiting for transfers between devices, body(): got = quarter if k == 0 else lax.ppermute(quarter, ALL, from_y(k))  12.5 us
    ppermute x1, starting transfers between devices, body(): o_out = lax.ppermute(o_out, ALL, OWNER)  11.2 us
    all_to_all x2, waiting for transfers between devices, gather(): return lax.all_to_all(copies, ('z', 'xl'), 0, 0, tiled=True)  10.8 us
    all_to_all x2, starting transfers between devices, scatter(): return lax.all_to_all(chunks, ('z', 'xl', 'xh'), 0, 0, tiled=True)  10.6 us
    unnamed x60, local copies, waits for them, and re-layouts  10.2 us
    pallas_call x2, Pallas kernels, attention(): pl.pallas_call(functools.partial(attend, first), in_specs=[whole] * 4, ou...  10.2 us
    all_to_all x2, starting transfers between devices, gather(): return lax.all_to_all(copies, ('z', 'xl'), 0, 0, tiled=True)  9.43 us
  transfers between devices with their start and end apart: 24, of which 10 were waited for; matrix products, arithmetic and copies ran while one was open for 19% of the time, Pallas kernels for 7%

profile of v2, /device:TPU:9, one launch (start us, length us, event | category | flops | bytes accessed | tf_op | source)
XLA Modules:
  0.0 174.9 jit_solution(12751680086053718723)
XLA Ops:
  0.7 1.4 convert_reduce_fusion.1
  2.1 1.5 fusion.15
  3.6 2.3 %fusion.10 = bf16[256,1536]{1,0:T(8,128)(2,1)} fusion(bf16[1,256,1536]{2,1,0:T(8,128)(2,1)} %param.5, f32[256]{0:T(256)S(1)} %add_rsqrt_fusion, f32[256]{0:T(256)S(1)} %broadcast_multiply_fusion.2), kind=kLoop, calls=%fused_computation.17 | loop fusion | flops 1572864 | bytes 1574912 | tf_op jit(solution)/shard_map/convert_element_type | solution.py:291
  5.9 4.6 %collective-permute-start.1 = (bf16[256,1536]{1,0:T(8,128)(2,1)}, bf16[256,1536]{1,0:T(8,128)(2,1)}, u32[]{:S(2)}, u32[]{:S(2)}) collective-permute-start(bf16[256,1536]{1,0:T(8,128)(2,1)} %fusion.10), channel_id=1, source_target_pairs={{1,3},{3,5},{5,7},{7,9},{9,11},{11,13},{13,15},{17,19},{19,21},{21... | collective-permute-start | bytes 2359304 | tf_op jit(solution)/shard_map/ppermute | solution.py:293
  10.7 0.4 reshape.80
  11.4 0.9 broadcast_in_dim.42
  12.3 5.1 %all-to-all-start = ((bf16[8,32,1152]{2,1,0:T(8,128)(2,1)}), bf16[8,32,1152]{2,1,0:T(8,128)(2,1)S(1)}, u32[]{:S(2)}, u32[]{:S(2)}) async-start(bf16[8,32,1152]{2,1,0:T(8,128)(2,1)} %broadcast_in_dim.42), calls=%async_computation | async-start | bytes 1179648 | tf_op jit(solution)/shard_map/all_to_all | solution.py:226
  17.3 0.7 collective-permute-start.7
  18.7 1.3 collective-permute-done
  20.2 10.0 %all-to-all-done = bf16[8,32,1152]{2,1,0:T(8,128)(2,1)S(1)} async-done(((bf16[8,32,1152]{2,1,0:T(8,128)(2,1)}), bf16[8,32,1152]{2,1,0:T(8,128)(2,1)S(1)}, u32[]{:S(2)}, u32[]{:S(2)}) %all-to-all-start) | async-done | bytes 589856 | tf_op jit(solution)/shard_map/all_to_all | solution.py:226
  30.4 2.3 %collective-permute-start.5 = (bf16[8,32,1152]{2,1,0:T(8,128)(2,1)S(1)}, bf16[8,32,1152]{2,1,0:T(8,128)(2,1)S(1)}, u32[]{:S(2)}, u32[]{:S(2)}) collective-permute-start(bf16[8,32,1152]{2,1,0:T(8,128)(2,1)S(1)} %all-to-all-done), channel_id=1, source_target_pairs={{8,0},{9,1},{10,2},{11,3},{12,4},{13,5},{14,6},{15,7},{0,8},{1,9},... | collective-permute-start | bytes 1769480 | tf_op jit(solution)/shard_map/ppermute | solution.py:267
  32.9 1.7 broadcast_in_dim.43
  34.6 4.4 %all-to-all-start.1 = ((bf16[8,128,1152]{2,1,0:T(8,128)(2,1)}), bf16[8,128,1152]{2,1,0:T(8,128)(2,1)}, u32[]{:S(2)}, u32[]{:S(2)}) async-start(bf16[8,128,1152]{2,1,0:T(8,128)(2,1)} %broadcast_in_dim.43), calls=%async_computation.1 | async-start | bytes 4718592 | tf_op jit(solution)/shard_map/all_to_all | solution.py:226
  39.3 1.7 collective-permute-start.6
  41.0 1.2 broadcast_select_fusion.1
  42.4 1.1 collective-permute-start.2
  43.5 1.6 broadcast_select_fusion.3
  45.1 1.6 bitcast_dynamic-update-slice_fusion.2
  46.7 12.1 %collective-permute-done.5 = bf16[8,32,1152]{2,1,0:T(8,128)(2,1)S(1)} collective-permute-done((bf16[8,32,1152]{2,1,0:T(8,128)(2,1)S(1)}, bf16[8,32,1152]{2,1,0:T(8,128)(2,1)S(1)}, u32[]{:S(2)}, u32[]{:S(2)}) %collective-permute-start.5) | collective-permute-done | bytes 589856 | tf_op jit(solution)/shard_map/ppermute | solution.py:267
  58.8 0.4 collective-permute-done.6
  59.6 1.1 copy-done.3
  60.8 1.4 collective-permute-start.8
  62.2 1.2 broadcast_select_fusion.4
  63.5 1.6 pad_maximum_fusion.low_ref
  65.4 0.9 copy-done.12
  66.3 1.0 convolution_convert_fusion.1
  67.3 0.9 all-to-all-done.1
  68.2 2.0 %constant_dynamic-update-slice_fusion = bf16[8,192,1152]{2,1,0:T(8,128)(2,1)S(1)} fusion(bf16[8,128,1152]{2,1,0:T(8,128)(2,1)} %all-to-all-done.1), kind=kLoop, calls=%fused_computation.113 | loop fusion | bytes 4718592
  70.2 0.3 copy-done.4
  70.8 1.0 copy-done.7
  71.7 0.8 copy-done.9
  72.6 0.8 copy-done.11
  73.4 3.2 %convolution_convert_fusion.proj_ref = bf16[768,1152]{1,0:T(8,128)(2,1)S(1)} fusion(bf16[1536,1152]{1,0:T(8,128)(2,1)S(1)} %bitcast.124, bf16[256,1536]{1,0:T(8,128)(2,1)S(1)} %copy-done.11, bf16[256,1536]{1,0:T(8,128)(2,1)S(1)} %copy-done.9, bf16[256,1536]{1,0:T(8,128)(2,1)S(1)} %copy-done.7), kind=kOutput, calls=%fused_computation.1 | convolution fusion | flops 2725871616 | bytes 7667712 | tf_op jit(solution)/shard_map/dot_general | solution.py:31
  76.6 5.1 %attend.2 = (bf16[256,384]{1,0:T(8,128)(2,1)S(1)}, bf16[256,384]{1,0:T(8,128)(2,1)S(1)}, f32[512,384]{1,0:T(8,128)S(1)}, f32[512,384]{1,0:T(8,128)S(1)}) custom-call(s32[4,128]{1,0:T(4,128)S(1)} %get-tuple-element.69.lo_ref, s32[4,128]{1,0:T(4,128)S(1)} %get-tuple-element.66.hi_ref, bf16[768,1152]{1,0:T(8,128)(2,1)S(1)} %convolution_convert_fusion.proj_ref, ...), custom_call_target="tpu_custom_call" | custom-call | tf_op jit(solution)/shard_map/attend/pallas_call | solution.py:81
  81.8 5.4 %collective-permute-start.10 = (bf16[256,768]{1,0:T(8,128)(2,1)S(1)}, bf16[256,768]{1,0:T(8,128)(2,1)S(1)}, u32[]{:S(2)}, u32[]{:S(2)}) collective-permute-start(bf16[256,768]{1,0:T(8,128)(2,1)S(1)} %pad_maximum_fusion.9), channel_id=1, source_target_pairs={{2,0},{3,1},{4,2},{5,3},{6,4},{7,5},{8,6},{9,7},{10,8},{11,9},{12,... | collective-permute-start | bytes 1179656 | tf_op jit(solution)/shard_map/ppermute | solution.py:310
  87.2 5.1 %attend.3 = (bf16[256,384]{1,0:T(8,128)(2,1)S(1)}, bf16[256,384]{1,0:T(8,128)(2,1)S(1)}, f32[512,384]{1,0:T(8,128)S(1)}, f32[512,384]{1,0:T(8,128)S(1)}) custom-call(s32[4,128]{1,0:T(4,128)S(1)} %get-tuple-element.68.lo_ref, s32[4,128]{1,0:T(4,128)S(1)} %get-tuple-element.67.hi_ref, bf16[768,1152]{1,0:T(8,128)(2,1)S(1)} %convolution_convert_fusion.proj_ref, ...), custom_call_target="tpu_custom_call" | custom-call | tf_op jit(solution)/shard_map/attend/pallas_call | solution.py:81
  92.4 1.0 fusion.35
  93.4 1.1 dynamic-slice_convert_fusion.1
  94.4 1.9 %collective-permute-start.9 = (bf16[256,1536]{1,0:T(8,128)(2,1)}, bf16[256,1536]{1,0:T(8,128)(2,1)}, u32[]{:S(2)}, u32[]{:S(2)}) collective-permute-start(bf16[256,1536]{1,0:T(8,128)(2,1)} %dynamic-slice_convert_fusion.1), channel_id=1, source_target_pairs={{0,1},{1,0},{2,3},{3,2},{4,5},{5,4},{6,7},{7,6},{8,9},{9,8},{10,11... | collective-permute-start | bytes 2359304 | tf_op jit(solution)/shard_map/ppermute | solution.py:124
  96.3 7.9 %weight_gradients.1 = (bf16[4,8,2,16,1152]{4,3,2,1,0:T(8,128)(2,1)}, bf16[8,2,4,16,1152]{4,3,2,1,0:T(8,128)(2,1)}) custom-call(bf16[256,384]{1,0:T(8,128)(2,1)S(1)} %get-tuple-element.23.ctx_a, bf16[256,384]{1,0:T(8,128)(2,1)S(1)} %get-tuple-element.24.ctx_b, bf16[512,1536]{1,0:T(8,128)(2,1)S(1)} %pad_maximum_fusion.1.up_ref, ...), custom_call_target="tpu_custom_call" | custom-call | tf_op jit(solution)/shard_map/weight_gradients/pallas_call | solution.py:182
  104.3 1.6 copy-done.14
  106.0 1.2 dynamic-slice_bitcast_fusion.2
  107.2 0.4 collective-permute-start.12
  107.6 1.8 %collective-permute-start.14 = (bf16[8,2,16,1152]{3,2,1,0:T(8,128)(2,1)S(1)}, bf16[8,2,16,1152]{3,2,1,0:T(8,128)(2,1)}, u32[]{:S(2)}, u32[]{:S(2)}) collective-permute-start(bf16[8,2,16,1152]{3,2,1,0:T(8,128)(2,1)S(1)} %get-tuple-element.41), channel_id=1, source_target_pairs={{4,0},{5,1},{6,2},{7,3},{8,4},{9,5},{10,6},{11,7},{12,8},{13,9},{1... | collective-permute-start | bytes 1769480 | tf_op jit(solution)/shard_map/ppermute | solution.py:326
  109.4 4.4 %all-to-all-start.2 = ((bf16[16,64,1152]{2,1,0:T(8,128)(2,1)}), bf16[16,64,1152]{2,1,0:T(8,128)(2,1)}, u32[]{:S(2)}, u32[]{:S(2)}) async-start(bf16[16,64,1152]{2,1,0:T(8,128)(2,1)} %bitcast.123), calls=%async_computation.2 | async-start | bytes 4718592 | tf_op jit(solution)/shard_map/all_to_all | solution.py:221
  113.8 1.1 fusion.34
  114.9 4.4 %fusion.19 = f32[512,1536]{1,0:T(8,128)S(1)} fusion(bf16[1536,1152]{1,0:T(8,128)(2,1)} %bitcast.125, bf16[256,768]{1,0:T(8,128)(2,1)S(1)} %fusion.34, bf16[256,384]{1,0:T(8,128)(2,1)S(1)} %get-tuple-element.30.dq_b, bf16[256,384]{1,0:T(8,128)(2,1)S(1)} %get-tuple-element.55, bf16[256,384]{1,0:T(8,128)(2,1)S(1)} %get-tuple-element.73, ...), kind=kOutput, calls=%fused_computation.37 | convolution fusion | flops 1817837568 | bytes 7864320 | tf_op jit(solution)/shard_map/dot_general | solution.py:23
  119.4 0.9 collective-permute-start.11
  120.3 2.3 %fusion.32 = bf16[1,256,1536]{2,1,0:T(8,128)(2,1)} fusion(bf16[256,1536]{1,0:T(8,128)(2,1)} %collective-permute-done.9, f32[512,1536]{1,0:T(8,128)S(1)} %copy-done.2, s32[]{:T(128)S(6)} %select_n.172), kind=kLoop, calls=%fused_computation.52 | loop fusion | flops 1179648 | bytes 3145732 | tf_op jit(solution)/shard_map/broadcast_in_dim | solution.py:369
  122.6 1.2 collective-permute-done.13
  123.8 11.7 %collective-permute-done.14 = bf16[8,2,16,1152]{3,2,1,0:T(8,128)(2,1)} collective-permute-done((bf16[8,2,16,1152]{3,2,1,0:T(8,128)(2,1)S(1)}, bf16[8,2,16,1152]{3,2,1,0:T(8,128)(2,1)}, u32[]{:S(2)}, u32[]{:S(2)}) %collective-permute-start.14) | collective-permute-done | bytes 589856 | tf_op jit(solution)/shard_map/ppermute | solution.py:326
  135.5 2.5 %fusion.31 = bf16[8,2,16,1152]{3,2,1,0:T(8,128)(2,1)} fusion(bf16[8,2,16,1152]{3,2,1,0:T(8,128)(2,1)} %collective-permute-done.14, bf16[8,2,16,1152]{3,2,1,0:T(8,128)(2,1)} %collective-permute-done.13, bf16[8,2,16,1152]{3,2,1,0:T(8,128)(2,1)S(1)} %collective-permute-done.12, bf16[4,8,2,16,1152]{4,3,2,1,0:T(8,128)(2,1)} %get-tuple-element.34, s32[]{:T(128)S(6)} %select_n.157), kind=kLoop, calls=%fused_computation.50 | loop fusion | flops 2359296 | bytes 2949124 | tf_op jit(solution)/shard_map/convert_element_type | solution.py:327
  138.0 0.5 fusion.36
  138.5 5.2 %all-to-all-done.2 = bf16[16,64,1152]{2,1,0:T(8,128)(2,1)} async-done(((bf16[16,64,1152]{2,1,0:T(8,128)(2,1)}), bf16[16,64,1152]{2,1,0:T(8,128)(2,1)}, u32[]{:S(2)}, u32[]{:S(2)}) %all-to-all-start.2) | async-done | bytes 2359328 | tf_op jit(solution)/shard_map/all_to_all | solution.py:221
  143.7 6.1 %all-to-all-start.3 = ((bf16[16,16,1152]{2,1,0:T(8,128)(2,1)}), bf16[16,16,1152]{2,1,0:T(8,128)(2,1)S(1)}, u32[]{:S(2)}, u32[]{:S(2)}) async-start(bf16[16,16,1152]{2,1,0:T(8,128)(2,1)} %bitcast.31), calls=%async_computation.3 | async-start | bytes 1179648 | tf_op jit(solution)/shard_map/all_to_all | solution.py:221
  149.8 2.0 %convert_reduce_fusion = f32[64,1152]{1,0:T(8,128)S(1)} fusion(bf16[16,64,1152]{2,1,0:T(8,128)(2,1)} %all-to-all-done.2), kind=kLoop, calls=%fused_computation | loop fusion | flops 2285568 | bytes 2654208 | tf_op jit(solution)/shard_map/reduce_sum | solution.py:330
  151.9 0.5 collective-permute-start.15
  152.4 3.1 %collective-permute-start.16 = (f32[16,1152]{1,0:T(8,128)S(1)}, f32[16,1152]{1,0:T(8,128)S(1)}, u32[]{:S(2)}, u32[]{:S(2)}) collective-permute-start(f32[16,1152]{1,0:T(8,128)S(1)} %get-tuple-element.61), channel_id=1, source_target_pairs={{8,0},{9,1},{10,2},{11,3},{12,4},{13,5},{14,6},{15,7},{0,8},{1,9},... | collective-permute-start | bytes 221192 | tf_op jit(solution)/shard_map/ppermute | solution.py:334
  155.5 2.0 %collective-permute-done.16 = f32[16,1152]{1,0:T(8,128)S(1)} collective-permute-done((f32[16,1152]{1,0:T(8,128)S(1)}, f32[16,1152]{1,0:T(8,128)S(1)}, u32[]{:S(2)}, u32[]{:S(2)}) %collective-permute-start.16) | collective-permute-done | bytes 73760 | tf_op jit(solution)/shard_map/ppermute | solution.py:334
  157.5 1.5 collective-permute-done.17
  159.2 11.2 %collective-permute-start.19 = (f32[6,1536]{1,0:T(8,128)S(1)}, f32[6,1536]{1,0:T(8,128)S(1)}, u32[]{:S(2)}, u32[]{:S(2)}) collective-permute-start(f32[6,1536]{1,0:T(8,128)S(1)} %pad_maximum_fusion.11), channel_id=1, source_target_pairs={{0,0},{1,64},{2,1},{3,65},{4,2},{5,66},{6,3},{7,67},{8,4},{9,68},{... | collective-permute-start | bytes 110600 | tf_op jit(solution)/shard_map/ppermute | solution.py:346
  170.5 2.8 %fusion.33 = bf16[1,256,1536]{2,1,0:T(8,128)(2,1)} fusion(bf16[1,256,1536]{2,1,0:T(8,128)(2,1)S(1)} %copy-done, f32[256]{0:T(256)S(1)} %broadcast_multiply_fusion, f32[256]{0:T(256)S(1)} %broadcast_multiply_fusion.1, f32[256]{0:T(256)S(1)} %copy-done.24, f32[256]{0:T(256)S(1)} %copy-done.21, bf16[256,1536]{1,0:T(8,128)(2,1)S(1)} %collective-permute-done.11, ...), kind=kLoop, calls=%fused_computation.53 | loop fusion | flops 3932160 | bytes 3936260 | tf_op jit(solution)/shard_map/broadcast_in_dim | solution.py:369
  173.6 0.7 copy.12
  174.2 0.6 copy.28
  (117 shorter events, 3.7 us)
Async XLA Ops:
  0.6 10.0 %copy-start.18 = (bf16[96,1536]{1,0:T(8,128)(2,1)S(1)}, bf16[96,1536]{1,0:T(8,128)(2,1)}, u32[]{:S(2)}) copy-start(bf16[96,1536]{1,0:T(8,128)(2,1)} %param.9) | copy-start | bytes 884740
  0.6 10.0 %copy-start.16 = (bf16[192,2304]{1,0:T(8,128)(2,1)S(1)}, bf16[192,2304]{1,0:T(8,128)(2,1)}, u32[]{:S(2)}) copy-start(bf16[192,2304]{1,0:T(8,128)(2,1)} %param.8) | copy-start | bytes 2654212
  2.1 1.5 copy-start.19
  3.6 2.3 %copy-start.22 = (f32[256]{0:T(256)}, f32[256]{0:T(256)S(1)}, u32[]{:S(2)}) copy-start(f32[256]{0:T(256)S(1)} %add_rsqrt_fusion) | copy-start | bytes 3076
  5.9 36.5 %collective-permute-start.1 = (bf16[256,1536]{1,0:T(8,128)(2,1)}, bf16[256,1536]{1,0:T(8,128)(2,1)}, u32[]{:S(2)}, u32[]{:S(2)}) collective-permute-start(bf16[256,1536]{1,0:T(8,128)(2,1)} %fusion.10), channel_id=1, source_target_pairs={{1,3},{3,5},{5,7},{7,9},{9,11},{11,13},{13,15},{17,19},{19,21},{21... | collective-permute-start | bytes 2359304 | tf_op jit(solution)/shard_map/ppermute | solution.py:293
  10.6 32.9 %collective-permute-start.3 = (bf16[256,1536]{1,0:T(8,128)(2,1)}, bf16[256,1536]{1,0:T(8,128)(2,1)}, u32[]{:S(2)}, u32[]{:S(2)}) collective-permute-start(bf16[256,1536]{1,0:T(8,128)(2,1)} %fusion.10), channel_id=1, source_target_pairs={{0,1},{1,0},{2,3},{3,2},{4,5},{5,4},{6,7},{7,6},{8,9},{9,8},{10,11... | collective-permute-start | bytes 2359304 | tf_op jit(solution)/shard_map/ppermute | solution.py:124
  10.7 7.4 %copy-start.25 = (s32[2,1,256]{2,1,0:T(1,128)S(1)}, s32[2,1,256]{2,1,0:T(1,128)}, u32[]{:S(2)}) copy-start(s32[2,1,256]{2,1,0:T(1,128)} %param.7) | copy-start | bytes 6148
  12.3 17.9 %all-to-all-start = ((bf16[8,32,1152]{2,1,0:T(8,128)(2,1)}), bf16[8,32,1152]{2,1,0:T(8,128)(2,1)S(1)}, u32[]{:S(2)}, u32[]{:S(2)}) async-start(bf16[8,32,1152]{2,1,0:T(8,128)(2,1)} %broadcast_in_dim.42), calls=%async_computation | async-start | bytes 1179648 | tf_op jit(solution)/shard_map/all_to_all | solution.py:226
  17.3 22.0 %collective-permute-start.7 = (bf16[256,1536]{1,0:T(8,128)(2,1)}, bf16[256,1536]{1,0:T(8,128)(2,1)S(1)}, u32[]{:S(2)}, u32[]{:S(2)}) collective-permute-start(bf16[256,1536]{1,0:T(8,128)(2,1)} %bitcast.17), channel_id=1, source_target_pairs={{0,1},{1,0},{2,3},{3,2},{4,5},{5,4},{6,7},{7,6},{8,9},{9,8},{10,11... | collective-permute-start | bytes 2359304 | tf_op jit(solution)/shard_map/ppermute | solution.py:124
  18.1 1.9 %collective-permute-start = (s32[256,2]{0,1:T(2,128)S(1)}, s32[256,2]{0,1:T(2,128)S(1)}, u32[]{:S(2)}, u32[]{:S(2)}) collective-permute-start(s32[256,2]{0,1:T(2,128)S(1)} %bitcast.132), channel_id=1, source_target_pairs={{0,1},{1,0},{2,3},{3,2},{4,5},{5,4},{6,7},{7,6},{8,9},{9,8},{10,11... | collective-permute-start | bytes 6152 | tf_op jit(solution)/shard_map/ppermute | solution.py:124
  30.2 14.9 %collective-permute-start.4 = (bf16[8,32,1152]{2,1,0:T(8,128)(2,1)S(1)}, bf16[8,32,1152]{2,1,0:T(8,128)(2,1)}, u32[]{:S(2)}, u32[]{:S(2)}) collective-permute-start(bf16[8,32,1152]{2,1,0:T(8,128)(2,1)S(1)} %all-to-all-done), channel_id=1, source_target_pairs={{4,0},{5,1},{6,2},{7,3},{8,4},{9,5},{10,6},{11,7},{12,8},{13,9},{1... | collective-permute-start | bytes 1769480 | tf_op jit(solution)/shard_map/ppermute | solution.py:267
  30.4 28.4 %collective-permute-start.5 = (bf16[8,32,1152]{2,1,0:T(8,128)(2,1)S(1)}, bf16[8,32,1152]{2,1,0:T(8,128)(2,1)S(1)}, u32[]{:S(2)}, u32[]{:S(2)}) collective-permute-start(bf16[8,32,1152]{2,1,0:T(8,128)(2,1)S(1)} %all-to-all-done), channel_id=1, source_target_pairs={{8,0},{9,1},{10,2},{11,3},{12,4},{13,5},{14,6},{15,7},{0,8},{1,9},... | collective-permute-start | bytes 1769480 | tf_op jit(solution)/shard_map/ppermute | solution.py:267
  34.6 33.5 %all-to-all-start.1 = ((bf16[8,128,1152]{2,1,0:T(8,128)(2,1)}), bf16[8,128,1152]{2,1,0:T(8,128)(2,1)}, u32[]{:S(2)}, u32[]{:S(2)}) async-start(bf16[8,128,1152]{2,1,0:T(8,128)(2,1)} %broadcast_in_dim.43), calls=%async_computation.1 | async-start | bytes 4718592 | tf_op jit(solution)/shard_map/all_to_all | solution.py:226
  39.3 20.0 %collective-permute-start.6 = (bf16[8,32,1152]{2,1,0:T(8,128)(2,1)S(1)}, bf16[8,32,1152]{2,1,0:T(8,128)(2,1)S(1)}, u32[]{:S(2)}, u32[]{:S(2)}) collective-permute-start(bf16[8,32,1152]{2,1,0:T(8,128)(2,1)S(1)} %all-to-all-done), channel_id=1, source_target_pairs={{12,0},{13,1},{14,2},{15,3},{0,4},{1,5},{2,6},{3,7},{4,8},{5,9},{6... | collective-permute-start | bytes 1769480 | tf_op jit(solution)/shard_map/ppermute | solution.py:267
  42.2 1.2 copy-start
  42.2 1.2 copy-start.20
  42.3 1.2 copy-start.23
  42.4 19.8 %collective-permute-start.2 = (bf16[256,1536]{1,0:T(8,128)(2,1)}, bf16[256,1536]{1,0:T(8,128)(2,1)S(1)}, u32[]{:S(2)}, u32[]{:S(2)}) collective-permute-start(bf16[256,1536]{1,0:T(8,128)(2,1)} %collective-permute-done.1), channel_id=1, source_target_pairs={{0,1},{1,0},{2,3},{3,2},{4,5},{5,4},{6,7},{7,6},{8,9},{9,8},{10,11... | collective-permute-start | bytes 2359304 | tf_op jit(solution)/shard_map/ppermute | solution.py:124
  45.1 18.4 %copy-start.8 = (bf16[256,1536]{1,0:T(8,128)(2,1)}, bf16[256,1536]{1,0:T(8,128)(2,1)S(1)}, u32[]{:S(2)}) copy-start(bf16[256,1536]{1,0:T(8,128)(2,1)S(1)} %get-tuple-element.51) | copy-start | bytes 2359300
  45.1 18.4 %copy-start.10 = (bf16[256,1536]{1,0:T(8,128)(2,1)}, bf16[256,1536]{1,0:T(8,128)(2,1)S(1)}, u32[]{:S(2)}) copy-start(bf16[256,1536]{1,0:T(8,128)(2,1)S(1)} %get-tuple-element.52) | copy-start | bytes 2359300
  59.3 1.4 copy-start.3
  60.8 4.4 %collective-permute-start.8 = (bf16[384,768]{1,0:T(8,128)(2,1)S(1)}, bf16[384,768]{1,0:T(8,128)(2,1)S(1)}, u32[]{:S(2)}, u32[]{:S(2)}) collective-permute-start(bf16[384,768]{1,0:T(8,128)(2,1)S(1)} %constant_dynamic-slice_fusion.2), channel_id=1, source_target_pairs={{0,1},{1,0},{2,3},{3,2},{4,5},{5,4},{6,7},{7,6},{8,9},{9,8},{10,11... | collective-permute-start | bytes 1769480 | tf_op jit(solution)/shard_map/ppermute | solution.py:124
  63.5 1.7 copy-start.6
  65.4 0.9 copy-start.12
  68.2 2.4 %copy-start.4 = (bf16[4,8,32,1152]{3,2,1,0:T(8,128)(2,1)S(1)}, bf16[4,8,32,1152]{3,2,1,0:T(8,128)(2,1)}, u32[]{:S(2)}) copy-start(bf16[4,8,32,1152]{3,2,1,0:T(8,128)(2,1)} %copy-done.3) | copy-start | bytes 7077892
  70.6 1.2 copy-start.7
  70.6 2.0 %copy-start.9 = (bf16[256,1536]{1,0:T(8,128)(2,1)S(1)}, bf16[256,1536]{1,0:T(8,128)(2,1)}, u32[]{:S(2)}) copy-start(bf16[256,1536]{1,0:T(8,128)(2,1)} %copy-done.8) | copy-start | bytes 2359300
  70.6 2.8 %copy-start.11 = (bf16[256,1536]{1,0:T(8,128)(2,1)S(1)}, bf16[256,1536]{1,0:T(8,128)(2,1)}, u32[]{:S(2)}) copy-start(bf16[256,1536]{1,0:T(8,128)(2,1)} %copy-done.10) | copy-start | bytes 2359300
  70.8 5.8 %copy-start.15 = (bf16[8,192,1152]{2,1,0:T(8,128)(2,1)}, bf16[8,192,1152]{2,1,0:T(8,128)(2,1)S(1)}, u32[]{:S(2)}) copy-start(bf16[8,192,1152]{2,1,0:T(8,128)(2,1)S(1)} %fusion.40) | copy-start | bytes 10616836
  76.6 15.7 %copy-start.13 = (bf16[384,768]{1,0:T(8,128)(2,1)S(1)}, bf16[384,768]{1,0:T(8,128)(2,1)}, u32[]{:S(2)}) copy-start(bf16[384,768]{1,0:T(8,128)(2,1)} %copy-done.12) | copy-start | bytes 1769476
  81.8 22.5 %collective-permute-start.10 = (bf16[256,768]{1,0:T(8,128)(2,1)S(1)}, bf16[256,768]{1,0:T(8,128)(2,1)S(1)}, u32[]{:S(2)}, u32[]{:S(2)}) collective-permute-start(bf16[256,768]{1,0:T(8,128)(2,1)S(1)} %pad_maximum_fusion.9), channel_id=1, source_target_pairs={{2,0},{3,1},{4,2},{5,3},{6,4},{7,5},{8,6},{9,7},{10,8},{11,9},{12,... | collective-permute-start | bytes 1179656 | tf_op jit(solution)/shard_map/ppermute | solution.py:310
  93.3 10.8 %copy-start.1 = (f32[512,1536]{1,0:T(8,128)}, f32[512,1536]{1,0:T(8,128)S(1)}, u32[]{:S(2)}) copy-start(f32[512,1536]{1,0:T(8,128)S(1)} %fusion.35) | copy-start | bytes 9437188
  94.4 25.9 %collective-permute-start.9 = (bf16[256,1536]{1,0:T(8,128)(2,1)}, bf16[256,1536]{1,0:T(8,128)(2,1)}, u32[]{:S(2)}, u32[]{:S(2)}) collective-permute-start(bf16[256,1536]{1,0:T(8,128)(2,1)} %dynamic-slice_convert_fusion.1), channel_id=1, source_target_pairs={{0,1},{1,0},{2,3},{3,2},{4,5},{5,4},{6,7},{7,6},{8,9},{9,8},{10,11... | collective-permute-start | bytes 2359304 | tf_op jit(solution)/shard_map/ppermute | solution.py:124
  104.2 1.8 %copy-start.14 = (bf16[4,8,2,16,1152]{4,3,2,1,0:T(8,128)(2,1)S(1)}, bf16[4,8,2,16,1152]{4,3,2,1,0:T(8,128)(2,1)}, u32[]{:S(2)}) copy-start(bf16[4,8,2,16,1152]{4,3,2,1,0:T(8,128)(2,1)} %get-tuple-element.34) | copy-start | bytes 7077892
  104.3 5.0 %copy-start.17 = (bf16[256,768]{1,0:T(8,128)(2,1)}, bf16[256,768]{1,0:T(8,128)(2,1)S(1)}, u32[]{:S(2)}) copy-start(bf16[256,768]{1,0:T(8,128)(2,1)S(1)} %collective-permute-done.10) | copy-start | bytes 1179652
  107.2 15.4 %collective-permute-start.12 = (bf16[8,2,16,1152]{3,2,1,0:T(8,128)(2,1)}, bf16[8,2,16,1152]{3,2,1,0:T(8,128)(2,1)S(1)}, u32[]{:S(2)}, u32[]{:S(2)}) collective-permute-start(bf16[8,2,16,1152]{3,2,1,0:T(8,128)(2,1)} %get-tuple-element.40), channel_id=1, source_target_pairs={{12,0},{13,1},{14,2},{15,3},{0,4},{1,5},{2,6},{3,7},{4,8},{5,9},{6... | collective-permute-start | bytes 1769480 | tf_op jit(solution)/shard_map/ppermute | solution.py:326
  107.6 16.3 %collective-permute-start.13 = (bf16[8,2,16,1152]{3,2,1,0:T(8,128)(2,1)}, bf16[8,2,16,1152]{3,2,1,0:T(8,128)(2,1)}, u32[]{:S(2)}, u32[]{:S(2)}) collective-permute-start(bf16[8,2,16,1152]{3,2,1,0:T(8,128)(2,1)} %get-tuple-element.42), channel_id=1, source_target_pairs={{8,0},{9,1},{10,2},{11,3},{12,4},{13,5},{14,6},{15,7},{0,8},{1,9},... | collective-permute-start | bytes 1769480 | tf_op jit(solution)/shard_map/ppermute | solution.py:326
  107.6 27.9 %collective-permute-start.14 = (bf16[8,2,16,1152]{3,2,1,0:T(8,128)(2,1)S(1)}, bf16[8,2,16,1152]{3,2,1,0:T(8,128)(2,1)}, u32[]{:S(2)}, u32[]{:S(2)}) collective-permute-start(bf16[8,2,16,1152]{3,2,1,0:T(8,128)(2,1)S(1)} %get-tuple-element.41), channel_id=1, source_target_pairs={{4,0},{5,1},{6,2},{7,3},{8,4},{9,5},{10,6},{11,7},{12,8},{13,9},{1... | collective-permute-start | bytes 1769480 | tf_op jit(solution)/shard_map/ppermute | solution.py:326
  109.4 34.3 %all-to-all-start.2 = ((bf16[16,64,1152]{2,1,0:T(8,128)(2,1)}), bf16[16,64,1152]{2,1,0:T(8,128)(2,1)}, u32[]{:S(2)}, u32[]{:S(2)}) async-start(bf16[16,64,1152]{2,1,0:T(8,128)(2,1)} %bitcast.123), calls=%async_computation.2 | async-start | bytes 4718592 | tf_op jit(solution)/shard_map/all_to_all | solution.py:221
  114.9 5.4 %copy-start.2 = (f32[512,1536]{1,0:T(8,128)S(1)}, f32[512,1536]{1,0:T(8,128)}, u32[]{:S(2)}) copy-start(f32[512,1536]{1,0:T(8,128)} %copy-done.1) | copy-start | bytes 9437188
  119.3 18.7 %copy-start.5 = (f32[512,1536]{1,0:T(8,128)}, f32[512,1536]{1,0:T(8,128)S(1)}, u32[]{:S(2)}) copy-start(f32[512,1536]{1,0:T(8,128)S(1)} %fusion.19) | copy-start | bytes 9437188
  119.4 18.6 %copy-start.21 = (f32[256]{0:T(256)S(1)}, f32[256]{0:T(256)}, u32[]{:S(2)}) copy-start(f32[256]{0:T(256)} %copy-done.19) | copy-start | bytes 3076
  119.4 18.6 %copy-start.24 = (f32[256]{0:T(256)S(1)}, f32[256]{0:T(256)}, u32[]{:S(2)}) copy-start(f32[256]{0:T(256)} %copy-done.22) | copy-start | bytes 3076
  119.4 18.6 %collective-permute-start.11 = (bf16[256,1536]{1,0:T(8,128)(2,1)S(1)}, bf16[256,1536]{1,0:T(8,128)(2,1)S(1)}, u32[]{:S(2)}, u32[]{:S(2)}) collective-permute-start(bf16[256,1536]{1,0:T(8,128)(2,1)S(1)} %dynamic-slice_convert_fusion), channel_id=1, source_target_pairs={{0,1},{1,0},{2,3},{3,2},{4,5},{5,4},{6,7},{7,6},{8,9},{9,8},{10,11... | collective-permute-start | bytes 2359304 | tf_op jit(solution)/shard_map/ppermute | solution.py:124
  143.7 15.3 %all-to-all-start.3 = ((bf16[16,16,1152]{2,1,0:T(8,128)(2,1)}), bf16[16,16,1152]{2,1,0:T(8,128)(2,1)S(1)}, u32[]{:S(2)}, u32[]{:S(2)}) async-start(bf16[16,16,1152]{2,1,0:T(8,128)(2,1)} %bitcast.31), calls=%async_computation.3 | async-start | bytes 1179648 | tf_op jit(solution)/shard_map/all_to_all | solution.py:221
  151.9 3.6 %collective-permute-start.15 = (f32[16,1152]{1,0:T(8,128)S(1)}, f32[16,1152]{1,0:T(8,128)S(1)}, u32[]{:S(2)}, u32[]{:S(2)}) collective-permute-start(f32[16,1152]{1,0:T(8,128)S(1)} %get-tuple-element.59), channel_id=1, source_target_pairs={{12,0},{13,1},{14,2},{15,3},{0,4},{1,5},{2,6},{3,7},{4,8},{5,9},{6... | collective-permute-start | bytes 221192 | tf_op jit(solution)/shard_map/ppermute | solution.py:334
  152.4 5.1 %collective-permute-start.16 = (f32[16,1152]{1,0:T(8,128)S(1)}, f32[16,1152]{1,0:T(8,128)S(1)}, u32[]{:S(2)}, u32[]{:S(2)}) collective-permute-start(f32[16,1152]{1,0:T(8,128)S(1)} %get-tuple-element.61), channel_id=1, source_target_pairs={{8,0},{9,1},{10,2},{11,3},{12,4},{13,5},{14,6},{15,7},{0,8},{1,9},... | collective-permute-start | bytes 221192 | tf_op jit(solution)/shard_map/ppermute | solution.py:334
  155.5 3.5 %collective-permute-start.17 = (f32[16,1152]{1,0:T(8,128)S(1)}, f32[16,1152]{1,0:T(8,128)S(1)}, u32[]{:S(2)}, u32[]{:S(2)}) collective-permute-start(f32[16,1152]{1,0:T(8,128)S(1)} %get-tuple-element.60), channel_id=1, source_target_pairs={{4,0},{5,1},{6,2},{7,3},{8,4},{9,5},{10,6},{11,7},{12,8},{13,9},{1... | collective-permute-start | bytes 221192 | tf_op jit(solution)/shard_map/ppermute | solution.py:334
  159.2 14.2 %collective-permute-start.19 = (f32[6,1536]{1,0:T(8,128)S(1)}, f32[6,1536]{1,0:T(8,128)S(1)}, u32[]{:S(2)}, u32[]{:S(2)}) collective-permute-start(f32[6,1536]{1,0:T(8,128)S(1)} %pad_maximum_fusion.11), channel_id=1, source_target_pairs={{0,0},{1,64},{2,1},{3,65},{4,2},{5,66},{6,3},{7,67},{8,4},{9,68},{... | collective-permute-start | bytes 110600 | tf_op jit(solution)/shard_map/ppermute | solution.py:346
  170.4 2.9 %collective-permute-start.18 = (f32[12,1152]{1,0:T(8,128)S(1)}, f32[12,1152]{1,0:T(8,128)S(1)}, u32[]{:S(2)}, u32[]{:S(2)}) collective-permute-start(f32[12,1152]{1,0:T(8,128)S(1)} %fusion.44), channel_id=1, source_target_pairs={{0,1},{1,0},{2,3},{3,2},{4,5},{5,4},{6,7},{7,6},{8,9},{9,8},{10,11... | collective-permute-start | bytes 165896 | tf_op jit(solution)/shard_map/ppermute | solution.py:124

commit v3 on v2

--- a/solution.py
+++ b/solution.py
@@ -13,6 +13,7 @@
 PRIOR = 4
 WINDOW = (PRIOR + 1) * STRETCH
 PAIR = 2 * HEAD_DIM
+LEAD = 128
 EPS = 1e-05
 
 BF = jnp.bfloat16
@@ -113,7 +114,6 @@
 SWAP = [(device(d, t, c), device(d, t, 1 - c)) for d, t, c in EVERY]
 ONWARD = [(device(d, t, 1), device(d, t + 1, 1)) for d, t, c in EVERY if c and t + 1 < CHIPS]
 BACK = [(device(d, t, c), device(d, t - 1, c)) for d, t, c in EVERY if t > 0]
-OWNER = [(device(d, t, c), c * DP * CHIPS + d * CHIPS + t) for d, t, c in EVERY]
 
 
 def from_y(by):
@@ -124,83 +124,116 @@
     return lax.ppermute(value, ALL, SWAP)
 
 
-def gradients(
-    ctx_a, ctx_b, up_ref, low_ref, dq_a, dq_b, dk_a, dk_b, dv_a, dv_b, first_ref, late_ref, out_scr, d_ref
-):
-    step = pl.program_id(0)
-
-    @pl.when(step == 0)
+def fill(d_ref, at, early, late, halo, take):
+    count = d_ref.shape[0] - early.shape[0]
+    cols = slice(at, at + take.stop - take.start)
+    d_ref[:halo, cols] = early[:halo, take].astype(BF)
+    d_ref[halo : halo + count, cols] = (early[halo:, take] + late[:halo, take]).astype(BF)
+    d_ref[halo + count :, cols] = late[halo:, take].astype(BF)
+
+
+def late_gradients(low_ref, dq_a, dq_b, dk_a, dk_b, dv_a, dv_b, late_ref, d_ref):
+    @pl.when(pl.program_id(0) == 0)
     def _():
-        count, width = ctx_a.shape
-        out_scr[...] = (
-            tn(ctx_a[...], up_ref[:count, :]) + tn(ctx_b[...], up_ref[count:, :])
-        ).astype(BF)
+        count, width = dq_a.shape
         halo = d_ref.shape[0] - 2 * count
         d_ref[:halo, :width] = jnp.zeros((halo, width), BF)
         d_ref[halo : halo + count, :width] = dq_a[...]
         d_ref[halo + count :, :width] = dq_b[...]
-        for at, early, late in ((width, dk_a, dk_b), (2 * width, dv_a, dv_b)):
-            cols = slice(at, at + width)
-            d_ref[:halo, cols] = early[:halo, :].astype(BF)
-            d_ref[halo : halo + count, cols] = (early[halo:, :] + late[:halo, :]).astype(BF)
-            d_ref[halo + count :, cols] = late[halo:, :].astype(BF)
+        fill(d_ref, width, dk_a, dk_b, halo, slice(0, width))
+        fill(d_ref, 2 * width, dv_a, dv_b, halo, slice(0, LEAD))
+
+    grad = tn(low_ref[...], d_ref[...])
+    for j in range(2 * CHIPS):
+        dp, y, xh = j // CHIPS, j % CHIPS // 2, j % 2
+        late_ref[dp, xh, y] = grad[j * 24 : j * 24 + 24].astype(BF)
+
+
+def first_gradients(
+    y_ref, ctx_ref, up_ref, low_ref, dv_a, dv_b, *rest
+):
+    outs, (out_scr, d_ref, grad_scr, fold_scr) = rest[:ROWS_Y], rest[ROWS_Y:]
+    step = pl.program_id(0)
+    width = dv_a.shape[1]
+
+    @pl.when(step == 0)
+    def _():
+        out_scr[...] = tn(ctx_ref[...], up_ref[...]).astype(BF)
+        halo = d_ref.shape[0] - ctx_ref.shape[0]
+        fill(d_ref, 0, dv_a, dv_b, halo, slice(LEAD, width))
 
     own = 2 * CHIPS
-    columns = d_ref.shape[1]
-    third = columns // 3
-    to = lax.broadcasted_iota(jnp.int32, (own * 8, own * 6), 0)
-    at = lax.broadcasted_iota(jnp.int32, (own * 8, own * 6), 1)
-    base, slot = to // 8 * 6, to % 8
-    keep = ((slot < 6) & (at == base + slot)).astype(BF)
-    rows = out_scr[pl.ds(pl.multiple_of(step * own * 6, 32), own * 6), :]
-    parts = []
-    for b in range(3):
-        tail = (((slot == 6) & (at == base + b)) | ((slot == 7) & (at == base + 3 + b))).astype(BF)
-        parts.append(
-            nn(keep, rows[:, b * third : (b + 1) * third]) + nn(tail, rows[:, 3 * third :])
-        )
-    folded = jnp.concatenate(parts, axis=1)
-    grad = tn(low_ref[...], d_ref[...])
-    for j in range(own):
-        dp, y, xh = j // CHIPS, j % CHIPS // 2, j % 2
-        late_ref[dp, xh, y] = grad[j * 24 : j * 24 + 16].astype(BF)
-        first_ref[y, dp, xh] = jnp.concatenate(
-            [grad[j * 24 + 16 : j * 24 + 24], folded[j * 8 : j * 8 + 8]], axis=0
-        ).astype(BF)
-
-
-def weight_gradients(grad_all, low_ext, contexts, d_queries, d_keys, d_values):
-    wide = grad_all.shape[1]
-    width = contexts[0].shape[1]
-    ext, columns = low_ext.shape[0], 3 * width
+    to = lax.broadcasted_iota(jnp.int32, (own * 24, own * 12), 0)
+    at = lax.broadcasted_iota(jnp.int32, (own * 24, own * 12), 1)
+    base, slot = to // 24 * 12, to % 24
+    rows = out_scr[pl.ds(pl.multiple_of(step * own * 12, 64), own * 12), :]
+    folded = jnp.zeros((own * 24, width), F32)
+    for q in range(2):
+        pick = (slot >= q * 12) & (slot < q * 12 + 12) & (at == base + slot - q * 12)
+        folded += nn(pick.astype(BF), rows[:, q * width : (q + 1) * width])
+    fold_scr[...] = folded
+    grad_scr[...] = tn(low_ref[...], d_ref[...])
+    for k in range(ROWS_Y):
+        y = lax.rem(y_ref[0] + k, ROWS_Y)
+        for dp in range(2):
+            for xh in range(2):
+                chunk = pl.ds(pl.multiple_of(((dp * ROWS_Y + y) * 2 + xh) * 24, 8), 24)
+                outs[k][dp, xh] = jnp.concatenate(
+                    [grad_scr[chunk, :], fold_scr[chunk, :]], axis=1
+                ).astype(BF)
+
+
+def whole(value):
+    return pl.BlockSpec(value.shape, lambda i: (0, 0))
+
+
+def late_part(low_ext, *parts):
+    ext, wide = low_ext.shape
+    columns = 2 * parts[0].shape[1] + LEAD
     steps = DP // 2
-    parts = (*d_queries, *d_keys, *d_values)
-
-    def whole(value):
-        return pl.BlockSpec(value.shape, lambda i: (0, 0))
-
     return pl.pallas_call(
-        gradients,
+        late_gradients,
         grid=(steps,),
         in_specs=[
-            whole(contexts[0]),
-            whole(contexts[1]),
-            whole(grad_all),
             pl.BlockSpec((ext, wide // steps), lambda i: (0, i)),
             *[whole(part) for part in parts],
         ],
-        out_specs=[
-            pl.BlockSpec((ROWS_Y, 2, 2, 16, columns), lambda i: (0, i, 0, 0, 0)),
-            pl.BlockSpec((2, 2, ROWS_Y, 16, columns), lambda i: (i, 0, 0, 0, 0)),
-        ],
-        out_shape=[
-            jax.ShapeDtypeStruct((ROWS_Y, DP, 2, 16, columns), BF),
-            jax.ShapeDtypeStruct((DP, 2, ROWS_Y, 16, columns), BF),
-        ],
-        scratch_shapes=[pltpu.VMEM((width, wide), BF), pltpu.VMEM((ext, columns), BF)],
+        out_specs=pl.BlockSpec((2, 2, ROWS_Y, 24, columns), lambda i: (i, 0, 0, 0, 0)),
+        out_shape=jax.ShapeDtypeStruct((DP, 2, ROWS_Y, 24, columns), BF),
+        scratch_shapes=[pltpu.VMEM((ext, columns), BF)],
         compiler_params=pltpu.CompilerParams(vmem_limit_bytes=48 * 1024 * 1024),
-        name="weight_gradients",
-    )(*contexts, grad_all, low_ext, *parts)
+        name="late_gradients",
+    )(low_ext, *parts)
+
+
+def first_part(y, context, up_half, low_ext, dv_a, dv_b):
+    ext, wide = low_ext.shape
+    width = dv_a.shape[1]
+    steps = DP // 2
+    columns = 2 * width - LEAD
+    block = pl.BlockSpec((2, 2, 24, columns), lambda i: (i, 0, 0, 0))
+    return pl.pallas_call(
+        first_gradients,
+        grid=(steps,),
+        in_specs=[
+            pl.BlockSpec(memory_space=pltpu.SMEM),
+            whole(context),
+            whole(up_half),
+            pl.BlockSpec((ext, wide // steps), lambda i: (0, i)),
+            whole(dv_a),
+            whole(dv_b),
+        ],
+        out_specs=[block] * ROWS_Y,
+        out_shape=[jax.ShapeDtypeStruct((DP, 2, 24, columns), BF)] * ROWS_Y,
+        scratch_shapes=[
+            pltpu.VMEM((context.shape[1], up_half.shape[1]), BF),
+            pltpu.VMEM((ext, width - LEAD), BF),
+            pltpu.VMEM((2 * CHIPS * 24, width - LEAD), F32),
+            pltpu.VMEM((2 * CHIPS * 24, width), F32),
+        ],
+        compiler_params=pltpu.CompilerParams(vmem_limit_bytes=48 * 1024 * 1024),
+        name="first_gradients",
+    )(y.reshape(1), context, up_half, low_ext, dv_a, dv_b)
 
 
 def own_half(core, value, size, axis=0):
@@ -221,9 +254,12 @@
     return lax.all_to_all(chunks, ("z", "xl", "xh"), 0, 0, tiled=True)
 
 
-def gather(shard):
-    copies = jnp.broadcast_to(shard[None], (DP,) + shard.shape)
-    return lax.all_to_all(copies, ("z", "xl"), 0, 0, tiled=True)
+def copies(shard):
+    return jnp.broadcast_to(shard[None], (DP,) + shard.shape)
+
+
+def gather(shards):
+    return lax.all_to_all(shards, ("z", "xl"), 0, 0, tiled=True)
 
 
 def body(frames, upstream, utt_span, w_qkv, w_out):
@@ -259,9 +295,17 @@
         ],
         axis=1,
     )
-    quarter = gather(lax.dynamic_index_in_dim(indirect, y, axis=0, keepdims=False))
-    shard, quarter = lax.optimization_barrier((mine[:direct], quarter))
-    full_direct = gather(shard)
+    pieces = copies(lax.dynamic_index_in_dim(indirect, y, axis=0, keepdims=False))
+    shards = copies(mine[:direct])
+    own_frames, own_grad, pieces = lax.optimization_barrier((own_frames, own_grad, pieces))
+    normed, inv_sigma = normalize(own_frames)
+    own_low = normed.astype(BF)
+    own_low, other_low = lax.optimization_barrier((own_low, swap(own_low)))
+    low = in_order(lower, own_low, other_low, 0)
+    past = lax.ppermute(own_low, ALL, ONWARD)
+    quarter = gather(pieces)
+    shards, quarter, past = lax.optimization_barrier((shards, quarter, past))
+    full_direct = gather(shards)
     quarters = jnp.zeros((ROWS_Y,) + quarter.shape, BF)
     for k in range(ROWS_Y):
         got = quarter if k == 0 else lax.ppermute(quarter, ALL, from_y(k))
@@ -287,12 +331,9 @@
         1,
     )
 
-    normed, inv_sigma = normalize(own_frames)
-    own_low = normed.astype(BF)
-    low = both(own_low)
-    past = lax.ppermute(own_low, ALL, ONWARD)
     low_ext = jnp.concatenate([jnp.where(lower, swap(past), past), low], axis=0)
     grad_all = both(own_grad)
+    up_half = own_half(core, grad_all, out_cols, axis=1)
 
     spans = jnp.swapaxes(utt_span[:, 0], 0, 1)
     spans = both(spans).T - (y * 2 + lax.axis_index("xh")) * (CORES * count) + halo
@@ -312,41 +353,43 @@
         count, blocked[0, middle:], blocked[1, middle:], projected, d_context[count:]
     )
     context = jnp.concatenate([ctx_a, ctx_b], axis=0)
+    all_context = in_order(lower, context, swap(context), 1)
 
     d_low = jnp.concatenate([dk_a[halo:] + dk_b[:halo], dv_a[halo:] + dv_b[:halo]], axis=1)
     d_low = jnp.concatenate([dq_a, d_low.astype(BF)], axis=1)
     d_last = jnp.concatenate([dk_b[halo:], dv_b[halo:]], axis=1)
-    first, late = weight_gradients(
-        grad_all, low_ext, (ctx_a, ctx_b), (dq_a, dq_b), (dk_a, dk_b), (dv_a, dv_b)
-    )
-    first, late, returned = lax.optimization_barrier((first, late, returned))
-    summed = lax.dynamic_index_in_dim(first, y, axis=0, keepdims=False).astype(F32)
+    late = late_part(low_ext, dq_a, dq_b, dk_a, dk_b, dv_a, dv_b)
+    late, returned, dv_a, dv_b, context = lax.optimization_barrier(
+        (late, returned, dv_a, dv_b, context)
+    )
+    arrived = scatter(late.reshape(chips // ROWS_Y, -1, late.shape[-1]))
+    first = first_part(y, all_context, up_half, low_ext, dv_a, dv_b)
+    summed = first[0].astype(F32)
     for k in range(1, ROWS_Y):
-        away = lax.dynamic_index_in_dim(first, (y + k) % ROWS_Y, axis=0, keepdims=False)
-        summed = summed + lax.ppermute(away, ALL, from_y(-k)).astype(F32)
-    summed = summed.astype(BF).reshape(chips // ROWS_Y, 16, 3 * width)
-    arrived = scatter(late.reshape(chips // ROWS_Y, ROWS_Y * 16, 3 * width))
-    summed, arrived = lax.optimization_barrier((summed, arrived))
-    planes = jnp.sum(arrived.astype(F32), axis=0).reshape(ROWS_Y, 16, 3 * width)
+        summed = summed + lax.ppermute(first[k], ALL, from_y(-k)).astype(F32)
+    summed = summed.astype(BF).reshape(chips // ROWS_Y, 24, -1)
+    summed, arrived, dq_b, d_low, d_last, returned = lax.optimization_barrier(
+        (summed, arrived, dq_b, d_low, d_last, returned)
+    )
+    planes = jnp.sum(arrived.astype(F32), axis=0).reshape(ROWS_Y, -1, late.shape[-1])
     total_late = lax.dynamic_index_in_dim(planes, y, axis=0, keepdims=False)
     for k in range(1, ROWS_Y):
         away = lax.dynamic_index_in_dim(planes, (y + k) % ROWS_Y, axis=0, keepdims=False)
         total_late = total_late + lax.ppermute(away, ALL, from_y(-k))
     total_first = jnp.sum(scatter(summed).astype(F32), axis=0)
-    total = jnp.concatenate([total_late, total_first], axis=0)
     d_proj = jnp.concatenate(
         [d_low, jnp.concatenate([dq_b, (d_last + returned.astype(F32)).astype(BF)], axis=1)], axis=0
     )
 
-    o_total = total[CORES * (wide // chips // CORES) :]
     o_rows = inner // chips // CORES
-    o_out = jnp.concatenate(
-        [o_total[:o_rows], o_total[o_rows:].reshape(o_rows, wide - 3 * width)], axis=1
-    )
-    o_out = lax.ppermute(o_out, ALL, OWNER)
+    folds = total_first[:, width - LEAD :].reshape(2, CORES * o_rows, width)
+    o_total = jnp.concatenate([folds[0], folds[1]], axis=1)
+    o_out = in_order(
+        lower, own_half(core, o_total, o_rows), swap(other_half(core, o_total, o_rows)), 1
+    )
 
     rows = wide // chips // CORES
-    total = total[: CORES * rows]
+    total = jnp.concatenate([total_late, total_first[:, : width - LEAD]], axis=1)
     q_kept = own_half(core, total, rows).reshape(rows, 3, width)
     q_other = swap(other_half(core, total, rows)).reshape(rows, 3, width)
     q_out = in_order(lower, q_kept, q_other, 2).reshape(rows, 3 * inner)

time: 177 us -> 169 us (0.955)
  starting transfers between devices: 57.4 us -> 45.5 us
  waiting for transfers between devices: 46.2 us -> 55.3 us
  other arithmetic: 23.2 us -> 17.3 us
  matrix products: 9.55 us -> 7.41 us
  Pallas kernels: 18.1 us -> 19.9 us
    ppermute x4 -> x3, starting transfers between devices: 13.4 us -> 2.46 us  [body(): summed = summed + lax.ppermute(first[k], ALL, from_y(-k)).astype(F32)]
    ppermute x1, waiting for transfers between devices: 0.01 us -> 8.45 us  [body(): past = lax.ppermute(own_low, ALL, ONWARD)]
    ppermute x4 -> x3, waiting for transfers between devices: 12.9 us -> 20 us  [body(): summed = summed + lax.ppermute(first[k], ALL, from_y(-k)).astype(F32)]
    ppermute x3, waiting for transfers between devices: 3.49 us -> 0.01 us  [body(): total_late = total_late + lax.ppermute(away, ALL, from_y(-k))]
    broadcast_in_dim x2, other arithmetic: 5.12 us -> 2.51 us  [body(): return (branch[None], grad_in.astype(BF)[None], q_out, o_out)]
    dot_general x2, matrix products: 5.37 us -> 3.22 us  [nt(): lax.dot_general(a, b, (((1,), (1,)), ((), ())), preferred_element_type=F32)]
    select_n x5 -> x7, other arithmetic: 3.11 us -> 5.16 us  [in_order(): jnp.where(lower, own, other)]
    convert_element_type x1, other arithmetic: 2.3 us -> 0.32 us  [body(): own_low = normed.astype(BF)]
  transfers between devices with their start and end apart: 24 -> 25, of which waited for: 10 -> 10; matrix products, arithmetic and copies ran while one was open for 19% -> 13% of each run, Pallas kernels for 7% -> 9%
where the time goes in v3:
time: 169 us; the launch traced here: 165 us
  waiting for transfers between devices  55.3 us (33%)
  starting transfers between devices  45.5 us (27%)
  Pallas kernels  19.9 us (12%)
  local copies, waits for them, and re-layouts  18.6 us (11%)
  other arithmetic  17.3 us (10%)
  matrix products  7.41 us (4%)
    ppermute x3, waiting for transfers between devices, body(): summed = summed + lax.ppermute(first[k], ALL, from_y(-k)).astype(F32)  20 us
    ppermute x3, waiting for transfers between devices, body(): got = quarter if k == 0 else lax.ppermute(quarter, ALL, from_y(k))  11.8 us
    all_to_all x2, starting transfers between devices, scatter(): return lax.all_to_all(chunks, ('z', 'xl', 'xh'), 0, 0, tiled=True)  11.2 us
    all_to_all x2, starting transfers between devices, gather(): return lax.all_to_all(shards, ('z', 'xl'), 0, 0, tiled=True)  10.6 us
    pallas_call x2, Pallas kernels, attention(): pl.pallas_call(functools.partial(attend, first), in_specs=[whole] * 4, ou...  10.2 us
    unnamed x62, local copies, waits for them, and re-layouts  10.1 us
    all_to_all x2, waiting for transfers between devices, gather(): return lax.all_to_all(shards, ('z', 'xl'), 0, 0, tiled=True)  10.1 us
    ppermute x1, waiting for transfers between devices, body(): past = lax.ppermute(own_low, ALL, ONWARD)  8.45 us
  transfers between devices with their start and end apart: 25, of which 10 were waited for; matrix products, arithmetic and copies ran while one was open for 13% of the time, Pallas kernels for 9%

profile of v3, /device:TPU:9, one launch (start us, length us, event | category | flops | bytes accessed | tf_op | source)
XLA Modules:
  0.0 165.5 jit_solution(9468424402678043637)
XLA Ops:
  0.7 1.0 constant_dynamic-slice_fusion
  1.6 2.2 %reshape.82 = bf16[192,3,768]{2,1,0:T(4,128)(2,1)S(1)} reshape(bf16[192,2304]{1,0:T(8,128)(2,1)} %param.8) | data formatting | bytes 1769472 | tf_op jit(solution)/shard_map/reshape | solution.py:281
  4.0 0.8 fusion.58
  4.9 0.9 broadcast_in_dim.46
  5.9 0.3 fusion.15
  6.3 0.3 fusion.7
  6.6 0.8 collective-permute-start
  7.5 6.0 %all-to-all-start = ((bf16[8,32,1152]{2,1,0:T(8,128)(2,1)}), bf16[8,32,1152]{2,1,0:T(8,128)(2,1)S(1)}, u32[]{:S(2)}, u32[]{:S(2)}) async-start(bf16[8,32,1152]{2,1,0:T(8,128)(2,1)} %broadcast_in_dim.46), calls=%async_computation | async-start | bytes 1179648 | tf_op jit(solution)/shard_map/all_to_all | solution.py:262
  13.4 0.7 collective-permute-start.7
  14.3 4.4 %collective-permute-start.1 = (bf16[256,1536]{1,0:T(8,128)(2,1)S(1)}, bf16[256,1536]{1,0:T(8,128)(2,1)}, u32[]{:S(2)}, u32[]{:S(2)}) collective-permute-start(bf16[256,1536]{1,0:T(8,128)(2,1)S(1)} %fusion.7), channel_id=1, source_target_pairs={{1,3},{3,5},{5,7},{7,9},{9,11},{11,13},{13,15},{17,19},{19,21},{21... | collective-permute-start | bytes 2359304 | tf_op jit(solution)/shard_map/ppermute | solution.py:305
  19.5 3.8 %all-to-all-done = bf16[8,32,1152]{2,1,0:T(8,128)(2,1)S(1)} async-done(((bf16[8,32,1152]{2,1,0:T(8,128)(2,1)}), bf16[8,32,1152]{2,1,0:T(8,128)(2,1)S(1)}, u32[]{:S(2)}, u32[]{:S(2)}) %all-to-all-start) | async-done | bytes 589856 | tf_op jit(solution)/shard_map/all_to_all | solution.py:262
  23.3 8.5 %collective-permute-done.1 = bf16[256,1536]{1,0:T(8,128)(2,1)} collective-permute-done((bf16[256,1536]{1,0:T(8,128)(2,1)S(1)}, bf16[256,1536]{1,0:T(8,128)(2,1)}, u32[]{:S(2)}, u32[]{:S(2)}) %collective-permute-start.1) | collective-permute-done | bytes 786464 | tf_op jit(solution)/shard_map/ppermute | solution.py:305
  31.8 1.7 %broadcast_in_dim.44 = bf16[8,128,1152]{2,1,0:T(8,128)(2,1)} broadcast(bf16[128,1152]{1,0:T(8,128)(2,1)S(1)} %copy.10), dimensions={1,2} | broadcast | bytes 2654208 | tf_op jit(solution)/shard_map/broadcast_in_dim | solution.py:258
  33.5 2.4 %broadcast_select_fusion.3 = (bf16[256,1536]{1,0:T(8,128)(2,1)}, bf16[256,1536]{1,0:T(8,128)(2,1)}) fusion(bf16[256,1536]{1,0:T(8,128)(2,1)S(1)} %fusion.7, bf16[256,1536]{1,0:T(8,128)(2,1)} %collective-permute-done, pred[]{:T(512)S(6)} %eq.11), kind=kLoop, calls=%fused_computation.56 | loop fusion | flops 786432 | bytes 3145729 | tf_op jit(solution)/shard_map/jit(_where)/select_n | solution.py:249
  35.9 1.5 collective-permute-start.6
  37.3 3.5 %collective-permute-start.5 = (bf16[8,32,1152]{2,1,0:T(8,128)(2,1)S(1)}, bf16[8,32,1152]{2,1,0:T(8,128)(2,1)S(1)}, u32[]{:S(2)}, u32[]{:S(2)}) collective-permute-start(bf16[8,32,1152]{2,1,0:T(8,128)(2,1)S(1)} %all-to-all-done), channel_id=1, source_target_pairs={{8,0},{9,1},{10,2},{11,3},{12,4},{13,5},{14,6},{15,7},{0,8},{1,9},... | collective-permute-start | bytes 1769480 | tf_op jit(solution)/shard_map/ppermute | solution.py:311
  40.8 4.6 %all-to-all-start.1 = ((bf16[8,128,1152]{2,1,0:T(8,128)(2,1)}), bf16[8,128,1152]{2,1,0:T(8,128)(2,1)}, u32[]{:S(2)}, u32[]{:S(2)}) async-start(bf16[8,128,1152]{2,1,0:T(8,128)(2,1)} %broadcast_in_dim.44), calls=%async_computation.1 | async-start | bytes 4718592 | tf_op jit(solution)/shard_map/all_to_all | solution.py:262
  45.8 2.2 %collective-permute-done.4 = bf16[8,32,1152]{2,1,0:T(8,128)(2,1)S(1)} collective-permute-done((bf16[8,32,1152]{2,1,0:T(8,128)(2,1)S(1)}, bf16[8,32,1152]{2,1,0:T(8,128)(2,1)S(1)}, u32[]{:S(2)}, u32[]{:S(2)}) %collective-permute-start.4) | collective-permute-done | bytes 589856 | tf_op jit(solution)/shard_map/ppermute | solution.py:311
  48.1 9.5 %collective-permute-done.5 = bf16[8,32,1152]{2,1,0:T(8,128)(2,1)S(1)} collective-permute-done((bf16[8,32,1152]{2,1,0:T(8,128)(2,1)S(1)}, bf16[8,32,1152]{2,1,0:T(8,128)(2,1)S(1)}, u32[]{:S(2)}, u32[]{:S(2)}) %collective-permute-start.5) | collective-permute-done | bytes 589856 | tf_op jit(solution)/shard_map/ppermute | solution.py:311
  58.0 1.1 copy-done.9
  59.6 1.3 broadcast_select_fusion.1
  60.9 1.5 broadcast_select_fusion.4
  62.8 0.8 copy-done.17
  63.6 1.0 fusion.16
  64.6 6.2 %all-to-all-done.1 = bf16[8,128,1152]{2,1,0:T(8,128)(2,1)} async-done(((bf16[8,128,1152]{2,1,0:T(8,128)(2,1)}), bf16[8,128,1152]{2,1,0:T(8,128)(2,1)}, u32[]{:S(2)}, u32[]{:S(2)}) %all-to-all-start.1) | async-done | bytes 2359328 | tf_op jit(solution)/shard_map/all_to_all | solution.py:262
  70.8 2.0 %constant_dynamic-update-slice_fusion = bf16[8,192,1152]{2,1,0:T(8,128)(2,1)S(1)} fusion(bf16[8,128,1152]{2,1,0:T(8,128)(2,1)} %all-to-all-done.1), kind=kLoop, calls=%fused_computation.113 | loop fusion | bytes 4718592
  72.9 0.3 copy-done.10
  73.4 1.0 copy-done.15
  74.4 0.8 copy-done.16
  75.2 3.2 %convolution_convert_fusion.proj_ref = bf16[768,1152]{1,0:T(8,128)(2,1)S(1)} fusion(bf16[1536,1152]{1,0:T(8,128)(2,1)S(1)} %bitcast.93, bf16[256,1536]{1,0:T(8,128)(2,1)S(1)} %copy-done.16, bf16[256,1536]{1,0:T(8,128)(2,1)S(1)} %copy-done.15, bf16[256,1536]{1,0:T(8,128)(2,1)S(1)} %broadcast_select_fusion.4), kind=kOutput, calls=%fused_computation.1 | convolution fusion | flops 2725871616 | bytes 7667712 | tf_op jit(solution)/shard_map/dot_general | solution.py:32
  78.4 5.1 %attend.2 = (bf16[256,384]{1,0:T(8,128)(2,1)S(1)}, bf16[256,384]{1,0:T(8,128)(2,1)S(1)}, f32[512,384]{1,0:T(8,128)S(1)}, f32[512,384]{1,0:T(8,128)S(1)}) custom-call(s32[4,128]{1,0:T(4,128)S(1)} %get-tuple-element.100.lo_ref, s32[4,128]{1,0:T(4,128)S(1)} %get-tuple-element.98.hi_ref, bf16[768,1152]{1,0:T(8,128)(2,1)S(1)} %convolution_convert_fusion.proj_ref, ...), custom_call_target="tpu_custom_call" | custom-call | tf_op jit(solution)/shard_map/attend/pallas_call | solution.py:82
  83.7 4.1 %collective-permute-start.9 = (bf16[256,768]{1,0:T(8,128)(2,1)S(1)}, bf16[256,768]{1,0:T(8,128)(2,1)S(1)}, u32[]{:S(2)}, u32[]{:S(2)}) collective-permute-start(bf16[256,768]{1,0:T(8,128)(2,1)S(1)} %pad_maximum_fusion.15), channel_id=1, source_target_pairs={{2,0},{3,1},{4,2},{5,3},{6,4},{7,5},{8,6},{9,7},{10,8},{11,9},{12,... | collective-permute-start | bytes 1179656 | tf_op jit(solution)/shard_map/ppermute | solution.py:351
  87.8 5.1 %attend.3 = (bf16[256,384]{1,0:T(8,128)(2,1)S(1)}, bf16[256,384]{1,0:T(8,128)(2,1)S(1)}, f32[512,384]{1,0:T(8,128)S(1)}, f32[512,384]{1,0:T(8,128)S(1)}) custom-call(s32[4,128]{1,0:T(4,128)S(1)} %get-tuple-element.99.lo_ref, s32[4,128]{1,0:T(4,128)S(1)} %get-tuple-element.97.hi_ref, bf16[768,1152]{1,0:T(8,128)(2,1)S(1)} %convolution_convert_fusion.proj_ref, ...), custom_call_target="tpu_custom_call" | custom-call | tf_op jit(solution)/shard_map/attend/pallas_call | solution.py:82
  93.3 0.5 copy-done.3
  93.8 4.5 %late_gradients.1 = bf16[8,2,4,24,896]{4,3,2,1,0:T(8,128)(2,1)} custom-call(bf16[768,1536]{1,0:T(8,128)(2,1)S(1)} %pad_maximum_fusion.low_ref, bf16[256,384]{1,0:T(8,128)(2,1)S(1)} %get-tuple-element.43.dq_a, bf16[256,384]{1,0:T(8,128)(2,1)S(1)} %get-tuple-element.61.dq_b, f32[512,384]{1,0:T(8,128)S(1)} %get-tuple-element.45.dk_a, ...), custom_call_target="tpu_custom_call" | custom-call | tf_op jit(solution)/shard_map/late_gradients/pallas_call | solution.py:194
  98.4 0.8 copy-done.24
  99.1 4.6 %all-to-all-start.2 = ((bf16[16,96,896]{2,1,0:T(8,128)(2,1)}), bf16[16,96,896]{2,1,0:T(8,128)(2,1)}, u32[]{:S(2)}, u32[]{:S(2)}) async-start(bf16[16,96,896]{2,1,0:T(8,128)(2,1)} %bitcast.90), calls=%async_computation.2 | async-start | bytes 5505024 | tf_op jit(solution)/shard_map/all_to_all | solution.py:254
  103.9 1.1 broadcast_select_fusion.8
  105.1 5.1 %first_gradients.1 = (bf16[8,2,24,640]{3,2,1,0:T(8,128)(2,1)S(1)}, bf16[8,2,24,640]{3,2,1,0:T(8,128)(2,1)S(1)}, bf16[8,2,24,640]{3,2,1,0:T(8,128)(2,1)S(1)}, bf16[8,2,24,640]{3,2,1,0:T(8,128)(2,1)S(1)}) custom-call(s32[1]{0:T(128)} %bitcast.26.y_ref, bf16[512,768]{1,0:T(8,128)(2,1)S(1)} %pad_maximum_fusion.10.ctx_ref, bf16[512,768]{1,0:T(8,128)(2,1)S(1)} %fusion.28.up_ref, ...), custom_call_target="tpu_custom_call" | custom-call | tf_op jit(solution)/shard_map/first_gradients/pallas_call | solution.py:215
  110.2 0.6 collective-permute-start.12
  110.8 0.9 collective-permute-start.13
  111.7 1.0 collective-permute-start.14
  112.7 1.0 fusion.29
  113.8 0.7 collective-permute-start.10
  114.7 8.5 %collective-permute-done.12 = bf16[8,2,24,640]{3,2,1,0:T(8,128)(2,1)S(1)} collective-permute-done((bf16[8,2,24,640]{3,2,1,0:T(8,128)(2,1)S(1)}, bf16[8,2,24,640]{3,2,1,0:T(8,128)(2,1)S(1)}, u32[]{:S(2)}, u32[]{:S(2)}) %collective-permute-start.12) | collective-permute-done | bytes 491552 | tf_op jit(solution)/shard_map/ppermute | solution.py:369
  123.3 1.7 %collective-permute-done.13 = bf16[8,2,24,640]{3,2,1,0:T(8,128)(2,1)S(1)} collective-permute-done((bf16[8,2,24,640]{3,2,1,0:T(8,128)(2,1)S(1)}, bf16[8,2,24,640]{3,2,1,0:T(8,128)(2,1)S(1)}, u32[]{:S(2)}, u32[]{:S(2)}) %collective-permute-start.13) | collective-permute-done | bytes 491552 | tf_op jit(solution)/shard_map/ppermute | solution.py:369
  125.0 9.7 %collective-permute-done.14 = bf16[8,2,24,640]{3,2,1,0:T(8,128)(2,1)S(1)} collective-permute-done((bf16[8,2,24,640]{3,2,1,0:T(8,128)(2,1)S(1)}, bf16[8,2,24,640]{3,2,1,0:T(8,128)(2,1)S(1)}, u32[]{:S(2)}, u32[]{:S(2)}) %collective-permute-start.14) | collective-permute-done | bytes 491552 | tf_op jit(solution)/shard_map/ppermute | solution.py:369
  134.7 1.0 add_convert_fusion.1
  135.8 1.1 fusion.26
  136.8 4.3 %all-to-all-done.2 = bf16[16,96,896]{2,1,0:T(8,128)(2,1)} async-done(((bf16[16,96,896]{2,1,0:T(8,128)(2,1)}), bf16[16,96,896]{2,1,0:T(8,128)(2,1)}, u32[]{:S(2)}, u32[]{:S(2)}) %all-to-all-start.2) | async-done | bytes 2752544 | tf_op jit(solution)/shard_map/all_to_all | solution.py:254
  141.1 6.6 %all-to-all-start.3 = ((bf16[16,24,640]{2,1,0:T(8,128)(2,1)}), bf16[16,24,640]{2,1,0:T(8,128)(2,1)S(1)}, u32[]{:S(2)}, u32[]{:S(2)}) async-start(bf16[16,24,640]{2,1,0:T(8,128)(2,1)} %bitcast.27), calls=%async_computation.3 | async-start | bytes 983040 | tf_op jit(solution)/shard_map/all_to_all | solution.py:254
  147.7 2.4 %convert_reduce_fusion = f32[96,896]{1,0:T(8,128)S(1)} fusion(bf16[16,96,896]{2,1,0:T(8,128)(2,1)} %all-to-all-done.2), kind=kLoop, calls=%fused_computation | loop fusion | flops 2666496 | bytes 3096576 | tf_op jit(solution)/shard_map/reduce_sum | solution.py:374
  150.1 0.6 collective-permute-start.16
  150.7 1.0 collective-permute-start.18
  151.7 0.3 collective-permute-start.17
  152.0 2.2 %fusion.20 = f32[512,1536]{1,0:T(8,128)S(1)} fusion(bf16[1536,1152]{1,0:T(8,128)(2,1)S(1)} %bitcast.94, bf16[256,768]{1,0:T(8,128)(2,1)S(1)} %add_convert_fusion.2, bf16[256,384]{1,0:T(8,128)(2,1)S(1)} %get-tuple-element.61.dq_b, bf16[256,1152]{1,0:T(8,128)(2,1)S(1)} %pad_maximum_fusion.14), kind=kOutput, calls=%fused_computation.39 | convolution fusion | flops 1815478272 | bytes 7864320 | tf_op jit(solution)/shard_map/dot_general | solution.py:24
  154.3 1.6 copy-done.11
  156.0 1.7 %collective-permute-start.15 = (bf16[256,1536]{1,0:T(8,128)(2,1)S(1)}, bf16[256,1536]{1,0:T(8,128)(2,1)S(1)}, u32[]{:S(2)}, u32[]{:S(2)}) collective-permute-start(bf16[256,1536]{1,0:T(8,128)(2,1)S(1)} %dynamic-slice_convert_fusion), channel_id=1, source_target_pairs={{0,1},{1,0},{2,3},{3,2},{4,5},{5,4},{6,7},{7,6},{8,9},{9,8},{10,11... | collective-permute-start | bytes 2359304 | tf_op jit(solution)/shard_map/ppermute | solution.py:124
  157.8 1.6 collective-permute-start.20
  159.6 0.7 collective-permute-done.20
  160.3 0.6 pad_maximum_fusion.17
  161.2 0.7 copy.12
  161.9 2.1 %fusion.30 = (f32[256]{0:T(256)S(1)}, f32[256]{0:T(256)S(1)}) fusion(bf16[256,1536]{1,0:T(8,128)(2,1)S(1)} %collective-permute-done.15, f32[512,1536]{1,0:T(8,128)} %copy-done.11, s32[]{:T(128)S(6)} %select_n.192, f32[256]{0:T(256)S(1)} %add_rsqrt_fusion, f32[256]{0:T(256)S(1)} %broadcast_multiply_fusion.2, bf16[256,1536]{1,0:T(8,128)(2,1)S(1)} %bitcast.88), kind=kLoop, calls=%fused_computation.66 | loop fusion | flops 3145216 | bytes 3149828 | tf_op jit(solution)/shard_map/reduce_sum | solution.py:409
  164.0 1.5 fusion.27
  (127 shorter events, 4.7 us)
Async XLA Ops:
  0.6 5.1 %copy-start.7 = (bf16[1,256,1536]{2,1,0:T(8,128)(2,1)S(1)}, bf16[1,256,1536]{2,1,0:T(8,128)(2,1)}, u32[]{:S(2)}) copy-start(bf16[1,256,1536]{2,1,0:T(8,128)(2,1)} %param.5) | copy-start | bytes 2359300
  4.0 3.3 %copy-start.26 = (s32[2,1,256]{2,1,0:T(1,128)S(1)}, s32[2,1,256]{2,1,0:T(1,128)}, u32[]{:S(2)}) copy-start(s32[2,1,256]{2,1,0:T(1,128)} %param.7) | copy-start | bytes 6148
  6.6 7.7 %collective-permute-start = (bf16[256,1536]{1,0:T(8,128)(2,1)S(1)}, bf16[256,1536]{1,0:T(8,128)(2,1)}, u32[]{:S(2)}, u32[]{:S(2)}) collective-permute-start(bf16[256,1536]{1,0:T(8,128)(2,1)S(1)} %fusion.7), channel_id=1, source_target_pairs={{0,1},{1,0},{2,3},{3,2},{4,5},{5,4},{6,7},{7,6},{8,9},{9,8},{10,11... | collective-permute-start | bytes 2359304 | tf_op jit(solution)/shard_map/ppermute | solution.py:124
  7.4 11.9 %collective-permute-start.3 = (s32[256,2]{0,1:T(2,128)S(1)}, s32[256,2]{0,1:T(2,128)S(1)}, u32[]{:S(2)}, u32[]{:S(2)}) collective-permute-start(s32[256,2]{0,1:T(2,128)S(1)} %bitcast.103), channel_id=1, source_target_pairs={{0,1},{1,0},{2,3},{3,2},{4,5},{5,4},{6,7},{7,6},{8,9},{9,8},{10,11... | collective-permute-start | bytes 6152 | tf_op jit(solution)/shard_map/ppermute | solution.py:124
  7.5 15.9 %all-to-all-start = ((bf16[8,32,1152]{2,1,0:T(8,128)(2,1)}), bf16[8,32,1152]{2,1,0:T(8,128)(2,1)S(1)}, u32[]{:S(2)}, u32[]{:S(2)}) async-start(bf16[8,32,1152]{2,1,0:T(8,128)(2,1)} %broadcast_in_dim.46), calls=%async_computation | async-start | bytes 1179648 | tf_op jit(solution)/shard_map/all_to_all | solution.py:262
  13.4 46.0 %collective-permute-start.7 = (bf16[256,1536]{1,0:T(8,128)(2,1)}, bf16[256,1536]{1,0:T(8,128)(2,1)}, u32[]{:S(2)}, u32[]{:S(2)}) collective-permute-start(bf16[256,1536]{1,0:T(8,128)(2,1)} %bitcast.99), channel_id=1, source_target_pairs={{0,1},{1,0},{2,3},{3,2},{4,5},{5,4},{6,7},{7,6},{8,9},{9,8},{10,11... | collective-permute-start | bytes 2359304 | tf_op jit(solution)/shard_map/ppermute | solution.py:124
  14.3 17.5 %collective-permute-start.1 = (bf16[256,1536]{1,0:T(8,128)(2,1)S(1)}, bf16[256,1536]{1,0:T(8,128)(2,1)}, u32[]{:S(2)}, u32[]{:S(2)}) collective-permute-start(bf16[256,1536]{1,0:T(8,128)(2,1)S(1)} %fusion.7), channel_id=1, source_target_pairs={{1,3},{3,5},{5,7},{7,9},{9,11},{11,13},{13,15},{17,19},{19,21},{21... | collective-permute-start | bytes 2359304 | tf_op jit(solution)/shard_map/ppermute | solution.py:305
  33.5 14.5 %collective-permute-start.4 = (bf16[8,32,1152]{2,1,0:T(8,128)(2,1)S(1)}, bf16[8,32,1152]{2,1,0:T(8,128)(2,1)S(1)}, u32[]{:S(2)}, u32[]{:S(2)}) collective-permute-start(bf16[8,32,1152]{2,1,0:T(8,128)(2,1)S(1)} %all-to-all-done), channel_id=1, source_target_pairs={{4,0},{5,1},{6,2},{7,3},{8,4},{9,5},{10,6},{11,7},{12,8},{13,9},{1... | collective-permute-start | bytes 1769480 | tf_op jit(solution)/shard_map/ppermute | solution.py:311
  35.9 21.8 %collective-permute-start.6 = (bf16[8,32,1152]{2,1,0:T(8,128)(2,1)S(1)}, bf16[8,32,1152]{2,1,0:T(8,128)(2,1)S(1)}, u32[]{:S(2)}, u32[]{:S(2)}) collective-permute-start(bf16[8,32,1152]{2,1,0:T(8,128)(2,1)S(1)} %all-to-all-done), channel_id=1, source_target_pairs={{12,0},{13,1},{14,2},{15,3},{0,4},{1,5},{2,6},{3,7},{4,8},{5,9},{6... | collective-permute-start | bytes 1769480 | tf_op jit(solution)/shard_map/ppermute | solution.py:311
  37.3 20.3 %collective-permute-start.5 = (bf16[8,32,1152]{2,1,0:T(8,128)(2,1)S(1)}, bf16[8,32,1152]{2,1,0:T(8,128)(2,1)S(1)}, u32[]{:S(2)}, u32[]{:S(2)}) collective-permute-start(bf16[8,32,1152]{2,1,0:T(8,128)(2,1)S(1)} %all-to-all-done), channel_id=1, source_target_pairs={{8,0},{9,1},{10,2},{11,3},{12,4},{13,5},{14,6},{15,7},{0,8},{1,9},... | collective-permute-start | bytes 1769480 | tf_op jit(solution)/shard_map/ppermute | solution.py:311
  40.8 30.0 %all-to-all-start.1 = ((bf16[8,128,1152]{2,1,0:T(8,128)(2,1)}), bf16[8,128,1152]{2,1,0:T(8,128)(2,1)}, u32[]{:S(2)}, u32[]{:S(2)}) async-start(bf16[8,128,1152]{2,1,0:T(8,128)(2,1)} %broadcast_in_dim.44), calls=%async_computation.1 | async-start | bytes 4718592 | tf_op jit(solution)/shard_map/all_to_all | solution.py:262
  45.5 15.5 %collective-permute-start.2 = (bf16[256,1536]{1,0:T(8,128)(2,1)}, bf16[256,1536]{1,0:T(8,128)(2,1)S(1)}, u32[]{:S(2)}, u32[]{:S(2)}) collective-permute-start(bf16[256,1536]{1,0:T(8,128)(2,1)} %collective-permute-done.1), channel_id=1, source_target_pairs={{0,1},{1,0},{2,3},{3,2},{4,5},{5,4},{6,7},{7,6},{8,9},{9,8},{10,11... | collective-permute-start | bytes 2359304 | tf_op jit(solution)/shard_map/ppermute | solution.py:124
  57.8 1.4 copy-start.9
  57.9 1.7 %copy-start.23 = (bf16[1,256,1536]{2,1,0:T(8,128)(2,1)S(1)}, bf16[1,256,1536]{2,1,0:T(8,128)(2,1)}, u32[]{:S(2)}) copy-start(bf16[1,256,1536]{2,1,0:T(8,128)(2,1)} %param.6) | copy-start | bytes 2359300
  59.2 3.3 %collective-permute-start.8 = (bf16[384,768]{1,0:T(8,128)(2,1)S(1)}, bf16[384,768]{1,0:T(8,128)(2,1)S(1)}, u32[]{:S(2)}, u32[]{:S(2)}) collective-permute-start(bf16[384,768]{1,0:T(8,128)(2,1)S(1)} %constant_dynamic-slice_fusion.2), channel_id=1, source_target_pairs={{0,1},{1,0},{2,3},{3,2},{4,5},{5,4},{6,7},{7,6},{8,9},{9,8},{10,11... | collective-permute-start | bytes 1769480 | tf_op jit(solution)/shard_map/ppermute | solution.py:124
  60.9 1.8 %copy-start.13 = (bf16[256,1536]{1,0:T(8,128)(2,1)}, bf16[256,1536]{1,0:T(8,128)(2,1)S(1)}, u32[]{:S(2)}) copy-start(bf16[256,1536]{1,0:T(8,128)(2,1)S(1)} %get-tuple-element.75) | copy-start | bytes 2359300
  62.7 0.8 copy-start.17
  62.7 1.8 %copy-start.19 = (bf16[384,768]{1,0:T(8,128)(2,1)}, bf16[384,768]{1,0:T(8,128)(2,1)S(1)}, u32[]{:S(2)}) copy-start(bf16[384,768]{1,0:T(8,128)(2,1)S(1)} %get-tuple-element.73) | copy-start | bytes 1769476
  70.8 2.4 %copy-start.10 = (bf16[4,8,32,1152]{3,2,1,0:T(8,128)(2,1)S(1)}, bf16[4,8,32,1152]{3,2,1,0:T(8,128)(2,1)}, u32[]{:S(2)}) copy-start(bf16[4,8,32,1152]{3,2,1,0:T(8,128)(2,1)} %copy-done.9) | copy-start | bytes 7077892
  73.2 1.2 copy-start.15
  73.2 2.0 %copy-start.16 = (bf16[256,1536]{1,0:T(8,128)(2,1)S(1)}, bf16[256,1536]{1,0:T(8,128)(2,1)}, u32[]{:S(2)}) copy-start(bf16[256,1536]{1,0:T(8,128)(2,1)} %get-tuple-element.77) | copy-start | bytes 2359300
  73.4 5.0 %copy-start.21 = (bf16[8,192,1152]{2,1,0:T(8,128)(2,1)}, bf16[8,192,1152]{2,1,0:T(8,128)(2,1)S(1)}, u32[]{:S(2)}) copy-start(bf16[8,192,1152]{2,1,0:T(8,128)(2,1)S(1)} %fusion.31) | copy-start | bytes 10616836
  83.6 9.7 %copy-start.1 = (f32[512,384]{1,0:T(8,128)}, f32[512,384]{1,0:T(8,128)S(1)}, u32[]{:S(2)}) copy-start(f32[512,384]{1,0:T(8,128)S(1)} %get-tuple-element.52.dv_a) | copy-start | bytes 2359300
  83.6 9.7 %copy-start.5 = (f32[512,384]{1,0:T(8,128)}, f32[512,384]{1,0:T(8,128)S(1)}, u32[]{:S(2)}) copy-start(f32[512,384]{1,0:T(8,128)S(1)} %get-tuple-element.45.dk_a) | copy-start | bytes 2359300
  83.7 14.7 %collective-permute-start.9 = (bf16[256,768]{1,0:T(8,128)(2,1)S(1)}, bf16[256,768]{1,0:T(8,128)(2,1)S(1)}, u32[]{:S(2)}, u32[]{:S(2)}) collective-permute-start(bf16[256,768]{1,0:T(8,128)(2,1)S(1)} %pad_maximum_fusion.15), channel_id=1, source_target_pairs={{2,0},{3,1},{4,2},{5,3},{6,4},{7,5},{8,6},{9,7},{10,8},{11,9},{12,... | collective-permute-start | bytes 1179656 | tf_op jit(solution)/shard_map/ppermute | solution.py:351
  93.0 0.9 copy-start.3
  93.0 10.8 %collective-permute-start.11 = (bf16[512,384]{1,0:T(8,128)(2,1)S(1)}, bf16[512,384]{1,0:T(8,128)(2,1)}, u32[]{:S(2)}, u32[]{:S(2)}) collective-permute-start(bf16[512,384]{1,0:T(8,128)(2,1)S(1)} %constant_dynamic-update-slice_fusion.1), channel_id=1, source_target_pairs={{0,1},{1,0},{2,3},{3,2},{4,5},{5,4},{6,7},{7,6},{8,9},{9,8},{10,11... | collective-permute-start | bytes 1179656 | tf_op jit(solution)/shard_map/ppermute | solution.py:124
  93.3 5.1 %copy-start = (bf16[768,1536]{1,0:T(8,128)(2,1)}, bf16[768,1536]{1,0:T(8,128)(2,1)S(1)}, u32[]{:S(2)}) copy-start(bf16[768,1536]{1,0:T(8,128)(2,1)S(1)} %pad_maximum_fusion.low_ref) | copy-start | bytes 7077892
  98.4 0.8 copy-start.24
  99.1 4.6 %copy-start.14 = (bf16[256,1536]{1,0:T(8,128)(2,1)S(1)}, bf16[256,1536]{1,0:T(8,128)(2,1)}, u32[]{:S(2)}) copy-start(bf16[256,1536]{1,0:T(8,128)(2,1)} %copy-done.13) | copy-start | bytes 2359300
  99.1 41.9 %all-to-all-start.2 = ((bf16[16,96,896]{2,1,0:T(8,128)(2,1)}), bf16[16,96,896]{2,1,0:T(8,128)(2,1)}, u32[]{:S(2)}, u32[]{:S(2)}) async-start(bf16[16,96,896]{2,1,0:T(8,128)(2,1)} %bitcast.90), calls=%async_computation.2 | async-start | bytes 5505024 | tf_op jit(solution)/shard_map/all_to_all | solution.py:254
  103.8 1.3 copy-start.2
  105.1 7.6 %copy-start.18 = (bf16[384,768]{1,0:T(8,128)(2,1)S(1)}, bf16[384,768]{1,0:T(8,128)(2,1)}, u32[]{:S(2)}) copy-start(bf16[384,768]{1,0:T(8,128)(2,1)} %copy-done.17) | copy-start | bytes 1769476
  105.1 7.6 %copy-start.20 = (bf16[384,768]{1,0:T(8,128)(2,1)S(1)}, bf16[384,768]{1,0:T(8,128)(2,1)}, u32[]{:S(2)}) copy-start(bf16[384,768]{1,0:T(8,128)(2,1)} %copy-done.19) | copy-start | bytes 1769476
  110.2 13.1 %collective-permute-start.12 = (bf16[8,2,24,640]{3,2,1,0:T(8,128)(2,1)S(1)}, bf16[8,2,24,640]{3,2,1,0:T(8,128)(2,1)S(1)}, u32[]{:S(2)}, u32[]{:S(2)}) collective-permute-start(bf16[8,2,24,640]{3,2,1,0:T(8,128)(2,1)S(1)} %get-tuple-element.55), channel_id=1, source_target_pairs={{12,0},{13,1},{14,2},{15,3},{0,4},{1,5},{2,6},{3,7},{4,8},{5,9},{6... | collective-permute-start | bytes 1474568 | tf_op jit(solution)/shard_map/ppermute | solution.py:369
  110.8 14.2 %collective-permute-start.13 = (bf16[8,2,24,640]{3,2,1,0:T(8,128)(2,1)S(1)}, bf16[8,2,24,640]{3,2,1,0:T(8,128)(2,1)S(1)}, u32[]{:S(2)}, u32[]{:S(2)}) collective-permute-start(bf16[8,2,24,640]{3,2,1,0:T(8,128)(2,1)S(1)} %get-tuple-element.56), channel_id=1, source_target_pairs={{8,0},{9,1},{10,2},{11,3},{12,4},{13,5},{14,6},{15,7},{0,8},{1,9},... | collective-permute-start | bytes 1474568 | tf_op jit(solution)/shard_map/ppermute | solution.py:369
  111.7 2.8 %copy-start.4 = (f32[512,384]{1,0:T(8,128)S(1)}, f32[512,384]{1,0:T(8,128)}, u32[]{:S(2)}) copy-start(f32[512,384]{1,0:T(8,128)} %copy-done.3) | copy-start | bytes 2359300
  111.7 2.8 %copy-start.6 = (f32[512,384]{1,0:T(8,128)S(1)}, f32[512,384]{1,0:T(8,128)}, u32[]{:S(2)}) copy-start(f32[512,384]{1,0:T(8,128)} %copy-done.5) | copy-start | bytes 2359300
  111.7 23.1 %collective-permute-start.14 = (bf16[8,2,24,640]{3,2,1,0:T(8,128)(2,1)S(1)}, bf16[8,2,24,640]{3,2,1,0:T(8,128)(2,1)S(1)}, u32[]{:S(2)}, u32[]{:S(2)}) collective-permute-start(bf16[8,2,24,640]{3,2,1,0:T(8,128)(2,1)S(1)} %get-tuple-element.57), channel_id=1, source_target_pairs={{4,0},{5,1},{6,2},{7,3},{8,4},{9,5},{10,6},{11,7},{12,8},{13,9},{1... | collective-permute-start | bytes 1474568 | tf_op jit(solution)/shard_map/ppermute | solution.py:369
  113.8 22.0 %collective-permute-start.10 = (bf16[256,1536]{1,0:T(8,128)(2,1)S(1)}, bf16[256,1536]{1,0:T(8,128)(2,1)S(1)}, u32[]{:S(2)}, u32[]{:S(2)}) collective-permute-start(bf16[256,1536]{1,0:T(8,128)(2,1)S(1)} %dynamic-slice_convert_fusion.1), channel_id=1, source_target_pairs={{0,1},{1,0},{2,3},{3,2},{4,5},{5,4},{6,7},{7,6},{8,9},{9,8},{10,11... | collective-permute-start | bytes 2359304 | tf_op jit(solution)/shard_map/ppermute | solution.py:124
  136.8 15.1 %copy-start.25 = (bf16[256,768]{1,0:T(8,128)(2,1)S(1)}, bf16[256,768]{1,0:T(8,128)(2,1)}, u32[]{:S(2)}) copy-start(bf16[256,768]{1,0:T(8,128)(2,1)} %copy-done.24) | copy-start | bytes 1179652
  141.1 16.6 %all-to-all-start.3 = ((bf16[16,24,640]{2,1,0:T(8,128)(2,1)}), bf16[16,24,640]{2,1,0:T(8,128)(2,1)S(1)}, u32[]{:S(2)}, u32[]{:S(2)}) async-start(bf16[16,24,640]{2,1,0:T(8,128)(2,1)} %bitcast.27), calls=%async_computation.3 | async-start | bytes 983040 | tf_op jit(solution)/shard_map/all_to_all | solution.py:254
  147.7 4.3 %copy-start.22 = (bf16[8,192,1152]{2,1,0:T(8,128)(2,1)S(1)}, bf16[8,192,1152]{2,1,0:T(8,128)(2,1)}, u32[]{:S(2)}) copy-start(bf16[8,192,1152]{2,1,0:T(8,128)(2,1)} %copy-done.21) | copy-start | bytes 10616836
  150.1 7.5 %collective-permute-start.16 = (f32[24,896]{1,0:T(8,128)S(1)}, f32[24,896]{1,0:T(8,128)S(1)}, u32[]{:S(2)}, u32[]{:S(2)}) collective-permute-start(f32[24,896]{1,0:T(8,128)S(1)} %get-tuple-element.86), channel_id=1, source_target_pairs={{12,0},{13,1},{14,2},{15,3},{0,4},{1,5},{2,6},{3,7},{4,8},{5,9},{6... | collective-permute-start | bytes 258056 | tf_op jit(solution)/shard_map/ppermute | solution.py:378
  150.7 7.0 %collective-permute-start.18 = (f32[24,896]{1,0:T(8,128)S(1)}, f32[24,896]{1,0:T(8,128)S(1)}, u32[]{:S(2)}, u32[]{:S(2)}) collective-permute-start(f32[24,896]{1,0:T(8,128)S(1)} %get-tuple-element.87), channel_id=1, source_target_pairs={{4,0},{5,1},{6,2},{7,3},{8,4},{9,5},{10,6},{11,7},{12,8},{13,9},{1... | collective-permute-start | bytes 258056 | tf_op jit(solution)/shard_map/ppermute | solution.py:378
  151.7 6.0 %collective-permute-start.17 = (f32[24,896]{1,0:T(8,128)S(1)}, f32[24,896]{1,0:T(8,128)S(1)}, u32[]{:S(2)}, u32[]{:S(2)}) collective-permute-start(f32[24,896]{1,0:T(8,128)S(1)} %get-tuple-element.88), channel_id=1, source_target_pairs={{8,0},{9,1},{10,2},{11,3},{12,4},{13,5},{14,6},{15,7},{0,8},{1,9},... | collective-permute-start | bytes 258056 | tf_op jit(solution)/shard_map/ppermute | solution.py:378
  154.3 1.6 copy-start.11
  155.9 6.0 %copy-start.8 = (bf16[1,256,1536]{2,1,0:T(8,128)(2,1)S(1)}, bf16[1,256,1536]{2,1,0:T(8,128)(2,1)}, u32[]{:S(2)}) copy-start(bf16[1,256,1536]{2,1,0:T(8,128)(2,1)} %param.5) | copy-start | bytes 2359300
  156.0 5.9 %collective-permute-start.15 = (bf16[256,1536]{1,0:T(8,128)(2,1)S(1)}, bf16[256,1536]{1,0:T(8,128)(2,1)S(1)}, u32[]{:S(2)}, u32[]{:S(2)}) collective-permute-start(bf16[256,1536]{1,0:T(8,128)(2,1)S(1)} %dynamic-slice_convert_fusion), channel_id=1, source_target_pairs={{0,1},{1,0},{2,3},{3,2},{4,5},{5,4},{6,7},{7,6},{8,9},{9,8},{10,11... | collective-permute-start | bytes 2359304 | tf_op jit(solution)/shard_map/ppermute | solution.py:124
  157.8 2.5 %collective-permute-start.20 = (f32[6,768]{1,0:T(8,128)S(1)}, f32[6,768]{1,0:T(8,128)S(1)}, u32[]{:S(2)}, u32[]{:S(2)}) collective-permute-start(f32[6,768]{1,0:T(8,128)S(1)} %fusion.41), channel_id=1, source_target_pairs={{0,1},{1,0},{2,3},{3,2},{4,5},{5,4},{6,7},{7,6},{8,9},{9,8},{10,11... | collective-permute-start | bytes 55304 | tf_op jit(solution)/shard_map/ppermute | solution.py:124
  159.5 1.5 collective-permute-start.19
  161.1 2.9 %copy-start.12 = (f32[512,1536]{1,0:T(8,128)S(1)}, f32[512,1536]{1,0:T(8,128)}, u32[]{:S(2)}) copy-start(f32[512,1536]{1,0:T(8,128)} %copy-done.11) | copy-start | bytes 9437188

commit v4 on v3

--- a/solution.py
+++ b/solution.py
@@ -278,7 +278,10 @@
         return in_order(lower, own, swap(own), 0)
 
     y = lax.axis_index("y")
-    mine = own_half(core, w_qkv.reshape(-1, 3, inner), width, axis=2).reshape(-1, 3 * width)
+    mine = jnp.concatenate(
+        [own_half(core, w_qkv[:, k * inner : (k + 1) * inner], width, axis=1) for k in range(3)],
+        axis=1,
+    )
     out_mine = own_half(core, w_out, out_cols, axis=1)
     deep = mine.shape[0]
     direct = deep * 2 // 3

time: 169 us -> 165 us (0.976)
  waiting for transfers between devices: 55.3 us -> 52 us
    dynamic_update_slice x4, local copies, waits for them, and re-layouts: 0.29 us -> 3.48 us  [body(): lax.dynamic_update_index_in_dim(quarters, got, (y + k) % ROWS_Y, 0)]
    all_to_all x2, waiting for transfers between devices: 10.1 us -> 7.09 us  [gather(): return lax.all_to_all(shards, ('z', 'xl'), 0, 0, tiled=True)]
    unnamed x62 -> x60, local copies, waits for them, and re-layouts: 10.1 us -> 7.74 us
    reshape x2 -> x0, local copies, waits for them, and re-layouts: 2.31 us -> none  [the longest x1 2.18 us: body(): w_qkv.reshape(-1, 3, inner)]
  transfers between devices with their start and end apart: 25 -> 25, of which waited for: 10 -> 10; matrix products, arithmetic and copies ran while one was open for 13% -> 15% of each run, Pallas kernels for 9% -> 9%
where the time goes in v4:
time: 165 us; the launch traced here: 162 us
  waiting for transfers between devices  52 us (32%)
  starting transfers between devices  45.7 us (28%)
  Pallas kernels  19.8 us (12%)
  other arithmetic  18 us (11%)
  local copies, waits for them, and re-layouts  17.6 us (11%)
  matrix products  7.4 us (4%)
    ppermute x3, waiting for transfers between devices, body(): summed = summed + lax.ppermute(first[k], ALL, from_y(-k)).astype(F32)  20.6 us
    ppermute x3, waiting for transfers between devices, body(): got = quarter if k == 0 else lax.ppermute(quarter, ALL, from_y(k))  11.5 us
    all_to_all x2, starting transfers between devices, scatter(): return lax.all_to_all(chunks, ('z', 'xl', 'xh'), 0, 0, tiled=True)  11.2 us
    all_to_all x2, starting transfers between devices, gather(): return lax.all_to_all(shards, ('z', 'xl'), 0, 0, tiled=True)  10.6 us
    pallas_call x2, Pallas kernels, attention(): pl.pallas_call(functools.partial(attend, first), in_specs=[whole] * 4, ou...  10.2 us
    ppermute x1, waiting for transfers between devices, body(): past = lax.ppermute(own_low, ALL, ONWARD)  8.45 us
    unnamed x60, local copies, waits for them, and re-layouts  7.74 us
    all_to_all x2, waiting for transfers between devices, gather(): return lax.all_to_all(shards, ('z', 'xl'), 0, 0, tiled=True)  7.09 us
  transfers between devices with their start and end apart: 25, of which 10 were waited for; matrix products, arithmetic and copies ran while one was open for 15% of the time, Pallas kernels for 9%

profile of v4, /device:TPU:9, one launch (start us, length us, event | category | flops | bytes accessed | tf_op | source)
XLA Modules:
  0.0 162.1 jit_solution(13700288987876612338)
XLA Ops:
  0.6 0.9 constant_dynamic-slice_fusion
  1.6 1.3 fusion.55
  2.8 0.8 fusion.59
  3.8 0.9 broadcast_in_dim.43
  4.8 0.3 fusion.15
  5.2 0.3 fusion.7
  5.5 0.8 collective-permute-start
  6.4 6.0 %all-to-all-start = ((bf16[8,32,1152]{2,1,0:T(8,128)(2,1)}), bf16[8,32,1152]{2,1,0:T(8,128)(2,1)S(1)}, u32[]{:S(2)}, u32[]{:S(2)}) async-start(bf16[8,32,1152]{2,1,0:T(8,128)(2,1)} %broadcast_in_dim.43), calls=%async_computation | async-start | bytes 1179648 | tf_op jit(solution)/shard_map/all_to_all | solution.py:262
  12.3 0.7 collective-permute-start.7
  13.2 4.3 %collective-permute-start.1 = (bf16[256,1536]{1,0:T(8,128)(2,1)S(1)}, bf16[256,1536]{1,0:T(8,128)(2,1)}, u32[]{:S(2)}, u32[]{:S(2)}) collective-permute-start(bf16[256,1536]{1,0:T(8,128)(2,1)S(1)} %fusion.7), channel_id=1, source_target_pairs={{1,3},{3,5},{5,7},{7,9},{9,11},{11,13},{13,15},{17,19},{19,21},{21... | collective-permute-start | bytes 2359304 | tf_op jit(solution)/shard_map/ppermute | solution.py:308
  17.8 2.1 %broadcast_select_fusion.3 = (bf16[256,1536]{1,0:T(8,128)(2,1)S(1)}, bf16[256,1536]{1,0:T(8,128)(2,1)}) fusion(bf16[256,1536]{1,0:T(8,128)(2,1)S(1)} %fusion.7, bf16[256,1536]{1,0:T(8,128)(2,1)} %collective-permute-done, pred[]{:T(512)S(6)} %eq.11), kind=kLoop, calls=%fused_computation.56 | loop fusion | flops 786432 | bytes 3145729 | tf_op jit(solution)/shard_map/jit(_where)/select_n | solution.py:249
  19.9 2.3 %all-to-all-done = bf16[8,32,1152]{2,1,0:T(8,128)(2,1)S(1)} async-done(((bf16[8,32,1152]{2,1,0:T(8,128)(2,1)}), bf16[8,32,1152]{2,1,0:T(8,128)(2,1)S(1)}, u32[]{:S(2)}, u32[]{:S(2)}) %all-to-all-start) | async-done | bytes 589856 | tf_op jit(solution)/shard_map/all_to_all | solution.py:262
  22.2 8.5 %collective-permute-done.1 = bf16[256,1536]{1,0:T(8,128)(2,1)} collective-permute-done((bf16[256,1536]{1,0:T(8,128)(2,1)S(1)}, bf16[256,1536]{1,0:T(8,128)(2,1)}, u32[]{:S(2)}, u32[]{:S(2)}) %collective-permute-start.1) | collective-permute-done | bytes 786464 | tf_op jit(solution)/shard_map/ppermute | solution.py:308
  30.7 1.7 %broadcast_in_dim.41 = bf16[8,128,1152]{2,1,0:T(8,128)(2,1)} broadcast(bf16[128,1152]{1,0:T(8,128)(2,1)S(1)} %slice.159), dimensions={1,2} | broadcast | bytes 2654208 | tf_op jit(solution)/shard_map/broadcast_in_dim | solution.py:258
  32.4 1.5 broadcast_select_fusion.1
  33.9 1.5 collective-permute-start.6
  35.4 3.5 %collective-permute-start.5 = (bf16[8,32,1152]{2,1,0:T(8,128)(2,1)S(1)}, bf16[8,32,1152]{2,1,0:T(8,128)(2,1)}, u32[]{:S(2)}, u32[]{:S(2)}) collective-permute-start(bf16[8,32,1152]{2,1,0:T(8,128)(2,1)S(1)} %all-to-all-done), channel_id=1, source_target_pairs={{8,0},{9,1},{10,2},{11,3},{12,4},{13,5},{14,6},{15,7},{0,8},{1,9},... | collective-permute-start | bytes 1769480 | tf_op jit(solution)/shard_map/ppermute | solution.py:314
  38.9 4.6 %all-to-all-start.1 = ((bf16[8,128,1152]{2,1,0:T(8,128)(2,1)}), bf16[8,128,1152]{2,1,0:T(8,128)(2,1)}, u32[]{:S(2)}, u32[]{:S(2)}) async-start(bf16[8,128,1152]{2,1,0:T(8,128)(2,1)} %broadcast_in_dim.41), calls=%async_computation.1 | async-start | bytes 4718592 | tf_op jit(solution)/shard_map/all_to_all | solution.py:262
  43.8 3.0 %collective-permute-done.4 = bf16[8,32,1152]{2,1,0:T(8,128)(2,1)} collective-permute-done((bf16[8,32,1152]{2,1,0:T(8,128)(2,1)S(1)}, bf16[8,32,1152]{2,1,0:T(8,128)(2,1)}, u32[]{:S(2)}, u32[]{:S(2)}) %collective-permute-start.4) | collective-permute-done | bytes 589856 | tf_op jit(solution)/shard_map/ppermute | solution.py:314
  46.9 1.1 bitcast_dynamic-update-slice_fusion.2
  48.0 8.5 %collective-permute-done.5 = bf16[8,32,1152]{2,1,0:T(8,128)(2,1)} collective-permute-done((bf16[8,32,1152]{2,1,0:T(8,128)(2,1)S(1)}, bf16[8,32,1152]{2,1,0:T(8,128)(2,1)}, u32[]{:S(2)}, u32[]{:S(2)}) %collective-permute-start.5) | collective-permute-done | bytes 589856 | tf_op jit(solution)/shard_map/ppermute | solution.py:314
  56.5 1.1 bitcast_dynamic-update-slice_fusion.1
  57.6 1.1 bitcast_dynamic-update-slice_fusion
  59.0 1.2 copy-done.10
  60.5 1.0 fusion.28.up_ref
  61.5 1.3 broadcast_select_fusion.4
  63.1 1.0 fusion.16
  64.2 4.7 %all-to-all-done.1 = bf16[8,128,1152]{2,1,0:T(8,128)(2,1)} async-done(((bf16[8,128,1152]{2,1,0:T(8,128)(2,1)}), bf16[8,128,1152]{2,1,0:T(8,128)(2,1)}, u32[]{:S(2)}, u32[]{:S(2)}) %all-to-all-start.1) | async-done | bytes 2359328 | tf_op jit(solution)/shard_map/all_to_all | solution.py:262
  68.9 2.0 %constant_dynamic-update-slice_fusion = bf16[8,192,1152]{2,1,0:T(8,128)(2,1)S(1)} fusion(bf16[8,128,1152]{2,1,0:T(8,128)(2,1)} %all-to-all-done.1), kind=kLoop, calls=%fused_computation.115 | loop fusion | bytes 4718592
  71.0 0.3 copy-done.11
  71.5 1.0 copy-done.16
  72.5 3.2 %convolution_convert_fusion.proj_ref = bf16[768,1152]{1,0:T(8,128)(2,1)S(1)} fusion(bf16[1536,1152]{1,0:T(8,128)(2,1)S(1)} %bitcast.93, bf16[256,1536]{1,0:T(8,128)(2,1)S(1)} %copy-done.16, bf16[256,1536]{1,0:T(8,128)(2,1)S(1)} %get-tuple-element.76, bf16[256,1536]{1,0:T(8,128)(2,1)S(1)} %broadcast_select_fusion.4), kind=kOutput, calls=%fused_computation.1 | convolution fusion | flops 2725871616 | bytes 7667712 | tf_op jit(solution)/shard_map/dot_general | solution.py:32
  75.7 5.1 %attend.2 = (bf16[256,384]{1,0:T(8,128)(2,1)S(1)}, bf16[256,384]{1,0:T(8,128)(2,1)S(1)}, f32[512,384]{1,0:T(8,128)S(1)}, f32[512,384]{1,0:T(8,128)S(1)}) custom-call(s32[4,128]{1,0:T(4,128)S(1)} %get-tuple-element.103.lo_ref, s32[4,128]{1,0:T(4,128)S(1)} %get-tuple-element.101.hi_ref, bf16[768,1152]{1,0:T(8,128)(2,1)S(1)} %convolution_convert_fusion.proj_ref, ...), custom_call_target="tpu_custom_call" | custom-call | tf_op jit(solution)/shard_map/attend/pallas_call | solution.py:82
  81.0 4.2 %collective-permute-start.9 = (bf16[256,768]{1,0:T(8,128)(2,1)S(1)}, bf16[256,768]{1,0:T(8,128)(2,1)S(1)}, u32[]{:S(2)}, u32[]{:S(2)}) collective-permute-start(bf16[256,768]{1,0:T(8,128)(2,1)S(1)} %pad_maximum_fusion.16), channel_id=1, source_target_pairs={{2,0},{3,1},{4,2},{5,3},{6,4},{7,5},{8,6},{9,7},{10,8},{11,9},{12,... | collective-permute-start | bytes 1179656 | tf_op jit(solution)/shard_map/ppermute | solution.py:354
  85.2 5.1 %attend.3 = (bf16[256,384]{1,0:T(8,128)(2,1)S(1)}, bf16[256,384]{1,0:T(8,128)(2,1)S(1)}, f32[512,384]{1,0:T(8,128)S(1)}, f32[512,384]{1,0:T(8,128)S(1)}) custom-call(s32[4,128]{1,0:T(4,128)S(1)} %get-tuple-element.102.lo_ref, s32[4,128]{1,0:T(4,128)S(1)} %get-tuple-element.100.hi_ref, bf16[768,1152]{1,0:T(8,128)(2,1)S(1)} %convolution_convert_fusion.proj_ref, ...), custom_call_target="tpu_custom_call" | custom-call | tf_op jit(solution)/shard_map/attend/pallas_call | solution.py:82
  90.7 0.5 copy-done.3
  91.2 4.5 %late_gradients.1 = bf16[8,2,4,24,896]{4,3,2,1,0:T(8,128)(2,1)} custom-call(bf16[768,1536]{1,0:T(8,128)(2,1)S(1)} %pad_maximum_fusion.low_ref, bf16[256,384]{1,0:T(8,128)(2,1)S(1)} %get-tuple-element.43.dq_a, bf16[256,384]{1,0:T(8,128)(2,1)S(1)} %get-tuple-element.61.dq_b, f32[512,384]{1,0:T(8,128)S(1)} %get-tuple-element.45.dk_a, ...), custom_call_target="tpu_custom_call" | custom-call | tf_op jit(solution)/shard_map/late_gradients/pallas_call | solution.py:194
  95.8 4.6 %all-to-all-start.2 = ((bf16[16,96,896]{2,1,0:T(8,128)(2,1)}), bf16[16,96,896]{2,1,0:T(8,128)(2,1)}, u32[]{:S(2)}, u32[]{:S(2)}) async-start(bf16[16,96,896]{2,1,0:T(8,128)(2,1)} %bitcast.90), calls=%async_computation.2 | async-start | bytes 5505024 | tf_op jit(solution)/shard_map/all_to_all | solution.py:254
  100.5 1.2 broadcast_select_fusion.8
  101.9 5.1 %first_gradients.1 = (bf16[8,2,24,640]{3,2,1,0:T(8,128)(2,1)S(1)}, bf16[8,2,24,640]{3,2,1,0:T(8,128)(2,1)S(1)}, bf16[8,2,24,640]{3,2,1,0:T(8,128)(2,1)S(1)}, bf16[8,2,24,640]{3,2,1,0:T(8,128)(2,1)S(1)}) custom-call(s32[1]{0:T(128)} %bitcast.26.y_ref, bf16[512,768]{1,0:T(8,128)(2,1)S(1)} %pad_maximum_fusion.10.ctx_ref, bf16[512,768]{1,0:T(8,128)(2,1)S(1)} %copy-done.5, ...), custom_call_target="tpu_custom_call" | custom-call | tf_op jit(solution)/shard_map/first_gradients/pallas_call | solution.py:215
  107.0 0.6 collective-permute-start.12
  107.6 1.2 collective-permute-start.13
  108.7 0.7 collective-permute-start.14
  109.5 1.0 fusion.29
  110.5 0.7 collective-permute-start.10
  111.4 8.6 %collective-permute-done.12 = bf16[8,2,24,640]{3,2,1,0:T(8,128)(2,1)S(1)} collective-permute-done((bf16[8,2,24,640]{3,2,1,0:T(8,128)(2,1)S(1)}, bf16[8,2,24,640]{3,2,1,0:T(8,128)(2,1)S(1)}, u32[]{:S(2)}, u32[]{:S(2)}) %collective-permute-start.12) | collective-permute-done | bytes 491552 | tf_op jit(solution)/shard_map/ppermute | solution.py:372
  120.1 1.7 %collective-permute-done.13 = bf16[8,2,24,640]{3,2,1,0:T(8,128)(2,1)S(1)} collective-permute-done((bf16[8,2,24,640]{3,2,1,0:T(8,128)(2,1)S(1)}, bf16[8,2,24,640]{3,2,1,0:T(8,128)(2,1)S(1)}, u32[]{:S(2)}, u32[]{:S(2)}) %collective-permute-start.13) | collective-permute-done | bytes 491552 | tf_op jit(solution)/shard_map/ppermute | solution.py:372
  121.8 10.3 %collective-permute-done.14 = bf16[8,2,24,640]{3,2,1,0:T(8,128)(2,1)S(1)} collective-permute-done((bf16[8,2,24,640]{3,2,1,0:T(8,128)(2,1)S(1)}, bf16[8,2,24,640]{3,2,1,0:T(8,128)(2,1)S(1)}, u32[]{:S(2)}, u32[]{:S(2)}) %collective-permute-start.14) | collective-permute-done | bytes 491552 | tf_op jit(solution)/shard_map/ppermute | solution.py:372
  132.1 1.0 add_convert_fusion.1
  133.1 1.1 fusion.26
  134.2 3.5 %all-to-all-done.2 = bf16[16,96,896]{2,1,0:T(8,128)(2,1)} async-done(((bf16[16,96,896]{2,1,0:T(8,128)(2,1)}), bf16[16,96,896]{2,1,0:T(8,128)(2,1)}, u32[]{:S(2)}, u32[]{:S(2)}) %all-to-all-start.2) | async-done | bytes 2752544 | tf_op jit(solution)/shard_map/all_to_all | solution.py:254
  137.7 6.6 %all-to-all-start.3 = ((bf16[16,24,640]{2,1,0:T(8,128)(2,1)}), bf16[16,24,640]{2,1,0:T(8,128)(2,1)S(1)}, u32[]{:S(2)}, u32[]{:S(2)}) async-start(bf16[16,24,640]{2,1,0:T(8,128)(2,1)} %bitcast.27), calls=%async_computation.3 | async-start | bytes 983040 | tf_op jit(solution)/shard_map/all_to_all | solution.py:254
  144.3 2.4 %convert_reduce_fusion = f32[96,896]{1,0:T(8,128)S(1)} fusion(bf16[16,96,896]{2,1,0:T(8,128)(2,1)} %all-to-all-done.2), kind=kLoop, calls=%fused_computation | loop fusion | flops 2666496 | bytes 3096576 | tf_op jit(solution)/shard_map/reduce_sum | solution.py:377
  146.7 0.6 collective-permute-start.16
  147.3 1.0 collective-permute-start.18
  148.6 2.2 %fusion.20 = f32[512,1536]{1,0:T(8,128)S(1)} fusion(bf16[1536,1152]{1,0:T(8,128)(2,1)S(1)} %bitcast.94, bf16[256,768]{1,0:T(8,128)(2,1)S(1)} %add_convert_fusion.2, bf16[256,384]{1,0:T(8,128)(2,1)S(1)} %get-tuple-element.61.dq_b, bf16[256,1152]{1,0:T(8,128)(2,1)S(1)} %pad_maximum_fusion.14), kind=kOutput, calls=%fused_computation.39 | convolution fusion | flops 1815478272 | bytes 7864320 | tf_op jit(solution)/shard_map/dot_general | solution.py:24
  150.9 1.6 %copy-done.12 = f32[512,1536]{1,0:T(8,128)} copy-done((f32[512,1536]{1,0:T(8,128)}, f32[512,1536]{1,0:T(8,128)S(1)}, u32[]{:S(2)}) %copy-start.12) | copy-done | bytes 3145752
  152.6 1.7 %collective-permute-start.15 = (bf16[256,1536]{1,0:T(8,128)(2,1)S(1)}, bf16[256,1536]{1,0:T(8,128)(2,1)S(1)}, u32[]{:S(2)}, u32[]{:S(2)}) collective-permute-start(bf16[256,1536]{1,0:T(8,128)(2,1)S(1)} %dynamic-slice_convert_fusion), channel_id=1, source_target_pairs={{0,1},{1,0},{2,3},{3,2},{4,5},{5,4},{6,7},{7,6},{8,9},{9,8},{10,11... | collective-permute-start | bytes 2359304 | tf_op jit(solution)/shard_map/ppermute | solution.py:124
  154.4 1.6 %collective-permute-start.20 = (f32[6,768]{1,0:T(8,128)S(1)}, f32[6,768]{1,0:T(8,128)S(1)}, u32[]{:S(2)}, u32[]{:S(2)}) collective-permute-start(f32[6,768]{1,0:T(8,128)S(1)} %fusion.41), channel_id=1, source_target_pairs={{0,1},{1,0},{2,3},{3,2},{4,5},{5,4},{6,7},{7,6},{8,9},{9,8},{10,11... | collective-permute-start | bytes 55304 | tf_op jit(solution)/shard_map/ppermute | solution.py:124
  156.2 0.7 collective-permute-done.20
  156.9 0.6 pad_maximum_fusion.19
  157.8 0.7 copy.10
  158.5 2.1 %fusion.30 = (f32[256]{0:T(256)S(1)}, f32[256]{0:T(256)S(1)}) fusion(bf16[256,1536]{1,0:T(8,128)(2,1)S(1)} %collective-permute-done.15, f32[512,1536]{1,0:T(8,128)} %copy-done.12, s32[]{:T(128)S(6)} %select_n.194, f32[256]{0:T(256)S(1)} %add_rsqrt_fusion, f32[256]{0:T(256)S(1)} %broadcast_multiply_fusion.2, bf16[256,1536]{1,0:T(8,128)(2,1)S(1)} %bitcast.88), kind=kLoop, calls=%fused_computation.67 | loop fusion | flops 3145216 | bytes 3149828 | tf_op jit(solution)/shard_map/reduce_sum | solution.py:412
  160.6 1.5 fusion.27
  (126 shorter events, 4.0 us)
Async XLA Ops:
  1.5 3.1 %copy-start.8 = (bf16[1,256,1536]{2,1,0:T(8,128)(2,1)S(1)}, bf16[1,256,1536]{2,1,0:T(8,128)(2,1)}, u32[]{:S(2)}) copy-start(bf16[1,256,1536]{2,1,0:T(8,128)(2,1)} %param.5) | copy-start | bytes 2359300
  3.7 2.6 %copy-start.25 = (s32[2,1,256]{2,1,0:T(1,128)S(1)}, s32[2,1,256]{2,1,0:T(1,128)}, u32[]{:S(2)}) copy-start(s32[2,1,256]{2,1,0:T(1,128)} %param.7) | copy-start | bytes 6148
  5.5 7.8 %collective-permute-start = (bf16[256,1536]{1,0:T(8,128)(2,1)S(1)}, bf16[256,1536]{1,0:T(8,128)(2,1)}, u32[]{:S(2)}, u32[]{:S(2)}) collective-permute-start(bf16[256,1536]{1,0:T(8,128)(2,1)S(1)} %fusion.7), channel_id=1, source_target_pairs={{0,1},{1,0},{2,3},{3,2},{4,5},{5,4},{6,7},{7,6},{8,9},{9,8},{10,11... | collective-permute-start | bytes 2359304 | tf_op jit(solution)/shard_map/ppermute | solution.py:124
  6.3 6.9 %collective-permute-start.3 = (s32[256,2]{0,1:T(2,128)S(1)}, s32[256,2]{0,1:T(2,128)S(1)}, u32[]{:S(2)}, u32[]{:S(2)}) collective-permute-start(s32[256,2]{0,1:T(2,128)S(1)} %bitcast.101), channel_id=1, source_target_pairs={{0,1},{1,0},{2,3},{3,2},{4,5},{5,4},{6,7},{7,6},{8,9},{9,8},{10,11... | collective-permute-start | bytes 6152 | tf_op jit(solution)/shard_map/ppermute | solution.py:124
  6.4 15.9 %all-to-all-start = ((bf16[8,32,1152]{2,1,0:T(8,128)(2,1)}), bf16[8,32,1152]{2,1,0:T(8,128)(2,1)S(1)}, u32[]{:S(2)}, u32[]{:S(2)}) async-start(bf16[8,32,1152]{2,1,0:T(8,128)(2,1)} %broadcast_in_dim.43), calls=%async_computation | async-start | bytes 1179648 | tf_op jit(solution)/shard_map/all_to_all | solution.py:262
  12.3 20.0 %collective-permute-start.7 = (bf16[256,1536]{1,0:T(8,128)(2,1)}, bf16[256,1536]{1,0:T(8,128)(2,1)}, u32[]{:S(2)}, u32[]{:S(2)}) collective-permute-start(bf16[256,1536]{1,0:T(8,128)(2,1)} %bitcast.1), channel_id=1, source_target_pairs={{0,1},{1,0},{2,3},{3,2},{4,5},{5,4},{6,7},{7,6},{8,9},{9,8},{10,11... | collective-permute-start | bytes 2359304 | tf_op jit(solution)/shard_map/ppermute | solution.py:124
  13.2 17.4 %collective-permute-start.1 = (bf16[256,1536]{1,0:T(8,128)(2,1)S(1)}, bf16[256,1536]{1,0:T(8,128)(2,1)}, u32[]{:S(2)}, u32[]{:S(2)}) collective-permute-start(bf16[256,1536]{1,0:T(8,128)(2,1)S(1)} %fusion.7), channel_id=1, source_target_pairs={{1,3},{3,5},{5,7},{7,9},{9,11},{11,13},{13,15},{17,19},{19,21},{21... | collective-permute-start | bytes 2359304 | tf_op jit(solution)/shard_map/ppermute | solution.py:308
  19.9 51.6 %copy-start.14 = (bf16[256,1536]{1,0:T(8,128)(2,1)}, bf16[256,1536]{1,0:T(8,128)(2,1)S(1)}, u32[]{:S(2)}) copy-start(bf16[256,1536]{1,0:T(8,128)(2,1)S(1)} %get-tuple-element.76) | copy-start | bytes 2359300
  32.4 14.5 %collective-permute-start.4 = (bf16[8,32,1152]{2,1,0:T(8,128)(2,1)S(1)}, bf16[8,32,1152]{2,1,0:T(8,128)(2,1)}, u32[]{:S(2)}, u32[]{:S(2)}) collective-permute-start(bf16[8,32,1152]{2,1,0:T(8,128)(2,1)S(1)} %all-to-all-done), channel_id=1, source_target_pairs={{4,0},{5,1},{6,2},{7,3},{8,4},{9,5},{10,6},{11,7},{12,8},{13,9},{1... | collective-permute-start | bytes 1769480 | tf_op jit(solution)/shard_map/ppermute | solution.py:314
  33.8 26.7 %copy-start.17 = (bf16[256,1536]{1,0:T(8,128)(2,1)}, bf16[256,1536]{1,0:T(8,128)(2,1)S(1)}, u32[]{:S(2)}) copy-start(bf16[256,1536]{1,0:T(8,128)(2,1)S(1)} %get-tuple-element.75) | copy-start | bytes 2359300
  33.9 23.8 %collective-permute-start.6 = (bf16[8,32,1152]{2,1,0:T(8,128)(2,1)S(1)}, bf16[8,32,1152]{2,1,0:T(8,128)(2,1)}, u32[]{:S(2)}, u32[]{:S(2)}) collective-permute-start(bf16[8,32,1152]{2,1,0:T(8,128)(2,1)S(1)} %all-to-all-done), channel_id=1, source_target_pairs={{12,0},{13,1},{14,2},{15,3},{0,4},{1,5},{2,6},{3,7},{4,8},{5,9},{6... | collective-permute-start | bytes 1769480 | tf_op jit(solution)/shard_map/ppermute | solution.py:314
  35.4 21.1 %collective-permute-start.5 = (bf16[8,32,1152]{2,1,0:T(8,128)(2,1)S(1)}, bf16[8,32,1152]{2,1,0:T(8,128)(2,1)}, u32[]{:S(2)}, u32[]{:S(2)}) collective-permute-start(bf16[8,32,1152]{2,1,0:T(8,128)(2,1)S(1)} %all-to-all-done), channel_id=1, source_target_pairs={{8,0},{9,1},{10,2},{11,3},{12,4},{13,5},{14,6},{15,7},{0,8},{1,9},... | collective-permute-start | bytes 1769480 | tf_op jit(solution)/shard_map/ppermute | solution.py:314
  38.9 30.0 %all-to-all-start.1 = ((bf16[8,128,1152]{2,1,0:T(8,128)(2,1)}), bf16[8,128,1152]{2,1,0:T(8,128)(2,1)}, u32[]{:S(2)}, u32[]{:S(2)}) async-start(bf16[8,128,1152]{2,1,0:T(8,128)(2,1)} %broadcast_in_dim.41), calls=%async_computation.1 | async-start | bytes 4718592 | tf_op jit(solution)/shard_map/all_to_all | solution.py:262
  43.6 17.9 %collective-permute-start.2 = (bf16[256,1536]{1,0:T(8,128)(2,1)}, bf16[256,1536]{1,0:T(8,128)(2,1)S(1)}, u32[]{:S(2)}, u32[]{:S(2)}) collective-permute-start(bf16[256,1536]{1,0:T(8,128)(2,1)} %collective-permute-done.1), channel_id=1, source_target_pairs={{0,1},{1,0},{2,3},{3,2},{4,5},{5,4},{6,7},{7,6},{8,9},{9,8},{10,11... | collective-permute-start | bytes 2359304 | tf_op jit(solution)/shard_map/ppermute | solution.py:124
  58.8 1.4 copy-start.10
  60.2 2.6 %collective-permute-start.8 = (bf16[384,768]{1,0:T(8,128)(2,1)S(1)}, bf16[384,768]{1,0:T(8,128)(2,1)S(1)}, u32[]{:S(2)}, u32[]{:S(2)}) collective-permute-start(bf16[384,768]{1,0:T(8,128)(2,1)S(1)} %constant_dynamic-slice_fusion.1), channel_id=1, source_target_pairs={{0,1},{1,0},{2,3},{3,2},{4,5},{5,4},{6,7},{7,6},{8,9},{9,8},{10,11... | collective-permute-start | bytes 1769480 | tf_op jit(solution)/shard_map/ppermute | solution.py:124
  61.5 1.6 %copy-start.18 = (bf16[256,1536]{1,0:T(8,128)(2,1)S(1)}, bf16[256,1536]{1,0:T(8,128)(2,1)}, u32[]{:S(2)}) copy-start(bf16[256,1536]{1,0:T(8,128)(2,1)} %copy-done.17) | copy-start | bytes 2359300
  63.1 1.0 copy-start.19
  63.1 1.0 copy-start.21
  68.9 2.4 %copy-start.11 = (bf16[4,8,32,1152]{3,2,1,0:T(8,128)(2,1)S(1)}, bf16[4,8,32,1152]{3,2,1,0:T(8,128)(2,1)}, u32[]{:S(2)}) copy-start(bf16[4,8,32,1152]{3,2,1,0:T(8,128)(2,1)} %copy-done.10) | copy-start | bytes 7077892
  71.3 1.2 copy-start.16
  71.5 4.2 %copy-start.23 = (bf16[8,192,1152]{2,1,0:T(8,128)(2,1)}, bf16[8,192,1152]{2,1,0:T(8,128)(2,1)S(1)}, u32[]{:S(2)}) copy-start(bf16[8,192,1152]{2,1,0:T(8,128)(2,1)S(1)} %fusion.31) | copy-start | bytes 10616836
  80.8 9.9 %copy-start.1 = (f32[512,384]{1,0:T(8,128)}, f32[512,384]{1,0:T(8,128)S(1)}, u32[]{:S(2)}) copy-start(f32[512,384]{1,0:T(8,128)S(1)} %get-tuple-element.52.dv_a) | copy-start | bytes 2359300
  80.8 9.9 %copy-start.6 = (f32[512,384]{1,0:T(8,128)}, f32[512,384]{1,0:T(8,128)S(1)}, u32[]{:S(2)}) copy-start(f32[512,384]{1,0:T(8,128)S(1)} %get-tuple-element.45.dk_a) | copy-start | bytes 2359300
  80.8 9.7 %copy-start.15 = (bf16[256,1536]{1,0:T(8,128)(2,1)S(1)}, bf16[256,1536]{1,0:T(8,128)(2,1)}, u32[]{:S(2)}) copy-start(bf16[256,1536]{1,0:T(8,128)(2,1)} %copy-done.14) | copy-start | bytes 2359300
  81.0 14.8 %collective-permute-start.9 = (bf16[256,768]{1,0:T(8,128)(2,1)S(1)}, bf16[256,768]{1,0:T(8,128)(2,1)S(1)}, u32[]{:S(2)}, u32[]{:S(2)}) collective-permute-start(bf16[256,768]{1,0:T(8,128)(2,1)S(1)} %pad_maximum_fusion.16), channel_id=1, source_target_pairs={{2,0},{3,1},{4,2},{5,3},{6,4},{7,5},{8,6},{9,7},{10,8},{11,9},{12,... | collective-permute-start | bytes 1179656 | tf_op jit(solution)/shard_map/ppermute | solution.py:354
  90.3 0.9 copy-start.3
  90.4 10.1 %collective-permute-start.11 = (bf16[512,384]{1,0:T(8,128)(2,1)S(1)}, bf16[512,384]{1,0:T(8,128)(2,1)}, u32[]{:S(2)}, u32[]{:S(2)}) collective-permute-start(bf16[512,384]{1,0:T(8,128)(2,1)S(1)} %constant_dynamic-update-slice_fusion.1), channel_id=1, source_target_pairs={{0,1},{1,0},{2,3},{3,2},{4,5},{5,4},{6,7},{7,6},{8,9},{9,8},{10,11... | collective-permute-start | bytes 1179656 | tf_op jit(solution)/shard_map/ppermute | solution.py:124
  90.7 5.1 %copy-start = (bf16[768,1536]{1,0:T(8,128)(2,1)}, bf16[768,1536]{1,0:T(8,128)(2,1)S(1)}, u32[]{:S(2)}) copy-start(bf16[768,1536]{1,0:T(8,128)(2,1)S(1)} %pad_maximum_fusion.low_ref) | copy-start | bytes 7077892
  95.7 4.6 %copy-start.4 = (f32[512,384]{1,0:T(8,128)S(1)}, f32[512,384]{1,0:T(8,128)}, u32[]{:S(2)}) copy-start(f32[512,384]{1,0:T(8,128)} %copy-done.3) | copy-start | bytes 2359300
  95.8 4.6 %copy-start.7 = (f32[512,384]{1,0:T(8,128)S(1)}, f32[512,384]{1,0:T(8,128)}, u32[]{:S(2)}) copy-start(f32[512,384]{1,0:T(8,128)} %copy-done.6) | copy-start | bytes 2359300
  95.8 41.9 %all-to-all-start.2 = ((bf16[16,96,896]{2,1,0:T(8,128)(2,1)}), bf16[16,96,896]{2,1,0:T(8,128)(2,1)}, u32[]{:S(2)}, u32[]{:S(2)}) async-start(bf16[16,96,896]{2,1,0:T(8,128)(2,1)} %bitcast.90), calls=%async_computation.2 | async-start | bytes 5505024 | tf_op jit(solution)/shard_map/all_to_all | solution.py:254
  100.4 1.4 copy-start.2
  100.4 1.5 copy-start.5
  101.9 7.6 %copy-start.20 = (bf16[384,768]{1,0:T(8,128)(2,1)S(1)}, bf16[384,768]{1,0:T(8,128)(2,1)}, u32[]{:S(2)}) copy-start(bf16[384,768]{1,0:T(8,128)(2,1)} %copy-done.19) | copy-start | bytes 1769476
  101.9 7.6 %copy-start.22 = (bf16[384,768]{1,0:T(8,128)(2,1)S(1)}, bf16[384,768]{1,0:T(8,128)(2,1)}, u32[]{:S(2)}) copy-start(bf16[384,768]{1,0:T(8,128)(2,1)} %copy-done.21) | copy-start | bytes 1769476
  107.0 13.1 %collective-permute-start.12 = (bf16[8,2,24,640]{3,2,1,0:T(8,128)(2,1)S(1)}, bf16[8,2,24,640]{3,2,1,0:T(8,128)(2,1)S(1)}, u32[]{:S(2)}, u32[]{:S(2)}) collective-permute-start(bf16[8,2,24,640]{3,2,1,0:T(8,128)(2,1)S(1)} %get-tuple-element.55), channel_id=1, source_target_pairs={{12,0},{13,1},{14,2},{15,3},{0,4},{1,5},{2,6},{3,7},{4,8},{5,9},{6... | collective-permute-start | bytes 1474568 | tf_op jit(solution)/shard_map/ppermute | solution.py:372
  107.6 14.2 %collective-permute-start.13 = (bf16[8,2,24,640]{3,2,1,0:T(8,128)(2,1)S(1)}, bf16[8,2,24,640]{3,2,1,0:T(8,128)(2,1)S(1)}, u32[]{:S(2)}, u32[]{:S(2)}) collective-permute-start(bf16[8,2,24,640]{3,2,1,0:T(8,128)(2,1)S(1)} %get-tuple-element.56), channel_id=1, source_target_pairs={{8,0},{9,1},{10,2},{11,3},{12,4},{13,5},{14,6},{15,7},{0,8},{1,9},... | collective-permute-start | bytes 1474568 | tf_op jit(solution)/shard_map/ppermute | solution.py:372
  108.7 23.4 %collective-permute-start.14 = (bf16[8,2,24,640]{3,2,1,0:T(8,128)(2,1)S(1)}, bf16[8,2,24,640]{3,2,1,0:T(8,128)(2,1)S(1)}, u32[]{:S(2)}, u32[]{:S(2)}) collective-permute-start(bf16[8,2,24,640]{3,2,1,0:T(8,128)(2,1)S(1)} %get-tuple-element.57), channel_id=1, source_target_pairs={{4,0},{5,1},{6,2},{7,3},{8,4},{9,5},{10,6},{11,7},{12,8},{13,9},{1... | collective-permute-start | bytes 1474568 | tf_op jit(solution)/shard_map/ppermute | solution.py:372
  110.5 22.6 %collective-permute-start.10 = (bf16[256,1536]{1,0:T(8,128)(2,1)S(1)}, bf16[256,1536]{1,0:T(8,128)(2,1)S(1)}, u32[]{:S(2)}, u32[]{:S(2)}) collective-permute-start(bf16[256,1536]{1,0:T(8,128)(2,1)S(1)} %dynamic-slice_convert_fusion.1), channel_id=1, source_target_pairs={{0,1},{1,0},{2,3},{3,2},{4,5},{5,4},{6,7},{7,6},{8,9},{9,8},{10,11... | collective-permute-start | bytes 2359304 | tf_op jit(solution)/shard_map/ppermute | solution.py:124
  137.7 16.6 %all-to-all-start.3 = ((bf16[16,24,640]{2,1,0:T(8,128)(2,1)}), bf16[16,24,640]{2,1,0:T(8,128)(2,1)S(1)}, u32[]{:S(2)}, u32[]{:S(2)}) async-start(bf16[16,24,640]{2,1,0:T(8,128)(2,1)} %bitcast.27), calls=%async_computation.3 | async-start | bytes 983040 | tf_op jit(solution)/shard_map/all_to_all | solution.py:254
  144.3 4.3 %copy-start.24 = (bf16[8,192,1152]{2,1,0:T(8,128)(2,1)S(1)}, bf16[8,192,1152]{2,1,0:T(8,128)(2,1)}, u32[]{:S(2)}) copy-start(bf16[8,192,1152]{2,1,0:T(8,128)(2,1)} %copy-done.23) | copy-start | bytes 10616836
  146.7 7.5 %collective-permute-start.16 = (f32[24,896]{1,0:T(8,128)S(1)}, f32[24,896]{1,0:T(8,128)S(1)}, u32[]{:S(2)}, u32[]{:S(2)}) collective-permute-start(f32[24,896]{1,0:T(8,128)S(1)} %get-tuple-element.89), channel_id=1, source_target_pairs={{12,0},{13,1},{14,2},{15,3},{0,4},{1,5},{2,6},{3,7},{4,8},{5,9},{6... | collective-permute-start | bytes 258056 | tf_op jit(solution)/shard_map/ppermute | solution.py:381
  147.3 7.0 %collective-permute-start.18 = (f32[24,896]{1,0:T(8,128)S(1)}, f32[24,896]{1,0:T(8,128)S(1)}, u32[]{:S(2)}, u32[]{:S(2)}) collective-permute-start(f32[24,896]{1,0:T(8,128)S(1)} %get-tuple-element.90), channel_id=1, source_target_pairs={{4,0},{5,1},{6,2},{7,3},{8,4},{9,5},{10,6},{11,7},{12,8},{13,9},{1... | collective-permute-start | bytes 258056 | tf_op jit(solution)/shard_map/ppermute | solution.py:381
  148.2 6.0 %collective-permute-start.17 = (f32[24,896]{1,0:T(8,128)S(1)}, f32[24,896]{1,0:T(8,128)S(1)}, u32[]{:S(2)}, u32[]{:S(2)}) collective-permute-start(f32[24,896]{1,0:T(8,128)S(1)} %get-tuple-element.91), channel_id=1, source_target_pairs={{8,0},{9,1},{10,2},{11,3},{12,4},{13,5},{14,6},{15,7},{0,8},{1,9},... | collective-permute-start | bytes 258056 | tf_op jit(solution)/shard_map/ppermute | solution.py:381
  150.9 1.6 %copy-start.12 = (f32[512,1536]{1,0:T(8,128)}, f32[512,1536]{1,0:T(8,128)S(1)}, u32[]{:S(2)}) copy-start(f32[512,1536]{1,0:T(8,128)S(1)} %fusion.20) | copy-start | bytes 9437188
  152.5 6.0 %copy-start.9 = (bf16[1,256,1536]{2,1,0:T(8,128)(2,1)S(1)}, bf16[1,256,1536]{2,1,0:T(8,128)(2,1)}, u32[]{:S(2)}) copy-start(bf16[1,256,1536]{2,1,0:T(8,128)(2,1)} %param.5) | copy-start | bytes 2359300
  152.6 5.9 %collective-permute-start.15 = (bf16[256,1536]{1,0:T(8,128)(2,1)S(1)}, bf16[256,1536]{1,0:T(8,128)(2,1)S(1)}, u32[]{:S(2)}, u32[]{:S(2)}) collective-permute-start(bf16[256,1536]{1,0:T(8,128)(2,1)S(1)} %dynamic-slice_convert_fusion), channel_id=1, source_target_pairs={{0,1},{1,0},{2,3},{3,2},{4,5},{5,4},{6,7},{7,6},{8,9},{9,8},{10,11... | collective-permute-start | bytes 2359304 | tf_op jit(solution)/shard_map/ppermute | solution.py:124
  154.4 2.5 %collective-permute-start.20 = (f32[6,768]{1,0:T(8,128)S(1)}, f32[6,768]{1,0:T(8,128)S(1)}, u32[]{:S(2)}, u32[]{:S(2)}) collective-permute-start(f32[6,768]{1,0:T(8,128)S(1)} %fusion.41), channel_id=1, source_target_pairs={{0,1},{1,0},{2,3},{3,2},{4,5},{5,4},{6,7},{7,6},{8,9},{9,8},{10,11... | collective-permute-start | bytes 55304 | tf_op jit(solution)/shard_map/ppermute | solution.py:124
  156.1 1.5 collective-permute-start.19
  157.7 2.9 %copy-start.13 = (f32[512,1536]{1,0:T(8,128)S(1)}, f32[512,1536]{1,0:T(8,128)}, u32[]{:S(2)}) copy-start(f32[512,1536]{1,0:T(8,128)} %copy-done.12) | copy-start | bytes 9437188

commit v5 on v4

--- a/solution.py
+++ b/solution.py
@@ -393,9 +393,13 @@
 
     rows = wide // chips // CORES
     total = jnp.concatenate([total_late, total_first[:, : width - LEAD]], axis=1)
-    q_kept = own_half(core, total, rows).reshape(rows, 3, width)
-    q_other = swap(other_half(core, total, rows)).reshape(rows, 3, width)
-    q_out = in_order(lower, q_kept, q_other, 2).reshape(rows, 3 * inner)
+    q_kept = own_half(core, total, rows)
+    q_other = swap(other_half(core, total, rows))
+    lower_q, upper_q = jnp.where(lower, q_kept, q_other), jnp.where(lower, q_other, q_kept)
+    pieces = []
+    for k in range(3):
+        pieces += [part[:, k * width : (k + 1) * width] for part in (lower_q, upper_q)]
+    q_out = jnp.concatenate(pieces, axis=1)
 
     partial = nn(context, full_out)
     branch = (

time: 165 us -> 164 us (level)
    unnamed x60 -> x65, local copies, waits for them, and re-layouts: 7.74 us -> 7.03 us
    select_n x7 -> x6, other arithmetic: 5.09 us -> 5.06 us  [in_order(): jnp.where(lower, own, other)]
where the time goes in v5:
time: 164 us; the launch traced here: 161 us
  waiting for transfers between devices  52 us (32%)
  starting transfers between devices  45.7 us (28%)
  Pallas kernels  19.8 us (12%)
  other arithmetic  17.8 us (11%)
  local copies, waits for them, and re-layouts  16.9 us (10%)
  matrix products  7.39 us (5%)
    ppermute x3, waiting for transfers between devices, body(): summed = summed + lax.ppermute(first[k], ALL, from_y(-k)).astype(F32)  20.7 us
    ppermute x3, waiting for transfers between devices, body(): got = quarter if k == 0 else lax.ppermute(quarter, ALL, from_y(k))  11.5 us
    all_to_all x2, starting transfers between devices, scatter(): return lax.all_to_all(chunks, ('z', 'xl', 'xh'), 0, 0, tiled=True)  11.2 us
    all_to_all x2, starting transfers between devices, gather(): return lax.all_to_all(shards, ('z', 'xl'), 0, 0, tiled=True)  10.6 us
    pallas_call x2, Pallas kernels, attention(): pl.pallas_call(functools.partial(attend, first), in_specs=[whole] * 4, ou...  10.2 us
    ppermute x1, waiting for transfers between devices, body(): past = lax.ppermute(own_low, ALL, ONWARD)  8.45 us
    all_to_all x2, waiting for transfers between devices, gather(): return lax.all_to_all(shards, ('z', 'xl'), 0, 0, tiled=True)  7.09 us
    unnamed x65, local copies, waits for them, and re-layouts  7.03 us
  transfers between devices with their start and end apart: 25, of which 10 were waited for; matrix products, arithmetic and copies ran while one was open for 15% of the time, Pallas kernels for 9%

profile of v5, /device:TPU:9, one launch (start us, length us, event | category | flops | bytes accessed | tf_op | source)
XLA Modules:
  0.0 161.2 jit_solution(11957852564414535343)
XLA Ops:
  0.6 0.9 constant_dynamic-slice_fusion
  1.6 1.3 fusion.55
  2.8 0.8 fusion.59
  3.8 0.9 broadcast_in_dim.43
  4.8 0.3 fusion.15
  5.2 0.3 fusion.7
  5.5 0.8 collective-permute-start
  6.4 6.0 %all-to-all-start = ((bf16[8,32,1152]{2,1,0:T(8,128)(2,1)}), bf16[8,32,1152]{2,1,0:T(8,128)(2,1)S(1)}, u32[]{:S(2)}, u32[]{:S(2)}) async-start(bf16[8,32,1152]{2,1,0:T(8,128)(2,1)} %broadcast_in_dim.43), calls=%async_computation | async-start | bytes 1179648 | tf_op jit(solution)/shard_map/all_to_all | solution.py:262
  12.3 0.7 collective-permute-start.7
  13.2 4.3 %collective-permute-start.1 = (bf16[256,1536]{1,0:T(8,128)(2,1)S(1)}, bf16[256,1536]{1,0:T(8,128)(2,1)}, u32[]{:S(2)}, u32[]{:S(2)}) collective-permute-start(bf16[256,1536]{1,0:T(8,128)(2,1)S(1)} %fusion.7), channel_id=1, source_target_pairs={{1,3},{3,5},{5,7},{7,9},{9,11},{11,13},{13,15},{17,19},{19,21},{21... | collective-permute-start | bytes 2359304 | tf_op jit(solution)/shard_map/ppermute | solution.py:308
  17.8 2.1 %broadcast_select_fusion.3 = (bf16[256,1536]{1,0:T(8,128)(2,1)S(1)}, bf16[256,1536]{1,0:T(8,128)(2,1)}) fusion(bf16[256,1536]{1,0:T(8,128)(2,1)S(1)} %fusion.7, bf16[256,1536]{1,0:T(8,128)(2,1)} %collective-permute-done, pred[]{:T(512)S(6)} %eq.11), kind=kLoop, calls=%fused_computation.56 | loop fusion | flops 786432 | bytes 3145729 | tf_op jit(solution)/shard_map/jit(_where)/select_n | solution.py:249
  19.9 2.3 %all-to-all-done = bf16[8,32,1152]{2,1,0:T(8,128)(2,1)S(1)} async-done(((bf16[8,32,1152]{2,1,0:T(8,128)(2,1)}), bf16[8,32,1152]{2,1,0:T(8,128)(2,1)S(1)}, u32[]{:S(2)}, u32[]{:S(2)}) %all-to-all-start) | async-done | bytes 589856 | tf_op jit(solution)/shard_map/all_to_all | solution.py:262
  22.2 8.5 %collective-permute-done.1 = bf16[256,1536]{1,0:T(8,128)(2,1)} collective-permute-done((bf16[256,1536]{1,0:T(8,128)(2,1)S(1)}, bf16[256,1536]{1,0:T(8,128)(2,1)}, u32[]{:S(2)}, u32[]{:S(2)}) %collective-permute-start.1) | collective-permute-done | bytes 786464 | tf_op jit(solution)/shard_map/ppermute | solution.py:308
  30.7 1.7 %broadcast_in_dim.41 = bf16[8,128,1152]{2,1,0:T(8,128)(2,1)} broadcast(bf16[128,1152]{1,0:T(8,128)(2,1)S(1)} %slice.183), dimensions={1,2} | broadcast | bytes 2654208 | tf_op jit(solution)/shard_map/broadcast_in_dim | solution.py:258
  32.4 1.5 broadcast_select_fusion.1
  33.9 1.5 collective-permute-start.6
  35.4 3.5 %collective-permute-start.5 = (bf16[8,32,1152]{2,1,0:T(8,128)(2,1)S(1)}, bf16[8,32,1152]{2,1,0:T(8,128)(2,1)}, u32[]{:S(2)}, u32[]{:S(2)}) collective-permute-start(bf16[8,32,1152]{2,1,0:T(8,128)(2,1)S(1)} %all-to-all-done), channel_id=1, source_target_pairs={{8,0},{9,1},{10,2},{11,3},{12,4},{13,5},{14,6},{15,7},{0,8},{1,9},... | collective-permute-start | bytes 1769480 | tf_op jit(solution)/shard_map/ppermute | solution.py:314
  38.9 4.6 %all-to-all-start.1 = ((bf16[8,128,1152]{2,1,0:T(8,128)(2,1)}), bf16[8,128,1152]{2,1,0:T(8,128)(2,1)}, u32[]{:S(2)}, u32[]{:S(2)}) async-start(bf16[8,128,1152]{2,1,0:T(8,128)(2,1)} %broadcast_in_dim.41), calls=%async_computation.1 | async-start | bytes 4718592 | tf_op jit(solution)/shard_map/all_to_all | solution.py:262
  43.8 3.0 %collective-permute-done.4 = bf16[8,32,1152]{2,1,0:T(8,128)(2,1)} collective-permute-done((bf16[8,32,1152]{2,1,0:T(8,128)(2,1)S(1)}, bf16[8,32,1152]{2,1,0:T(8,128)(2,1)}, u32[]{:S(2)}, u32[]{:S(2)}) %collective-permute-start.4) | collective-permute-done | bytes 589856 | tf_op jit(solution)/shard_map/ppermute | solution.py:314
  46.9 1.1 bitcast_dynamic-update-slice_fusion.2
  48.0 8.5 %collective-permute-done.5 = bf16[8,32,1152]{2,1,0:T(8,128)(2,1)} collective-permute-done((bf16[8,32,1152]{2,1,0:T(8,128)(2,1)S(1)}, bf16[8,32,1152]{2,1,0:T(8,128)(2,1)}, u32[]{:S(2)}, u32[]{:S(2)}) %collective-permute-start.5) | collective-permute-done | bytes 589856 | tf_op jit(solution)/shard_map/ppermute | solution.py:314
  56.5 1.1 bitcast_dynamic-update-slice_fusion.1
  57.6 1.1 bitcast_dynamic-update-slice_fusion
  59.0 1.1 copy-done.10
  60.5 1.0 fusion.28.up_ref
  61.5 1.3 broadcast_select_fusion.4
  63.1 1.0 fusion.16
  64.2 4.7 %all-to-all-done.1 = bf16[8,128,1152]{2,1,0:T(8,128)(2,1)} async-done(((bf16[8,128,1152]{2,1,0:T(8,128)(2,1)}), bf16[8,128,1152]{2,1,0:T(8,128)(2,1)}, u32[]{:S(2)}, u32[]{:S(2)}) %all-to-all-start.1) | async-done | bytes 2359328 | tf_op jit(solution)/shard_map/all_to_all | solution.py:262
  68.9 2.0 %constant_dynamic-update-slice_fusion = bf16[8,192,1152]{2,1,0:T(8,128)(2,1)S(1)} fusion(bf16[8,128,1152]{2,1,0:T(8,128)(2,1)} %all-to-all-done.1), kind=kLoop, calls=%fused_computation.112 | loop fusion | bytes 4718592
  71.0 0.3 copy-done.11
  71.5 1.0 copy-done.16
  72.5 3.2 %convolution_convert_fusion.proj_ref = bf16[768,1152]{1,0:T(8,128)(2,1)S(1)} fusion(bf16[1536,1152]{1,0:T(8,128)(2,1)S(1)} %bitcast.90, bf16[256,1536]{1,0:T(8,128)(2,1)S(1)} %copy-done.16, bf16[256,1536]{1,0:T(8,128)(2,1)S(1)} %get-tuple-element.76, bf16[256,1536]{1,0:T(8,128)(2,1)S(1)} %broadcast_select_fusion.4), kind=kOutput, calls=%fused_computation.1 | convolution fusion | flops 2725871616 | bytes 7667712 | tf_op jit(solution)/shard_map/dot_general | solution.py:32
  75.7 5.1 %attend.2 = (bf16[256,384]{1,0:T(8,128)(2,1)S(1)}, bf16[256,384]{1,0:T(8,128)(2,1)S(1)}, f32[512,384]{1,0:T(8,128)S(1)}, f32[512,384]{1,0:T(8,128)S(1)}) custom-call(s32[4,128]{1,0:T(4,128)S(1)} %get-tuple-element.103.lo_ref, s32[4,128]{1,0:T(4,128)S(1)} %get-tuple-element.101.hi_ref, bf16[768,1152]{1,0:T(8,128)(2,1)S(1)} %convolution_convert_fusion.proj_ref, ...), custom_call_target="tpu_custom_call" | custom-call | tf_op jit(solution)/shard_map/attend/pallas_call | solution.py:82
  81.0 4.3 %collective-permute-start.9 = (bf16[256,768]{1,0:T(8,128)(2,1)S(1)}, bf16[256,768]{1,0:T(8,128)(2,1)S(1)}, u32[]{:S(2)}, u32[]{:S(2)}) collective-permute-start(bf16[256,768]{1,0:T(8,128)(2,1)S(1)} %pad_maximum_fusion.16), channel_id=1, source_target_pairs={{2,0},{3,1},{4,2},{5,3},{6,4},{7,5},{8,6},{9,7},{10,8},{11,9},{12,... | collective-permute-start | bytes 1179656 | tf_op jit(solution)/shard_map/ppermute | solution.py:354
  85.2 5.1 %attend.3 = (bf16[256,384]{1,0:T(8,128)(2,1)S(1)}, bf16[256,384]{1,0:T(8,128)(2,1)S(1)}, f32[512,384]{1,0:T(8,128)S(1)}, f32[512,384]{1,0:T(8,128)S(1)}) custom-call(s32[4,128]{1,0:T(4,128)S(1)} %get-tuple-element.102.lo_ref, s32[4,128]{1,0:T(4,128)S(1)} %get-tuple-element.100.hi_ref, bf16[768,1152]{1,0:T(8,128)(2,1)S(1)} %convolution_convert_fusion.proj_ref, ...), custom_call_target="tpu_custom_call" | custom-call | tf_op jit(solution)/shard_map/attend/pallas_call | solution.py:82
  90.7 0.5 copy-done.3
  91.2 4.5 %late_gradients.1 = bf16[8,2,4,24,896]{4,3,2,1,0:T(8,128)(2,1)} custom-call(bf16[768,1536]{1,0:T(8,128)(2,1)S(1)} %pad_maximum_fusion.low_ref, bf16[256,384]{1,0:T(8,128)(2,1)S(1)} %get-tuple-element.43.dq_a, bf16[256,384]{1,0:T(8,128)(2,1)S(1)} %get-tuple-element.61.dq_b, f32[512,384]{1,0:T(8,128)S(1)} %get-tuple-element.45.dk_a, ...), custom_call_target="tpu_custom_call" | custom-call | tf_op jit(solution)/shard_map/late_gradients/pallas_call | solution.py:194
  95.8 4.6 %all-to-all-start.2 = ((bf16[16,96,896]{2,1,0:T(8,128)(2,1)}), bf16[16,96,896]{2,1,0:T(8,128)(2,1)}, u32[]{:S(2)}, u32[]{:S(2)}) async-start(bf16[16,96,896]{2,1,0:T(8,128)(2,1)} %bitcast.87), calls=%async_computation.2 | async-start | bytes 5505024 | tf_op jit(solution)/shard_map/all_to_all | solution.py:254
  100.5 1.2 broadcast_select_fusion.8
  101.9 5.1 %first_gradients.1 = (bf16[8,2,24,640]{3,2,1,0:T(8,128)(2,1)S(1)}, bf16[8,2,24,640]{3,2,1,0:T(8,128)(2,1)S(1)}, bf16[8,2,24,640]{3,2,1,0:T(8,128)(2,1)S(1)}, bf16[8,2,24,640]{3,2,1,0:T(8,128)(2,1)S(1)}) custom-call(s32[1]{0:T(128)} %bitcast.26.y_ref, bf16[512,768]{1,0:T(8,128)(2,1)S(1)} %pad_maximum_fusion.10.ctx_ref, bf16[512,768]{1,0:T(8,128)(2,1)S(1)} %copy-done.5, ...), custom_call_target="tpu_custom_call" | custom-call | tf_op jit(solution)/shard_map/first_gradients/pallas_call | solution.py:215
  107.0 0.6 collective-permute-start.12
  107.6 1.2 collective-permute-start.13
  108.7 0.7 collective-permute-start.14
  109.5 1.0 fusion.29
  110.5 0.7 collective-permute-start.10
  111.4 8.7 %collective-permute-done.12 = bf16[8,2,24,640]{3,2,1,0:T(8,128)(2,1)S(1)} collective-permute-done((bf16[8,2,24,640]{3,2,1,0:T(8,128)(2,1)S(1)}, bf16[8,2,24,640]{3,2,1,0:T(8,128)(2,1)S(1)}, u32[]{:S(2)}, u32[]{:S(2)}) %collective-permute-start.12) | collective-permute-done | bytes 491552 | tf_op jit(solution)/shard_map/ppermute | solution.py:372
  120.1 1.7 %collective-permute-done.13 = bf16[8,2,24,640]{3,2,1,0:T(8,128)(2,1)S(1)} collective-permute-done((bf16[8,2,24,640]{3,2,1,0:T(8,128)(2,1)S(1)}, bf16[8,2,24,640]{3,2,1,0:T(8,128)(2,1)S(1)}, u32[]{:S(2)}, u32[]{:S(2)}) %collective-permute-start.13) | collective-permute-done | bytes 491552 | tf_op jit(solution)/shard_map/ppermute | solution.py:372
  121.8 10.3 %collective-permute-done.14 = bf16[8,2,24,640]{3,2,1,0:T(8,128)(2,1)S(1)} collective-permute-done((bf16[8,2,24,640]{3,2,1,0:T(8,128)(2,1)S(1)}, bf16[8,2,24,640]{3,2,1,0:T(8,128)(2,1)S(1)}, u32[]{:S(2)}, u32[]{:S(2)}) %collective-permute-start.14) | collective-permute-done | bytes 491552 | tf_op jit(solution)/shard_map/ppermute | solution.py:372
  132.1 1.0 add_convert_fusion.1
  133.1 1.1 fusion.26
  134.2 3.5 %all-to-all-done.2 = bf16[16,96,896]{2,1,0:T(8,128)(2,1)} async-done(((bf16[16,96,896]{2,1,0:T(8,128)(2,1)}), bf16[16,96,896]{2,1,0:T(8,128)(2,1)}, u32[]{:S(2)}, u32[]{:S(2)}) %all-to-all-start.2) | async-done | bytes 2752544 | tf_op jit(solution)/shard_map/all_to_all | solution.py:254
  137.7 6.6 %all-to-all-start.3 = ((bf16[16,24,640]{2,1,0:T(8,128)(2,1)}), bf16[16,24,640]{2,1,0:T(8,128)(2,1)S(1)}, u32[]{:S(2)}, u32[]{:S(2)}) async-start(bf16[16,24,640]{2,1,0:T(8,128)(2,1)} %bitcast.27), calls=%async_computation.3 | async-start | bytes 983040 | tf_op jit(solution)/shard_map/all_to_all | solution.py:254
  144.3 2.4 %convert_reduce_fusion = f32[96,896]{1,0:T(8,128)S(1)} fusion(bf16[16,96,896]{2,1,0:T(8,128)(2,1)} %all-to-all-done.2), kind=kLoop, calls=%fused_computation | loop fusion | flops 2666496 | bytes 3096576 | tf_op jit(solution)/shard_map/reduce_sum | solution.py:377
  146.7 0.5 collective-permute-start.16
  147.3 1.0 collective-permute-start.18
  148.3 0.3 collective-permute-start.17
  148.6 2.2 %fusion.20 = f32[512,1536]{1,0:T(8,128)S(1)} fusion(bf16[1536,1152]{1,0:T(8,128)(2,1)S(1)} %bitcast.91, bf16[256,768]{1,0:T(8,128)(2,1)S(1)} %add_convert_fusion.2, bf16[256,384]{1,0:T(8,128)(2,1)S(1)} %get-tuple-element.61.dq_b, bf16[256,1152]{1,0:T(8,128)(2,1)S(1)} %pad_maximum_fusion.14), kind=kOutput, calls=%fused_computation.39 | convolution fusion | flops 1815478272 | bytes 7864320 | tf_op jit(solution)/shard_map/dot_general | solution.py:24
  150.9 1.6 %copy-done.12 = f32[512,1536]{1,0:T(8,128)} copy-done((f32[512,1536]{1,0:T(8,128)}, f32[512,1536]{1,0:T(8,128)S(1)}, u32[]{:S(2)}) %copy-start.12) | copy-done | bytes 3145752
  152.6 1.7 %collective-permute-start.15 = (bf16[256,1536]{1,0:T(8,128)(2,1)S(1)}, bf16[256,1536]{1,0:T(8,128)(2,1)S(1)}, u32[]{:S(2)}, u32[]{:S(2)}) collective-permute-start(bf16[256,1536]{1,0:T(8,128)(2,1)S(1)} %dynamic-slice_convert_fusion), channel_id=1, source_target_pairs={{0,1},{1,0},{2,3},{3,2},{4,5},{5,4},{6,7},{7,6},{8,9},{9,8},{10,11... | collective-permute-start | bytes 2359304 | tf_op jit(solution)/shard_map/ppermute | solution.py:124
  154.4 1.7 %collective-permute-start.20 = (f32[6,768]{1,0:T(8,128)S(1)}, f32[6,768]{1,0:T(8,128)S(1)}, u32[]{:S(2)}, u32[]{:S(2)}) collective-permute-start(f32[6,768]{1,0:T(8,128)S(1)} %fusion.41), channel_id=1, source_target_pairs={{0,1},{1,0},{2,3},{3,2},{4,5},{5,4},{6,7},{7,6},{8,9},{9,8},{10,11... | collective-permute-start | bytes 55304 | tf_op jit(solution)/shard_map/ppermute | solution.py:124
  156.2 0.7 collective-permute-done.20
  157.0 0.6 pad_maximum_fusion.18
  157.7 1.9 %fusion.30 = (f32[256]{0:T(256)S(1)}, f32[256]{0:T(256)S(1)}) fusion(bf16[256,1536]{1,0:T(8,128)(2,1)S(1)} %collective-permute-done.15, f32[512,1536]{1,0:T(8,128)} %copy-done.12, s32[]{:T(128)S(6)} %select_n.188, f32[256]{0:T(256)S(1)} %add_rsqrt_fusion, f32[256]{0:T(256)S(1)} %broadcast_multiply_fusion.2, bf16[256,1536]{1,0:T(8,128)(2,1)S(1)} %bitcast.85), kind=kLoop, calls=%fused_computation.67 | loop fusion | flops 3145216 | bytes 3149828 | tf_op jit(solution)/shard_map/reduce_sum | solution.py:416
  159.7 1.5 fusion.27
  (129 shorter events, 3.6 us)
Async XLA Ops:
  1.5 3.1 %copy-start.8 = (bf16[1,256,1536]{2,1,0:T(8,128)(2,1)S(1)}, bf16[1,256,1536]{2,1,0:T(8,128)(2,1)}, u32[]{:S(2)}) copy-start(bf16[1,256,1536]{2,1,0:T(8,128)(2,1)} %param.5) | copy-start | bytes 2359300
  3.7 2.6 %copy-start.25 = (s32[2,1,256]{2,1,0:T(1,128)S(1)}, s32[2,1,256]{2,1,0:T(1,128)}, u32[]{:S(2)}) copy-start(s32[2,1,256]{2,1,0:T(1,128)} %param.7) | copy-start | bytes 6148
  5.5 7.8 %collective-permute-start = (bf16[256,1536]{1,0:T(8,128)(2,1)S(1)}, bf16[256,1536]{1,0:T(8,128)(2,1)}, u32[]{:S(2)}, u32[]{:S(2)}) collective-permute-start(bf16[256,1536]{1,0:T(8,128)(2,1)S(1)} %fusion.7), channel_id=1, source_target_pairs={{0,1},{1,0},{2,3},{3,2},{4,5},{5,4},{6,7},{7,6},{8,9},{9,8},{10,11... | collective-permute-start | bytes 2359304 | tf_op jit(solution)/shard_map/ppermute | solution.py:124
  6.3 6.9 %collective-permute-start.3 = (s32[256,2]{0,1:T(2,128)S(1)}, s32[256,2]{0,1:T(2,128)S(1)}, u32[]{:S(2)}, u32[]{:S(2)}) collective-permute-start(s32[256,2]{0,1:T(2,128)S(1)} %bitcast.96), channel_id=1, source_target_pairs={{0,1},{1,0},{2,3},{3,2},{4,5},{5,4},{6,7},{7,6},{8,9},{9,8},{10,11... | collective-permute-start | bytes 6152 | tf_op jit(solution)/shard_map/ppermute | solution.py:124
  6.4 15.9 %all-to-all-start = ((bf16[8,32,1152]{2,1,0:T(8,128)(2,1)}), bf16[8,32,1152]{2,1,0:T(8,128)(2,1)S(1)}, u32[]{:S(2)}, u32[]{:S(2)}) async-start(bf16[8,32,1152]{2,1,0:T(8,128)(2,1)} %broadcast_in_dim.43), calls=%async_computation | async-start | bytes 1179648 | tf_op jit(solution)/shard_map/all_to_all | solution.py:262
  12.3 20.0 %collective-permute-start.7 = (bf16[256,1536]{1,0:T(8,128)(2,1)}, bf16[256,1536]{1,0:T(8,128)(2,1)}, u32[]{:S(2)}, u32[]{:S(2)}) collective-permute-start(bf16[256,1536]{1,0:T(8,128)(2,1)} %bitcast.1), channel_id=1, source_target_pairs={{0,1},{1,0},{2,3},{3,2},{4,5},{5,4},{6,7},{7,6},{8,9},{9,8},{10,11... | collective-permute-start | bytes 2359304 | tf_op jit(solution)/shard_map/ppermute | solution.py:124
  13.2 17.4 %collective-permute-start.1 = (bf16[256,1536]{1,0:T(8,128)(2,1)S(1)}, bf16[256,1536]{1,0:T(8,128)(2,1)}, u32[]{:S(2)}, u32[]{:S(2)}) collective-permute-start(bf16[256,1536]{1,0:T(8,128)(2,1)S(1)} %fusion.7), channel_id=1, source_target_pairs={{1,3},{3,5},{5,7},{7,9},{9,11},{11,13},{13,15},{17,19},{19,21},{21... | collective-permute-start | bytes 2359304 | tf_op jit(solution)/shard_map/ppermute | solution.py:308
  19.9 51.6 %copy-start.14 = (bf16[256,1536]{1,0:T(8,128)(2,1)}, bf16[256,1536]{1,0:T(8,128)(2,1)S(1)}, u32[]{:S(2)}) copy-start(bf16[256,1536]{1,0:T(8,128)(2,1)S(1)} %get-tuple-element.76) | copy-start | bytes 2359300
  32.4 14.5 %collective-permute-start.4 = (bf16[8,32,1152]{2,1,0:T(8,128)(2,1)S(1)}, bf16[8,32,1152]{2,1,0:T(8,128)(2,1)}, u32[]{:S(2)}, u32[]{:S(2)}) collective-permute-start(bf16[8,32,1152]{2,1,0:T(8,128)(2,1)S(1)} %all-to-all-done), channel_id=1, source_target_pairs={{4,0},{5,1},{6,2},{7,3},{8,4},{9,5},{10,6},{11,7},{12,8},{13,9},{1... | collective-permute-start | bytes 1769480 | tf_op jit(solution)/shard_map/ppermute | solution.py:314
  33.8 26.6 %copy-start.17 = (bf16[256,1536]{1,0:T(8,128)(2,1)}, bf16[256,1536]{1,0:T(8,128)(2,1)S(1)}, u32[]{:S(2)}) copy-start(bf16[256,1536]{1,0:T(8,128)(2,1)S(1)} %get-tuple-element.75) | copy-start | bytes 2359300
  33.9 23.8 %collective-permute-start.6 = (bf16[8,32,1152]{2,1,0:T(8,128)(2,1)S(1)}, bf16[8,32,1152]{2,1,0:T(8,128)(2,1)}, u32[]{:S(2)}, u32[]{:S(2)}) collective-permute-start(bf16[8,32,1152]{2,1,0:T(8,128)(2,1)S(1)} %all-to-all-done), channel_id=1, source_target_pairs={{12,0},{13,1},{14,2},{15,3},{0,4},{1,5},{2,6},{3,7},{4,8},{5,9},{6... | collective-permute-start | bytes 1769480 | tf_op jit(solution)/shard_map/ppermute | solution.py:314
  35.4 21.1 %collective-permute-start.5 = (bf16[8,32,1152]{2,1,0:T(8,128)(2,1)S(1)}, bf16[8,32,1152]{2,1,0:T(8,128)(2,1)}, u32[]{:S(2)}, u32[]{:S(2)}) collective-permute-start(bf16[8,32,1152]{2,1,0:T(8,128)(2,1)S(1)} %all-to-all-done), channel_id=1, source_target_pairs={{8,0},{9,1},{10,2},{11,3},{12,4},{13,5},{14,6},{15,7},{0,8},{1,9},... | collective-permute-start | bytes 1769480 | tf_op jit(solution)/shard_map/ppermute | solution.py:314
  38.9 30.0 %all-to-all-start.1 = ((bf16[8,128,1152]{2,1,0:T(8,128)(2,1)}), bf16[8,128,1152]{2,1,0:T(8,128)(2,1)}, u32[]{:S(2)}, u32[]{:S(2)}) async-start(bf16[8,128,1152]{2,1,0:T(8,128)(2,1)} %broadcast_in_dim.41), calls=%async_computation.1 | async-start | bytes 4718592 | tf_op jit(solution)/shard_map/all_to_all | solution.py:262
  43.5 17.9 %collective-permute-start.2 = (bf16[256,1536]{1,0:T(8,128)(2,1)}, bf16[256,1536]{1,0:T(8,128)(2,1)S(1)}, u32[]{:S(2)}, u32[]{:S(2)}) collective-permute-start(bf16[256,1536]{1,0:T(8,128)(2,1)} %collective-permute-done.1), channel_id=1, source_target_pairs={{0,1},{1,0},{2,3},{3,2},{4,5},{5,4},{6,7},{7,6},{8,9},{9,8},{10,11... | collective-permute-start | bytes 2359304 | tf_op jit(solution)/shard_map/ppermute | solution.py:124
  58.8 1.4 copy-start.10
  60.2 2.6 %collective-permute-start.8 = (bf16[384,768]{1,0:T(8,128)(2,1)S(1)}, bf16[384,768]{1,0:T(8,128)(2,1)S(1)}, u32[]{:S(2)}, u32[]{:S(2)}) collective-permute-start(bf16[384,768]{1,0:T(8,128)(2,1)S(1)} %constant_dynamic-slice_fusion.1), channel_id=1, source_target_pairs={{0,1},{1,0},{2,3},{3,2},{4,5},{5,4},{6,7},{7,6},{8,9},{9,8},{10,11... | collective-permute-start | bytes 1769480 | tf_op jit(solution)/shard_map/ppermute | solution.py:124
  61.5 1.6 %copy-start.18 = (bf16[256,1536]{1,0:T(8,128)(2,1)S(1)}, bf16[256,1536]{1,0:T(8,128)(2,1)}, u32[]{:S(2)}) copy-start(bf16[256,1536]{1,0:T(8,128)(2,1)} %copy-done.17) | copy-start | bytes 2359300
  63.1 1.0 copy-start.19
  63.1 1.0 copy-start.21
  68.9 2.4 %copy-start.11 = (bf16[4,8,32,1152]{3,2,1,0:T(8,128)(2,1)S(1)}, bf16[4,8,32,1152]{3,2,1,0:T(8,128)(2,1)}, u32[]{:S(2)}) copy-start(bf16[4,8,32,1152]{3,2,1,0:T(8,128)(2,1)} %copy-done.10) | copy-start | bytes 7077892
  71.3 1.2 copy-start.16
  71.5 4.2 %copy-start.23 = (bf16[8,192,1152]{2,1,0:T(8,128)(2,1)}, bf16[8,192,1152]{2,1,0:T(8,128)(2,1)S(1)}, u32[]{:S(2)}) copy-start(bf16[8,192,1152]{2,1,0:T(8,128)(2,1)S(1)} %fusion.31) | copy-start | bytes 10616836
  80.8 9.9 %copy-start.1 = (f32[512,384]{1,0:T(8,128)}, f32[512,384]{1,0:T(8,128)S(1)}, u32[]{:S(2)}) copy-start(f32[512,384]{1,0:T(8,128)S(1)} %get-tuple-element.52.dv_a) | copy-start | bytes 2359300
  80.8 9.9 %copy-start.6 = (f32[512,384]{1,0:T(8,128)}, f32[512,384]{1,0:T(8,128)S(1)}, u32[]{:S(2)}) copy-start(f32[512,384]{1,0:T(8,128)S(1)} %get-tuple-element.45.dk_a) | copy-start | bytes 2359300
  80.8 9.7 %copy-start.15 = (bf16[256,1536]{1,0:T(8,128)(2,1)S(1)}, bf16[256,1536]{1,0:T(8,128)(2,1)}, u32[]{:S(2)}) copy-start(bf16[256,1536]{1,0:T(8,128)(2,1)} %copy-done.14) | copy-start | bytes 2359300
  81.0 14.8 %collective-permute-start.9 = (bf16[256,768]{1,0:T(8,128)(2,1)S(1)}, bf16[256,768]{1,0:T(8,128)(2,1)S(1)}, u32[]{:S(2)}, u32[]{:S(2)}) collective-permute-start(bf16[256,768]{1,0:T(8,128)(2,1)S(1)} %pad_maximum_fusion.16), channel_id=1, source_target_pairs={{2,0},{3,1},{4,2},{5,3},{6,4},{7,5},{8,6},{9,7},{10,8},{11,9},{12,... | collective-permute-start | bytes 1179656 | tf_op jit(solution)/shard_map/ppermute | solution.py:354
  90.3 0.9 copy-start.3
  90.4 10.1 %collective-permute-start.11 = (bf16[512,384]{1,0:T(8,128)(2,1)S(1)}, bf16[512,384]{1,0:T(8,128)(2,1)}, u32[]{:S(2)}, u32[]{:S(2)}) collective-permute-start(bf16[512,384]{1,0:T(8,128)(2,1)S(1)} %constant_dynamic-update-slice_fusion.1), channel_id=1, source_target_pairs={{0,1},{1,0},{2,3},{3,2},{4,5},{5,4},{6,7},{7,6},{8,9},{9,8},{10,11... | collective-permute-start | bytes 1179656 | tf_op jit(solution)/shard_map/ppermute | solution.py:124
  90.7 5.1 %copy-start = (bf16[768,1536]{1,0:T(8,128)(2,1)}, bf16[768,1536]{1,0:T(8,128)(2,1)S(1)}, u32[]{:S(2)}) copy-start(bf16[768,1536]{1,0:T(8,128)(2,1)S(1)} %pad_maximum_fusion.low_ref) | copy-start | bytes 7077892
  95.8 4.6 %copy-start.4 = (f32[512,384]{1,0:T(8,128)S(1)}, f32[512,384]{1,0:T(8,128)}, u32[]{:S(2)}) copy-start(f32[512,384]{1,0:T(8,128)} %copy-done.3) | copy-start | bytes 2359300
  95.8 4.6 %copy-start.7 = (f32[512,384]{1,0:T(8,128)S(1)}, f32[512,384]{1,0:T(8,128)}, u32[]{:S(2)}) copy-start(f32[512,384]{1,0:T(8,128)} %copy-done.6) | copy-start | bytes 2359300
  95.8 41.9 %all-to-all-start.2 = ((bf16[16,96,896]{2,1,0:T(8,128)(2,1)}), bf16[16,96,896]{2,1,0:T(8,128)(2,1)}, u32[]{:S(2)}, u32[]{:S(2)}) async-start(bf16[16,96,896]{2,1,0:T(8,128)(2,1)} %bitcast.87), calls=%async_computation.2 | async-start | bytes 5505024 | tf_op jit(solution)/shard_map/all_to_all | solution.py:254
  100.4 1.4 copy-start.2
  100.4 1.5 copy-start.5
  101.9 7.6 %copy-start.20 = (bf16[384,768]{1,0:T(8,128)(2,1)S(1)}, bf16[384,768]{1,0:T(8,128)(2,1)}, u32[]{:S(2)}) copy-start(bf16[384,768]{1,0:T(8,128)(2,1)} %copy-done.19) | copy-start | bytes 1769476
  101.9 7.6 %copy-start.22 = (bf16[384,768]{1,0:T(8,128)(2,1)S(1)}, bf16[384,768]{1,0:T(8,128)(2,1)}, u32[]{:S(2)}) copy-start(bf16[384,768]{1,0:T(8,128)(2,1)} %copy-done.21) | copy-start | bytes 1769476
  107.0 13.1 %collective-permute-start.12 = (bf16[8,2,24,640]{3,2,1,0:T(8,128)(2,1)S(1)}, bf16[8,2,24,640]{3,2,1,0:T(8,128)(2,1)S(1)}, u32[]{:S(2)}, u32[]{:S(2)}) collective-permute-start(bf16[8,2,24,640]{3,2,1,0:T(8,128)(2,1)S(1)} %get-tuple-element.55), channel_id=1, source_target_pairs={{12,0},{13,1},{14,2},{15,3},{0,4},{1,5},{2,6},{3,7},{4,8},{5,9},{6... | collective-permute-start | bytes 1474568 | tf_op jit(solution)/shard_map/ppermute | solution.py:372
  107.6 14.2 %collective-permute-start.13 = (bf16[8,2,24,640]{3,2,1,0:T(8,128)(2,1)S(1)}, bf16[8,2,24,640]{3,2,1,0:T(8,128)(2,1)S(1)}, u32[]{:S(2)}, u32[]{:S(2)}) collective-permute-start(bf16[8,2,24,640]{3,2,1,0:T(8,128)(2,1)S(1)} %get-tuple-element.56), channel_id=1, source_target_pairs={{8,0},{9,1},{10,2},{11,3},{12,4},{13,5},{14,6},{15,7},{0,8},{1,9},... | collective-permute-start | bytes 1474568 | tf_op jit(solution)/shard_map/ppermute | solution.py:372
  108.7 23.4 %collective-permute-start.14 = (bf16[8,2,24,640]{3,2,1,0:T(8,128)(2,1)S(1)}, bf16[8,2,24,640]{3,2,1,0:T(8,128)(2,1)S(1)}, u32[]{:S(2)}, u32[]{:S(2)}) collective-permute-start(bf16[8,2,24,640]{3,2,1,0:T(8,128)(2,1)S(1)} %get-tuple-element.57), channel_id=1, source_target_pairs={{4,0},{5,1},{6,2},{7,3},{8,4},{9,5},{10,6},{11,7},{12,8},{13,9},{1... | collective-permute-start | bytes 1474568 | tf_op jit(solution)/shard_map/ppermute | solution.py:372
  110.5 22.6 %collective-permute-start.10 = (bf16[256,1536]{1,0:T(8,128)(2,1)S(1)}, bf16[256,1536]{1,0:T(8,128)(2,1)S(1)}, u32[]{:S(2)}, u32[]{:S(2)}) collective-permute-start(bf16[256,1536]{1,0:T(8,128)(2,1)S(1)} %dynamic-slice_convert_fusion.1), channel_id=1, source_target_pairs={{0,1},{1,0},{2,3},{3,2},{4,5},{5,4},{6,7},{7,6},{8,9},{9,8},{10,11... | collective-permute-start | bytes 2359304 | tf_op jit(solution)/shard_map/ppermute | solution.py:124
  137.7 16.6 %all-to-all-start.3 = ((bf16[16,24,640]{2,1,0:T(8,128)(2,1)}), bf16[16,24,640]{2,1,0:T(8,128)(2,1)S(1)}, u32[]{:S(2)}, u32[]{:S(2)}) async-start(bf16[16,24,640]{2,1,0:T(8,128)(2,1)} %bitcast.27), calls=%async_computation.3 | async-start | bytes 983040 | tf_op jit(solution)/shard_map/all_to_all | solution.py:254
  144.3 4.3 %copy-start.24 = (bf16[8,192,1152]{2,1,0:T(8,128)(2,1)S(1)}, bf16[8,192,1152]{2,1,0:T(8,128)(2,1)}, u32[]{:S(2)}) copy-start(bf16[8,192,1152]{2,1,0:T(8,128)(2,1)} %copy-done.23) | copy-start | bytes 10616836
  146.7 7.5 %collective-permute-start.16 = (f32[24,896]{1,0:T(8,128)S(1)}, f32[24,896]{1,0:T(8,128)S(1)}, u32[]{:S(2)}, u32[]{:S(2)}) collective-permute-start(f32[24,896]{1,0:T(8,128)S(1)} %get-tuple-element.89), channel_id=1, source_target_pairs={{12,0},{13,1},{14,2},{15,3},{0,4},{1,5},{2,6},{3,7},{4,8},{5,9},{6... | collective-permute-start | bytes 258056 | tf_op jit(solution)/shard_map/ppermute | solution.py:381
  147.3 7.0 %collective-permute-start.18 = (f32[24,896]{1,0:T(8,128)S(1)}, f32[24,896]{1,0:T(8,128)S(1)}, u32[]{:S(2)}, u32[]{:S(2)}) collective-permute-start(f32[24,896]{1,0:T(8,128)S(1)} %get-tuple-element.90), channel_id=1, source_target_pairs={{4,0},{5,1},{6,2},{7,3},{8,4},{9,5},{10,6},{11,7},{12,8},{13,9},{1... | collective-permute-start | bytes 258056 | tf_op jit(solution)/shard_map/ppermute | solution.py:381
  148.3 6.0 %collective-permute-start.17 = (f32[24,896]{1,0:T(8,128)S(1)}, f32[24,896]{1,0:T(8,128)S(1)}, u32[]{:S(2)}, u32[]{:S(2)}) collective-permute-start(f32[24,896]{1,0:T(8,128)S(1)} %get-tuple-element.91), channel_id=1, source_target_pairs={{8,0},{9,1},{10,2},{11,3},{12,4},{13,5},{14,6},{15,7},{0,8},{1,9},... | collective-permute-start | bytes 258056 | tf_op jit(solution)/shard_map/ppermute | solution.py:381
  150.9 1.6 %copy-start.12 = (f32[512,1536]{1,0:T(8,128)}, f32[512,1536]{1,0:T(8,128)S(1)}, u32[]{:S(2)}) copy-start(f32[512,1536]{1,0:T(8,128)S(1)} %fusion.20) | copy-start | bytes 9437188
  152.5 5.2 %copy-start.9 = (bf16[1,256,1536]{2,1,0:T(8,128)(2,1)S(1)}, bf16[1,256,1536]{2,1,0:T(8,128)(2,1)}, u32[]{:S(2)}) copy-start(bf16[1,256,1536]{2,1,0:T(8,128)(2,1)} %param.5) | copy-start | bytes 2359300
  152.6 5.1 %collective-permute-start.15 = (bf16[256,1536]{1,0:T(8,128)(2,1)S(1)}, bf16[256,1536]{1,0:T(8,128)(2,1)S(1)}, u32[]{:S(2)}, u32[]{:S(2)}) collective-permute-start(bf16[256,1536]{1,0:T(8,128)(2,1)S(1)} %dynamic-slice_convert_fusion), channel_id=1, source_target_pairs={{0,1},{1,0},{2,3},{3,2},{4,5},{5,4},{6,7},{7,6},{8,9},{9,8},{10,11... | collective-permute-start | bytes 2359304 | tf_op jit(solution)/shard_map/ppermute | solution.py:124
  154.3 5.4 %copy-start.13 = (f32[512,1536]{1,0:T(8,128)S(1)}, f32[512,1536]{1,0:T(8,128)}, u32[]{:S(2)}) copy-start(f32[512,1536]{1,0:T(8,128)} %copy-done.12) | copy-start | bytes 9437188
  154.4 2.5 %collective-permute-start.20 = (f32[6,768]{1,0:T(8,128)S(1)}, f32[6,768]{1,0:T(8,128)S(1)}, u32[]{:S(2)}, u32[]{:S(2)}) collective-permute-start(f32[6,768]{1,0:T(8,128)S(1)} %fusion.41), channel_id=1, source_target_pairs={{0,1},{1,0},{2,3},{3,2},{4,5},{5,4},{6,7},{7,6},{8,9},{9,8},{10,11... | collective-permute-start | bytes 55304 | tf_op jit(solution)/shard_map/ppermute | solution.py:124
  156.1 1.5 collective-permute-start.19
  157.7 3.5 %copy-start.26 = (f32[12,2304]{1,0:T(8,128)}, f32[12,2304]{1,0:T(8,128)S(1)}, u32[]{:S(2)}) copy-start(f32[12,2304]{1,0:T(8,128)S(1)} %constant_dynamic-update-slice_fusion.3) | copy-start | bytes 331780
